TPU v7x, 512 devices: a whole 4x4x16 slice. The times are simulated.
512 devices in a mesh: box: 128 (over y, z, core), sub: 4 (over x).
Axes of the slice: x: 4, y: 4, z: 16, core: 2. Of those that a mesh axis runs over, the one named last changes fastest.
Arguments:
- charges: bfloat16 [24576, 1024], P(('box', 'sub')), may hold values from -6 to 6
- coords: float32 [24576, 192], P(('box', 'sub')), may hold values from 0 to 2
- basis: bfloat16 [24576, 4096], P(('box', 'sub')), may hold values from -0.75 to 0.75
- transfer: bfloat16 [24576, 4096], P(('box', 'sub')), may hold values from -0.5 to 0.5
- leaf_table: bfloat16 [96, 4096], replicated, may hold values from -0.078125 to 0.078125
- upper_table: bfloat16 [64, 4096], replicated, may hold values from -0.09375 to 0.09375
- near_ids: int32 [24576, 27], P(('box', 'sub')), may hold values from 0 to 24575, as said below
- near_count: int32 [24576], P(('box', 'sub')), may hold values from 1 to 27, as said below
- leaf_ids: int32 [24576, 96], P(('box', 'sub')), may hold values from 0 to 24575, as said below
- parent_ids: int32 [3072, 64], P(('box', 'sub')), may hold values from 0 to 3071, as said below
Outputs:
- potential: float32 [24576, 1024], P(('box', 'sub'))
Inputs may be any that keep to these rules, and one draw needn't show every extreme that they name: `near_ids`: A device holds 48 consecutive leaf boxes. Entry 0 of a list is the box itself; the others are distinct boxes other than itself on the same device or the devices just before and after it. Only the first near_count entries of a list are used; the first box of every device uses all 27. `leaf_ids`: sources are boxes other than the box itself on the same device or the devices just before and after it; they may repeat. `parent_ids`: parents are numbered in Morton order, 24 consecutive ones to each index of box. Sources are parents other than the parent itself in the same group or the groups just before and after it; they may repeat.
All inputs are finite; a program needn't handle non-finite values.
Results may differ from a plain program's by a relative error of at most 0.011.
Values may be sent and summed in bfloat16 or wider, within the bound.
No kernel may reach another device: no remote copies, remote signals or barrier semaphores. Data moves between devices by JAX's collectives and lax.ppermute only.
A program may use at most 64 MiB of HBM per device.

v0:
```python
import math

import jax
import jax.numpy as jnp
from jax import lax
from jax.sharding import PartitionSpec as P

SOFT = 0.05
QUARTER = 0.25 / math.pi


def with_halo(shard, sides, width):
    for axis, dim in sides:
        peers, length = (lax.axis_size(axis), shard.shape[dim])
        up = [(i, (i + 1) % peers) for i in range(peers - 1)]
        down = [(j, i) for i, j in up]
        last = lax.slice_in_dim(shard, length - width, length, axis=dim)
        initial = lax.slice_in_dim(shard, 0, width, axis=dim)
        before = lax.ppermute(last, axis, up)
        after = lax.ppermute(initial, axis, down)
        shard = jnp.concatenate([before, shard, after], axis=dim)
    return shard


def local(
    charges,
    coords,
    basis,
    transfer,
    leaf_table,
    upper_table,
    near_ids,
    near_count,
    leaf_ids,
    parent_ids,
):
    leaf_rows = charges.shape[0]
    points = coords.shape[1] // 3
    rhs_count = charges.shape[1] // points
    rank_width = basis.shape[1] // points
    parent_rows = leaf_rows // 8
    near_slots = near_ids.shape[1]
    leaf_count = leaf_table.shape[0]
    upper_count = upper_table.shape[0]
    sub_count = lax.axis_size("sub")
    first_box = (lax.axis_index(("box", "sub")) - 1) * leaf_rows
    first_parent = (lax.axis_index("box") - 1) * parent_rows * sub_count
    charge_cube = charges.reshape(leaf_rows, points, rhs_count)
    bases = basis.reshape(leaf_rows, points, rank_width)
    shifts = transfer.reshape(leaf_rows, rank_width, rank_width)
    skeleton = jnp.einsum(
        "bpk,bpr->brk", bases, charge_cube, preferred_element_type=jnp.float32
    ).astype(jnp.bfloat16)
    skeleton_flat = skeleton.reshape(leaf_rows, rhs_count * rank_width)
    charge_rim = with_halo(charges, ((("box", "sub"), 0),), leaf_rows)
    skeleton_rim = with_halo(skeleton_flat, ((("box", "sub"), 0),), leaf_rows)
    point_rim = with_halo(coords.astype(jnp.bfloat16), ((("box", "sub"), 0),), leaf_rows).astype(
        coords.dtype
    )
    lifted = jnp.einsum("bjk,brj->brk", shifts, skeleton, preferred_element_type=jnp.float32)
    upper_skeleton = jnp.sum(lifted.reshape(parent_rows, 8, rhs_count, rank_width), axis=1).astype(
        jnp.bfloat16
    )
    upper_skeleton = upper_skeleton.reshape(parent_rows, rhs_count * rank_width)
    gathered = lax.all_gather(upper_skeleton, "sub", axis=0, tiled=True)
    upper_rim = with_halo(gathered, (("box", 0),), gathered.shape[0])
    offset_block = math.gcd(leaf_count, 16)
    table_blocks = leaf_table.reshape(
        leaf_count // offset_block, offset_block, rank_width, rank_width
    )
    local_ids = (leaf_ids - first_box).T.reshape(
        leaf_count // offset_block, offset_block, leaf_rows
    )

    def add_offsets(running, block_data):
        tables, source_ids = block_data
        sources = jnp.take(skeleton_rim, source_ids, axis=0).reshape(
            offset_block, leaf_rows * rhs_count, rank_width
        )
        product = lax.dot_general(
            sources, tables, (((0, 2), (0, 2)), ((), ())), preferred_element_type=jnp.float32
        )
        return (running + product, None)

    starting = jnp.zeros((leaf_rows * rhs_count, rank_width), jnp.float32)
    local_field, _ = lax.scan(add_offsets, starting, (table_blocks, local_ids))
    local_field = local_field.reshape(leaf_rows, rhs_count, rank_width)
    upper_sources = jnp.take(upper_rim, (parent_ids - first_parent).T, axis=0).reshape(
        upper_count, parent_rows * rhs_count, rank_width
    )
    upper_ops = upper_table.reshape(upper_count, rank_width, rank_width)
    upper_field = lax.dot_general(
        upper_sources, upper_ops, (((0, 2), (0, 2)), ((), ())), preferred_element_type=jnp.float32
    )
    upper_field = upper_field.astype(jnp.bfloat16).reshape(parent_rows, rhs_count, rank_width)
    descended = jnp.einsum(
        "bjk,brk->brj",
        shifts,
        jnp.repeat(upper_field, 8, axis=0),
        preferred_element_type=jnp.float32,
    )
    field = (local_field + descended).astype(jnp.bfloat16)
    far_field = jnp.einsum("bpk,brk->bpr", bases, field, preferred_element_type=jnp.float32)
    near_block = math.gcd(leaf_rows, 32)
    block_count = leaf_rows // near_block
    point_cube = coords.reshape(leaf_rows, 3, points)

    def near_part(block_data):
        source_ids, counts, targets = block_data
        source_q = jnp.take(charge_rim, source_ids, axis=0).reshape(
            near_block, near_slots * points, rhs_count
        )
        source_x = jnp.take(point_rim, source_ids, axis=0).reshape(
            near_block, near_slots, 3, points
        )
        distance = None
        for axis_index in range(3):
            separation = targets[:, axis_index, :, None, None] - source_x[:, None, :, axis_index, :]
            squared = separation * separation
            distance = squared if distance is None else distance + squared
        active_slot = jnp.arange(near_slots, dtype=jnp.int32)[None, :] < counts[:, None]
        kernel = jnp.where(
            active_slot[:, None, :, None], QUARTER / jnp.sqrt(distance + SOFT), 0.0
        ).astype(jnp.bfloat16)
        kernel = kernel.reshape(near_block, points, near_slots * points)
        return jnp.einsum("bim,bmr->bir", kernel, source_q, preferred_element_type=jnp.float32)

    near_field = lax.map(
        near_part,
        (
            (near_ids - first_box).reshape(block_count, near_block, near_slots),
            near_count.reshape(block_count, near_block),
            point_cube.reshape(block_count, near_block, 3, points),
        ),
    )
    near_field = near_field.reshape(leaf_rows, points, rhs_count)
    return (near_field + far_field).reshape(leaf_rows, points * rhs_count)


def solution(mesh):
    placed = (
        P(("box", "sub"), None),
        P(("box", "sub"), None),
        P(("box", "sub"), None),
        P(("box", "sub"), None),
        P(),
        P(),
        P(("box", "sub"), None),
        P(("box", "sub")),
        P(("box", "sub"), None),
        P(("box", "sub"), None),
    )
    return jax.shard_map(
        local, mesh=mesh, in_specs=placed, out_specs=P(("box", "sub"), None), check_vma=False
    )
```

profile of v0, /device:TPU:24, one launch (start us, length us, event | category | flops | bytes accessed | tf_op | source)
XLA Modules:
  0.0 275.0 jit_solution(4623368034672546717)
XLA Ops:
  1.5 13.2 %collective-permute-start.1 = (bf16[48,192]{1,0:T(8,128)(2,1)}, bf16[48,192]{1,0:T(8,128)(2,1)}, u32[]{:S(2)}, u32[]{:S(2)}) collective-permute-start(bf16[48,192]{1,0:T(8,128)(2,1)} %convert_element_type.26), channel_id=1, source_target_pairs={{1,0},{2,1},{3,2},{4,3},{5,4},{6,5},{7,6},{8,7},{9,8},{10,9},{11,1... | collective-permute-start | bytes 55304 | tf_op jit(solution)/shard_map/ppermute | solution.py:20
  16.7 7.9 %collective-permute-start.3 = (bf16[48,1024]{1,0:T(8,128)(2,1)}, bf16[48,1024]{1,0:T(8,128)(2,1)}, u32[]{:S(2)}, u32[]{:S(2)}) collective-permute-start(bf16[48,1024]{1,0:T(8,128)(2,1)} %param.14), channel_id=1, source_target_pairs={{1,0},{2,1},{3,2},{4,3},{5,4},{6,5},{7,6},{8,7},{9,8},{10,9},{11,1... | collective-permute-start | bytes 294920 | tf_op jit(solution)/shard_map/ppermute | solution.py:20
  32.2 11.9 %all-gather = bf16[4,6,1024]{2,1,0:T(8,128)(2,1)S(1)} all-gather(bf16[1,6,1024]{2,1,0:T(8,128)(2,1)S(1)} %reshape.246), channel_id=1, replica_groups=mesh['box'=128,'sub'=4] {'sub'}, dimensions={0}, use_global_device_ids=true | all-gather | bytes 61440 | tf_op jit(solution)/shard_map/all_gather | solution.py:65
  44.7 2.6 collective-permute-start.7
  52.9 2.7 reshape.199
  62.8 8.1 %collective-permute-start.5 = (bf16[48,1024]{1,0:T(8,128)(2,1)}, bf16[48,1024]{1,0:T(8,128)(2,1)}, u32[]{:S(2)}, u32[]{:S(2)}) collective-permute-start(bf16[48,1024]{1,0:T(8,128)(2,1)} %reshape.198), channel_id=1, source_target_pairs={{1,0},{2,1},{3,2},{4,3},{5,4},{6,5},{7,6},{8,7},{9,8},{10,9},{11,1... | collective-permute-start | bytes 294920 | tf_op jit(solution)/shard_map/ppermute | solution.py:20
  71.8 2.1 collective-permute-start.4
  77.1 2.2 broadcast_select_fusion.2
  79.4 2.7 select_n.84
  85.6 77.4 %while.21 = (s32[]{:T(128)}, f32[3,16,64,16]{2,3,1,0:T(8,128)S(1)}, s32[3,16]{1,0:T(4,128)S(1)}, f32[3,16,3,64]{3,1,2,0:T(8,128)S(1)}, s32[3,16,27]{2,1,0:T(8,12...) while((s32[]{:T(128)}, f32[3,16,64,16]{2,3,1,0:T(8,128)S(1)}, ...), condition=%wide.region_1.2_spmd, body=%wide.region_0.0_spmd.sunk | while | flops 78387424 | bytes 8533921 | solution.py:128
  87.9 7.0 %gather.37 = bf16[16,1728,16]{2,1,0:T(8,128)(2,1)} reshape(bf16[432,1024]{1,0:T(8,128)(2,1)S(1)} %gather_fusion) | data formatting | bytes 1769472 | tf_op jit(solution)/shard_map/while/body/eval_jaxpr/jit(_take)/gather | solution.py:110
  100.5 10.9 %fusion.51 = f32[3,16,64,16]{2,3,1,0:T(8,128)S(1)} fusion(f32[3,16,64,16]{2,3,1,0:T(8,128)S(1)} %get-tuple-element.230, s32[]{:T(128)S(6)} %copy.52, bf16[16,1728,16]{2,1,0:T(8,128)(2,1)} %gather.37, pred[16,1728]{1,0:T(8,128)(4,1)S(1)} %broadcast_in_dim.162, f32[16,1728]{1,0:T(8,128)S(1)} %sub.181, f32[16,64]{1,0:T(8,128)S(1)} %get-tuple-element.211, ...), kind=kOutput, calls=%fused_computation.30.clone.1 | convolution fusion | flops 78299136 | bytes 1441796 | tf_op jit(solution)/shard_map/while/body/eval_jaxpr/bim,bmr->bir/dot_general | solution.py:126
  113.7 7.0 %gather.37 = bf16[16,1728,16]{2,1,0:T(8,128)(2,1)} reshape(bf16[432,1024]{1,0:T(8,128)(2,1)S(1)} %gather_fusion) | data formatting | bytes 1769472 | tf_op jit(solution)/shard_map/while/body/eval_jaxpr/jit(_take)/gather | solution.py:110
  126.3 10.9 %fusion.51 = f32[3,16,64,16]{2,3,1,0:T(8,128)S(1)} fusion(f32[3,16,64,16]{2,3,1,0:T(8,128)S(1)} %get-tuple-element.230, s32[]{:T(128)S(6)} %copy.52, bf16[16,1728,16]{2,1,0:T(8,128)(2,1)} %gather.37, pred[16,1728]{1,0:T(8,128)(4,1)S(1)} %broadcast_in_dim.162, f32[16,1728]{1,0:T(8,128)S(1)} %sub.181, f32[16,64]{1,0:T(8,128)S(1)} %get-tuple-element.211, ...), kind=kOutput, calls=%fused_computation.30.clone.1 | convolution fusion | flops 78299136 | bytes 1441796 | tf_op jit(solution)/shard_map/while/body/eval_jaxpr/bim,bmr->bir/dot_general | solution.py:126
  139.5 7.0 %gather.37 = bf16[16,1728,16]{2,1,0:T(8,128)(2,1)} reshape(bf16[432,1024]{1,0:T(8,128)(2,1)S(1)} %gather_fusion) | data formatting | bytes 1769472 | tf_op jit(solution)/shard_map/while/body/eval_jaxpr/jit(_take)/gather | solution.py:110
  152.1 10.9 %fusion.51 = f32[3,16,64,16]{2,3,1,0:T(8,128)S(1)} fusion(f32[3,16,64,16]{2,3,1,0:T(8,128)S(1)} %get-tuple-element.230, s32[]{:T(128)S(6)} %copy.52, bf16[16,1728,16]{2,1,0:T(8,128)(2,1)} %gather.37, pred[16,1728]{1,0:T(8,128)(4,1)S(1)} %broadcast_in_dim.162, f32[16,1728]{1,0:T(8,128)S(1)} %sub.181, f32[16,64]{1,0:T(8,128)S(1)} %get-tuple-element.211, ...), kind=kOutput, calls=%fused_computation.30.clone.1 | convolution fusion | flops 78299136 | bytes 1441796 | tf_op jit(solution)/shard_map/while/body/eval_jaxpr/bim,bmr->bir/dot_general | solution.py:126
  164.2 106.1 %while.22 = (s32[]{:T(128)}, f32[768,64]{0,1:T(8,128)}, s32[6,16,48]{2,1,0:T(8,128)}, bf16[144,1024]{1,0:T(8,128)(2,1)S(1)}, bf16[6,16,64,64]{3,2,1,0:T(8,128)(2,1)}, /*index=5*/s32[]{:T(128)}, s32[]{:T(128)}) while((s32[]{:T(128)}, f32[768,64]{0,1:T(8,128)}, s32[6,16,48]{2,1,0:T(8,128)}, bf16[144,1024]{1,0:T(8,128)(2,1)S(1)}, ...), condition=%wide.region_3.4_spmd.clone, body=%wide.region_2.3_spmd.clone.sunk | while | flops 101555968 | bytes 14887531 | solution.py:86
  165.3 2.3 broadcast_in_dim.168
  167.6 2.5 broadcast_in_dim.169
  170.8 2.8 %gather_fusion.2 = bf16[768,1024]{1,0:T(8,128)(2,1)S(1)} fusion(bf16[144,1024]{1,0:T(8,128)(2,1)S(1)} %get-tuple-element.262, s32[1024]{0:T(1024)S(1)} %pad_clamp_fusion.6), kind=kCustom, calls=%fused_computation.2.clone.clone.1 | custom fusion | bytes 3148800 | tf_op jit(solution)/shard_map/while/body/eval_jaxpr/jit(_take)/gather | solution.py:77
  175.0 4.1 %select_n.131 = bf16[16,768,64]{2,1,0:T(8,128)(2,1)S(1)} reshape(bf16[16,48,1024]{2,1,0:T(8,128)(2,1)} %broadcast_select_fusion.6) | data formatting | bytes 3145728 | tf_op jit(solution)/shard_map/while/body/eval_jaxpr/jit(_take)/select_n | solution.py:77
  179.1 2.7 fusion.54
  182.9 2.3 broadcast_in_dim.168
  185.2 2.5 broadcast_in_dim.169
  188.4 2.8 %gather_fusion.2 = bf16[768,1024]{1,0:T(8,128)(2,1)S(1)} fusion(bf16[144,1024]{1,0:T(8,128)(2,1)S(1)} %get-tuple-element.262, s32[1024]{0:T(1024)S(1)} %pad_clamp_fusion.6), kind=kCustom, calls=%fused_computation.2.clone.clone.1 | custom fusion | bytes 3148800 | tf_op jit(solution)/shard_map/while/body/eval_jaxpr/jit(_take)/gather | solution.py:77
  192.6 4.1 %select_n.131 = bf16[16,768,64]{2,1,0:T(8,128)(2,1)S(1)} reshape(bf16[16,48,1024]{2,1,0:T(8,128)(2,1)} %broadcast_select_fusion.6) | data formatting | bytes 3145728 | tf_op jit(solution)/shard_map/while/body/eval_jaxpr/jit(_take)/select_n | solution.py:77
  196.8 2.8 %fusion.54 = f32[768,64]{0,1:T(8,128)} fusion(bf16[16,768,64]{2,1,0:T(8,128)(2,1)S(1)} %select_n.131, bf16[6,16,64,64]{3,2,1,0:T(8,128)(2,1)} %get-tuple-element.263, s32[]{:T(128)S(6)} %copy.58, f32[768,64]{0,1:T(8,128)} %get-tuple-element.253, pred[]{:T(512)S(6)} %compare.3), kind=kOutput, calls=%fused_computation.5.clone.1 | convolution fusion | flops 100761600 | bytes 2228229 | tf_op jit(solution)/shard_map/while/body/eval_jaxpr/dot_general | solution.py:80
  200.6 2.3 broadcast_in_dim.168
  202.9 2.5 broadcast_in_dim.169
  206.1 2.8 %gather_fusion.2 = bf16[768,1024]{1,0:T(8,128)(2,1)S(1)} fusion(bf16[144,1024]{1,0:T(8,128)(2,1)S(1)} %get-tuple-element.262, s32[1024]{0:T(1024)S(1)} %pad_clamp_fusion.6), kind=kCustom, calls=%fused_computation.2.clone.clone.1 | custom fusion | bytes 3148800 | tf_op jit(solution)/shard_map/while/body/eval_jaxpr/jit(_take)/gather | solution.py:77
  210.3 4.1 %select_n.131 = bf16[16,768,64]{2,1,0:T(8,128)(2,1)S(1)} reshape(bf16[16,48,1024]{2,1,0:T(8,128)(2,1)} %broadcast_select_fusion.6) | data formatting | bytes 3145728 | tf_op jit(solution)/shard_map/while/body/eval_jaxpr/jit(_take)/select_n | solution.py:77
  214.4 2.8 %fusion.54 = f32[768,64]{0,1:T(8,128)} fusion(bf16[16,768,64]{2,1,0:T(8,128)(2,1)S(1)} %select_n.131, bf16[6,16,64,64]{3,2,1,0:T(8,128)(2,1)} %get-tuple-element.263, s32[]{:T(128)S(6)} %copy.58, f32[768,64]{0,1:T(8,128)} %get-tuple-element.253, pred[]{:T(512)S(6)} %compare.3), kind=kOutput, calls=%fused_computation.5.clone.1 | convolution fusion | flops 100761600 | bytes 2228229 | tf_op jit(solution)/shard_map/while/body/eval_jaxpr/dot_general | solution.py:80
  218.3 2.3 broadcast_in_dim.168
  220.6 2.5 broadcast_in_dim.169
  223.8 2.8 %gather_fusion.2 = bf16[768,1024]{1,0:T(8,128)(2,1)S(1)} fusion(bf16[144,1024]{1,0:T(8,128)(2,1)S(1)} %get-tuple-element.262, s32[1024]{0:T(1024)S(1)} %pad_clamp_fusion.6), kind=kCustom, calls=%fused_computation.2.clone.clone.1 | custom fusion | bytes 3148800 | tf_op jit(solution)/shard_map/while/body/eval_jaxpr/jit(_take)/gather | solution.py:77
  228.0 4.1 %select_n.131 = bf16[16,768,64]{2,1,0:T(8,128)(2,1)S(1)} reshape(bf16[16,48,1024]{2,1,0:T(8,128)(2,1)} %broadcast_select_fusion.6) | data formatting | bytes 3145728 | tf_op jit(solution)/shard_map/while/body/eval_jaxpr/jit(_take)/select_n | solution.py:77
  232.1 2.8 %fusion.54 = f32[768,64]{0,1:T(8,128)} fusion(bf16[16,768,64]{2,1,0:T(8,128)(2,1)S(1)} %select_n.131, bf16[6,16,64,64]{3,2,1,0:T(8,128)(2,1)} %get-tuple-element.263, s32[]{:T(128)S(6)} %copy.58, f32[768,64]{0,1:T(8,128)} %get-tuple-element.253, pred[]{:T(512)S(6)} %compare.3), kind=kOutput, calls=%fused_computation.5.clone.1 | convolution fusion | flops 100761600 | bytes 2228229 | tf_op jit(solution)/shard_map/while/body/eval_jaxpr/dot_general | solution.py:80
  236.0 2.3 broadcast_in_dim.168
  238.2 2.5 broadcast_in_dim.169
  241.5 2.8 %gather_fusion.2 = bf16[768,1024]{1,0:T(8,128)(2,1)S(1)} fusion(bf16[144,1024]{1,0:T(8,128)(2,1)S(1)} %get-tuple-element.262, s32[1024]{0:T(1024)S(1)} %pad_clamp_fusion.6), kind=kCustom, calls=%fused_computation.2.clone.clone.1 | custom fusion | bytes 3148800 | tf_op jit(solution)/shard_map/while/body/eval_jaxpr/jit(_take)/gather | solution.py:77
  245.7 4.1 %select_n.131 = bf16[16,768,64]{2,1,0:T(8,128)(2,1)S(1)} reshape(bf16[16,48,1024]{2,1,0:T(8,128)(2,1)} %broadcast_select_fusion.6) | data formatting | bytes 3145728 | tf_op jit(solution)/shard_map/while/body/eval_jaxpr/jit(_take)/select_n | solution.py:77
  249.8 2.8 %fusion.54 = f32[768,64]{0,1:T(8,128)} fusion(bf16[16,768,64]{2,1,0:T(8,128)(2,1)S(1)} %select_n.131, bf16[6,16,64,64]{3,2,1,0:T(8,128)(2,1)} %get-tuple-element.263, s32[]{:T(128)S(6)} %copy.58, f32[768,64]{0,1:T(8,128)} %get-tuple-element.253, pred[]{:T(512)S(6)} %compare.3), kind=kOutput, calls=%fused_computation.5.clone.1 | convolution fusion | flops 100761600 | bytes 2228229 | tf_op jit(solution)/shard_map/while/body/eval_jaxpr/dot_general | solution.py:80
  253.7 2.3 broadcast_in_dim.168
  255.9 2.5 broadcast_in_dim.169
  259.2 2.8 %gather_fusion.2 = bf16[768,1024]{1,0:T(8,128)(2,1)S(1)} fusion(bf16[144,1024]{1,0:T(8,128)(2,1)S(1)} %get-tuple-element.262, s32[1024]{0:T(1024)S(1)} %pad_clamp_fusion.6), kind=kCustom, calls=%fused_computation.2.clone.clone.1 | custom fusion | bytes 3148800 | tf_op jit(solution)/shard_map/while/body/eval_jaxpr/jit(_take)/gather | solution.py:77
  263.4 4.1 %select_n.131 = bf16[16,768,64]{2,1,0:T(8,128)(2,1)S(1)} reshape(bf16[16,48,1024]{2,1,0:T(8,128)(2,1)} %broadcast_select_fusion.6) | data formatting | bytes 3145728 | tf_op jit(solution)/shard_map/while/body/eval_jaxpr/jit(_take)/select_n | solution.py:77
  267.5 2.8 %fusion.54 = f32[768,64]{0,1:T(8,128)} fusion(bf16[16,768,64]{2,1,0:T(8,128)(2,1)S(1)} %select_n.131, bf16[6,16,64,64]{3,2,1,0:T(8,128)(2,1)} %get-tuple-element.263, s32[]{:T(128)S(6)} %copy.58, f32[768,64]{0,1:T(8,128)} %get-tuple-element.253, pred[]{:T(512)S(6)} %compare.3), kind=kOutput, calls=%fused_computation.5.clone.1 | convolution fusion | flops 100761600 | bytes 2228229 | tf_op jit(solution)/shard_map/while/body/eval_jaxpr/dot_general | solution.py:80
  271.4 2.4 fusion.29
  (176 shorter events, 78.0 us)
Async XLA Ops:
  0.0 51.4 %copy-start.10 = (s32[48]{0:T(128)S(1)}, s32[48]{0:T(128)}, u32[]{:S(2)}) copy-start(s32[48]{0:T(128)} %param.21) | copy-start | bytes 580
  0.0 52.9 %copy-start.2 = (bf16[96,4096]{1,0:T(8,128)(2,1)S(1)}, bf16[96,4096]{1,0:T(8,128)(2,1)}, u32[]{:S(2)}) copy-start(bf16[96,4096]{1,0:T(8,128)(2,1)} %param.18) | copy-start | bytes 2359300
  0.0 58.8 %copy-start.3 = (bf16[64,4096]{1,0:T(8,128)(2,1)S(1)}, bf16[64,4096]{1,0:T(8,128)(2,1)}, u32[]{:S(2)}) copy-start(bf16[64,4096]{1,0:T(8,128)(2,1)} %param.19) | copy-start | bytes 1572868
  1.5 59.4 %collective-permute-start.1 = (bf16[48,192]{1,0:T(8,128)(2,1)}, bf16[48,192]{1,0:T(8,128)(2,1)}, u32[]{:S(2)}, u32[]{:S(2)}) collective-permute-start(bf16[48,192]{1,0:T(8,128)(2,1)} %convert_element_type.26), channel_id=1, source_target_pairs={{1,0},{2,1},{3,2},{4,3},{5,4},{6,5},{7,6},{8,7},{9,8},{10,9},{11,1... | collective-permute-start | bytes 55304 | tf_op jit(solution)/shard_map/ppermute | solution.py:20
  14.7 48.1 %collective-permute-start = (bf16[48,192]{1,0:T(8,128)(2,1)}, bf16[48,192]{1,0:T(8,128)(2,1)}, u32[]{:S(2)}, u32[]{:S(2)}) collective-permute-start(bf16[48,192]{1,0:T(8,128)(2,1)} %convert_element_type.26), channel_id=1, source_target_pairs={{0,1},{1,2},{2,3},{3,4},{4,5},{5,6},{6,7},{7,8},{8,9},{9,10},{10,1... | collective-permute-start | bytes 55304 | tf_op jit(solution)/shard_map/ppermute | solution.py:19
  16.7 68.0 %collective-permute-start.3 = (bf16[48,1024]{1,0:T(8,128)(2,1)}, bf16[48,1024]{1,0:T(8,128)(2,1)}, u32[]{:S(2)}, u32[]{:S(2)}) collective-permute-start(bf16[48,1024]{1,0:T(8,128)(2,1)} %param.14), channel_id=1, source_target_pairs={{1,0},{2,1},{3,2},{4,3},{5,4},{6,5},{7,6},{8,7},{9,8},{10,9},{11,1... | collective-permute-start | bytes 294920 | tf_op jit(solution)/shard_map/ppermute | solution.py:20
  24.5 60.1 %collective-permute-start.2 = (bf16[48,1024]{1,0:T(8,128)(2,1)}, bf16[48,1024]{1,0:T(8,128)(2,1)}, u32[]{:S(2)}, u32[]{:S(2)}) collective-permute-start(bf16[48,1024]{1,0:T(8,128)(2,1)} %param.14), channel_id=1, source_target_pairs={{0,1},{1,2},{2,3},{3,4},{4,5},{5,6},{6,7},{7,8},{8,9},{9,10},{10,1... | collective-permute-start | bytes 294920 | tf_op jit(solution)/shard_map/ppermute | solution.py:19
  29.3 33.5 %copy-start = (bf16[48,64,64]{2,1,0:T(8,128)(2,1)}, bf16[48,64,64]{2,1,0:T(8,128)(2,1)S(1)}, u32[]{:S(2)}) copy-start(bf16[48,64,64]{2,1,0:T(8,128)(2,1)S(1)} %reshape.197) | copy-start | bytes 1179652
  31.4 45.4 %copy-start.1 = (bf16[48,64,64]{2,1,0:T(8,128)(2,1)}, bf16[48,64,64]{2,1,0:T(8,128)(2,1)S(1)}, u32[]{:S(2)}) copy-start(bf16[48,64,64]{2,1,0:T(8,128)(2,1)S(1)} %reshape.201) | copy-start | bytes 1179652
  44.7 27.0 %collective-permute-start.7 = (bf16[24,1024]{1,0:T(8,128)(2,1)}, bf16[24,1024]{1,0:T(8,128)(2,1)}, u32[]{:S(2)}, u32[]{:S(2)}) collective-permute-start(bf16[24,1024]{1,0:T(8,128)(2,1)} %reshape.247), channel_id=1, source_target_pairs={{4,0},{8,4},{12,8},{16,12},{20,16},{24,20},{28,24},{32,28},{36,32}... | collective-permute-start | bytes 147464 | tf_op jit(solution)/shard_map/ppermute | solution.py:20
  60.9 13.0 %collective-permute-start.6 = (bf16[24,1024]{1,0:T(8,128)(2,1)}, bf16[24,1024]{1,0:T(8,128)(2,1)S(1)}, u32[]{:S(2)}, u32[]{:S(2)}) collective-permute-start(bf16[24,1024]{1,0:T(8,128)(2,1)} %reshape.247), channel_id=1, source_target_pairs={{0,4},{4,8},{8,12},{12,16},{16,20},{20,24},{24,28},{28,32},{32,36}... | collective-permute-start | bytes 147464 | tf_op jit(solution)/shard_map/ppermute | solution.py:19
  62.8 100.2 %collective-permute-start.5 = (bf16[48,1024]{1,0:T(8,128)(2,1)}, bf16[48,1024]{1,0:T(8,128)(2,1)}, u32[]{:S(2)}, u32[]{:S(2)}) collective-permute-start(bf16[48,1024]{1,0:T(8,128)(2,1)} %reshape.198), channel_id=1, source_target_pairs={{1,0},{2,1},{3,2},{4,3},{5,4},{6,5},{7,6},{8,7},{9,8},{10,9},{11,1... | collective-permute-start | bytes 294920 | tf_op jit(solution)/shard_map/ppermute | solution.py:20
  71.8 91.3 %collective-permute-start.4 = (bf16[48,1024]{1,0:T(8,128)(2,1)}, bf16[48,1024]{1,0:T(8,128)(2,1)}, u32[]{:S(2)}, u32[]{:S(2)}) collective-permute-start(bf16[48,1024]{1,0:T(8,128)(2,1)} %reshape.198), channel_id=1, source_target_pairs={{0,1},{1,2},{2,3},{3,4},{4,5},{5,6},{6,7},{7,8},{8,9},{9,10},{10,1... | collective-permute-start | bytes 294920 | tf_op jit(solution)/shard_map/ppermute | solution.py:19
  76.8 8.8 %copy-start.4 = (s32[48,27]{1,0:T(8,128)S(1)}, s32[48,27]{1,0:T(8,128)}, u32[]{:S(2)}) copy-start(s32[48,27]{1,0:T(8,128)} %copy.34) | copy-start | bytes 15556
  77.1 7.5 %copy-start.5 = (bf16[48,1024]{1,0:T(8,128)(2,1)S(1)}, bf16[48,1024]{1,0:T(8,128)(2,1)}, u32[]{:S(2)}) copy-start(bf16[48,1024]{1,0:T(8,128)(2,1)} %param.14) | copy-start | bytes 294916
  77.1 8.5 %copy-start.7 = (f32[3,16,64,16]{2,3,1,0:T(8,128)S(1)}, f32[3,16,64,16]{2,3,1,0:T(8,128)}, u32[]{:S(2)}) copy-start(f32[3,16,64,16]{2,3,1,0:T(8,128)} %custom-call.9) | copy-start | bytes 589828
  85.6 77.4 %copy-start.6 = (bf16[48,1024]{1,0:T(8,128)(2,1)S(1)}, bf16[48,1024]{1,0:T(8,128)(2,1)}, u32[]{:S(2)}) copy-start(bf16[48,1024]{1,0:T(8,128)(2,1)} %reshape.198) | copy-start | bytes 294916
  163.0 1.1 copy-start.8
  164.2 107.2 %copy-start.9 = (bf16[96,64]{1,0:T(8,128)(2,1)S(1)}, bf16[96,64]{1,0:T(8,128)(2,1)}, u32[]{:S(2)}) copy-start(bf16[96,64]{1,0:T(8,128)(2,1)} %copy.43) | copy-start | bytes 36868
where the time goes:
time: 277 us; the launch traced here: 275 us
  local copies, waits for them, and re-layouts  140 us (51%)
  matrix products  54.1 us (20%)
  starting transfers between devices  39.6 us (14%)
  other arithmetic  28.5 us (10%)
  blocking collectives  11.9 us (4%)
    dot_general x3, matrix products, near_part(): jnp.einsum('bim,bmr->bir', kernel, source_q, preferred_element_type=jnp.f...  32.7 us
    ppermute x4, starting transfers between devices, with_halo(): after = lax.ppermute(initial, axis, down)  31.8 us
    broadcast_in_dim x24, local copies, waits for them, and re-layouts, add_offsets(): jnp.take(skeleton_rim, source_ids, axis=0)  30.6 us
    gather x6, local copies, waits for them, and re-layouts, near_part(): jnp.take(charge_rim, source_ids, axis=0)  27.4 us
    select_n x12, local copies, waits for them, and re-layouts, add_offsets(): jnp.take(skeleton_rim, source_ids, axis=0)  25.2 us
    gather x6, local copies, waits for them, and re-layouts, add_offsets(): jnp.take(skeleton_rim, source_ids, axis=0)  16.9 us
    dot_general x6, matrix products, add_offsets(): lax.dot_general(sources, tables, (((0, 2), (0, 2)), ((), ())), preferred_...  16.5 us
    select_n x12, other arithmetic, add_offsets(): jnp.take(skeleton_rim, source_ids, axis=0)  12.4 us
  transfers between devices with their start and end apart: 8, of which 0 were waited for; matrix products, arithmetic and copies ran while one was open for 40% of the time, Pallas kernels for 0%

commit v1 on v0

v1 whole, which is shorter than its diff:
```python
import functools
import math

import jax
import jax.numpy as jnp
from jax import lax
from jax.experimental import pallas as pl
from jax.experimental.pallas import tpu as pltpu
from jax.sharding import PartitionSpec as P

SOFT = 0.05
SCALE = 16.0 * math.pi * math.pi
F32 = jnp.float32
BF16 = jnp.bfloat16
BOXES = 48
PAIRS = BOXES // 2
NEAR = 27
OFFSETS = 96
UPPER = 64
PARENTS = 6
S_ROWS = PAIRS * 16
U_ROWS = PARENTS // 2 * 16
VMEM_LIMIT = 48 * 1024 * 1024


def nn(a, b):
    return lax.dot_general(a, b, (((1,), (0,)), ((), ())), preferred_element_type=F32)


def nt(a, b):
    return lax.dot_general(a, b, (((1,), (1,)), ((), ())), preferred_element_type=F32)


def iota(shape, dim):
    return lax.broadcasted_iota(jnp.int32, shape, dim)


def onehot(cond):
    return jnp.where(cond, 1.0, 0.0).astype(BF16)


def half_swap(x):
    return pltpu.roll(x, 64, 1)


def skeleton_kernel(q_ref, v_ref, e_ref, su_ref, xv_ref, xe_ref, qs, vs, es):
    for i in range(8):
        qs[i * BOXES : (i + 1) * BOXES] = q_ref[:, i * 128 : (i + 1) * 128].astype(F32)
    for t in range(32):
        vs[t * BOXES : (t + 1) * BOXES] = v_ref[:, t * 128 : (t + 1) * 128].astype(F32)
    for t in range(32):
        es[t * BOXES : (t + 1) * BOXES] = e_ref[:, t * 128 : (t + 1) * 128].astype(F32)
    row = iota((32, 128), 0)
    lane = iota((32, 128), 1)
    pick = onehot((lane % 32) == row)
    lane8 = iota((8, 128), 1) // 32
    lane16 = iota((16, 128), 1)
    low = lane16 < 64
    group = lane // 32
    for g in range(BOXES // 4):
        parts = []
        for c in range(4):
            b = g * 4 + c
            rows = qs[pl.ds(b, 8, stride=BOXES), :]
            parts += [jnp.where(lane8 == m, rows, 0.0) for m in range(4)]
        weights = jnp.concatenate(parts, axis=0).astype(BF16)
        q2 = nt(pick, weights)
        lhs = jnp.concatenate([jnp.where(group == c, q2, 0.0) for c in range(4)], axis=0).astype(BF16)
        vb = []
        for c in range(4):
            b = g * 4 + c
            vb += [vs[pl.ds(m * BOXES + b, 8, stride=4 * BOXES), :] for m in range(4)]
        xv = jnp.concatenate(vb, axis=0).astype(BF16)
        xv_ref[g * 128 : (g + 1) * 128] = xv
        z = nn(lhs, xv)
        for u in range(2):
            o = u * 64
            even = z[o : o + 16] + half_swap(z[o + 16 : o + 32])
            odd = half_swap(z[o + 32 : o + 48]) + z[o + 48 : o + 64]
            r = (g * 2 + u) * 16
            su_ref[r : r + 16] = jnp.where(low, even, odd).astype(BF16)
    prow = iota((256, 256), 0)
    pcol = iota((256, 256), 1)
    spread = onehot(
        ((prow // 64) == ((pcol % 128) // 32)) & ((prow % 64) == 2 * (pcol % 32) + pcol // 128)
    )
    lifted = []
    for p in range(PARENTS):
        lhs = []
        xe = []
        for h in range(2):
            g = p * 2 + h
            s = su_ref[g * 32 : g * 32 + 32]
            wide = jnp.concatenate([s[:16], s[16:]], axis=1)
            moved = nn(wide, spread)
            lhs.append(jnp.concatenate([moved[:, :128], moved[:, 128:]], axis=0))
            for c in range(4):
                xe.append(es[pl.ds(g * 4 + c, 32, stride=BOXES), :])
        lhs = jnp.concatenate(lhs, axis=1).astype(BF16)
        xe = jnp.concatenate(xe, axis=0).astype(BF16)
        xe_ref[p * 256 : (p + 1) * 256] = xe
        z = nn(lhs, xe)
        if p % 2 == 0:
            lifted = z[:16] + half_swap(z[16:])
        else:
            other = half_swap(z[:16]) + z[16:]
            r = S_ROWS + (p // 2) * 16
            su_ref[r : r + 16] = jnp.where(low, lifted, other).astype(BF16)


def pack_kernel(q_ref, x_ref, out_ref, qs):
    for i in range(8):
        qs[i * BOXES : (i + 1) * BOXES] = q_ref[:, i * 128 : (i + 1) * 128].astype(F32)
    own = iota((8, 128), 0) == iota((8, 128), 1) // 16
    pick = onehot((iota((16, 128), 1) % 16) == iota((16, 128), 0))
    for u in range(PAIRS):
        parts = []
        for c in range(2):
            rows = qs[pl.ds(u * 2 + c, 8, stride=BOXES), :]
            for i in range(8):
                parts.append(jnp.where(own, jnp.broadcast_to(rows[i : i + 1], (8, 128)), 0.0))
        weights = jnp.concatenate(parts, axis=0).astype(BF16)
        out_ref[u * 16 : u * 16 + 16] = nt(pick, weights).astype(BF16)
    out_ref[S_ROWS : S_ROWS + BOXES] = x_ref[:, :128].astype(BF16)
    out_ref[S_ROWS + BOXES : S_ROWS + 2 * BOXES] = jnp.concatenate(
        [x_ref[:, 128:], jnp.zeros((BOXES, 64), F32)], axis=1
    ).astype(BF16)


def table_kernel(leaf_ref, upper_ref, wl_ref, wu_ref, ts):
    low = iota((32, 128), 1) < 64
    for ref, out, count in ((leaf_ref, wl_ref, OFFSETS), (upper_ref, wu_ref, UPPER)):
        for t in range(32):
            ts[t * count : (t + 1) * count] = ref[:, t * 128 : (t + 1) * 128].astype(F32)
        for u in range(count // 2):
            first = ts[pl.ds(2 * u, 32, stride=count), :]
            second = ts[pl.ds(2 * u + 1, 32, stride=count), :]
            even = jnp.where(low, first, half_swap(second))
            odd = jnp.where(low, half_swap(first), second)
            out[:, u * 128 : (u + 1) * 128] = jnp.concatenate([even, odd], axis=0).astype(BF16)


def split3(x):
    a = x.astype(BF16).astype(F32)
    rest = x - a
    b = rest.astype(BF16).astype(F32)
    return a, b, rest - b


def dup_matrix():
    r = iota((128, 256), 0)
    c = iota((128, 256), 1)
    return onehot((r // 64 == c // 128) & (r % 64 == c % 64))


def spread_pairs(src_ref, rows, dst_ref, base):
    wide = nn(src_ref[:rows], dup_matrix()).astype(BF16)
    for u in range(rows // 16):
        dst_ref[base + 2 * u] = wide[u * 16 : u * 16 + 16, :128]
        dst_ref[base + 2 * u + 1] = wide[u * 16 : u * 16 + 16, 128:]


STEP = 4


def near_kernel(
    info, ids, counts, own_ref, prev_ref, next_ref, x_ref, out_ref, qt, yt, at, ks, bs, acc, place, sums
):
    first = info[0]
    for side, ref in enumerate((prev_ref, own_ref, next_ref)):
        spread_pairs(ref, S_ROWS, qt, side * BOXES)
    qt[3 * BOXES] = jnp.zeros((16, 128), BF16)
    total = 3 * BOXES
    lanes = iota((BOXES, 128), 1) < 64

    def dup3(xy, z):
        flip = half_swap(xy)
        return jnp.where(lanes, xy, flip), jnp.where(lanes, flip, xy), jnp.where(lanes, z, half_swap(z))

    ones = jnp.ones((BOXES, 128), F32)
    zeros = jnp.zeros((BOXES, 128), F32)
    for side, ref in enumerate((prev_ref, own_ref, next_ref)):
        xy = ref[S_ROWS : S_ROWS + BOXES].astype(F32)
        z = ref[S_ROWS + BOXES : S_ROWS + 2 * BOXES].astype(F32)
        y0, y1, y2 = dup3(xy, z)
        n = split3(SCALE * (y0 * y0 + y1 * y1 + y2 * y2))
        for k, v in enumerate((y0, y0, y0, y1, y1, y1, y2, y2, y2, *n, ones, ones, ones, zeros)):
            bs[k * BOXES : (k + 1) * BOXES] = v
        for b in range(BOXES):
            yt[side * BOXES + b] = bs[pl.ds(b, 16, stride=BOXES), :].astype(BF16)
    yt[total] = onehot(iota((16, 128), 0) >= 12)
    zx = jnp.concatenate([x_ref[:, 128:], jnp.zeros((BOXES, 64), F32)], axis=1)
    x0, x1, x2 = dup3(x_ref[:, :128], zx)
    n = split3(SCALE * (x0 * x0 + x1 * x1 + x2 * x2 + SOFT))
    cols = []
    for x in (x0, x1, x2):
        cols += list(split3((-2.0 * SCALE) * x))
    for k, v in enumerate((*cols, ones, ones, ones, *n, zeros)):
        bs[k * BOXES : (k + 1) * BOXES] = v
    eye = onehot((iota((64, 128), 0) == iota((64, 128), 1)))
    for b in range(BOXES):
        at[b] = nt(eye, bs[pl.ds(b, 16, stride=BOXES), :].astype(BF16)).astype(BF16)
        acc[b] = jnp.zeros((16, 64), F32)
    acc[BOXES] = jnp.zeros((16, 64), F32)
    at[BOXES] = jnp.zeros((64, 16), BF16) + onehot(iota((64, 16), 1) == 12)
    low = iota((16, 128), 1) < 64

    def advance(box, chunk):
        here = jnp.minimum(box, BOXES - 1)
        more = (chunk + 1) * 8 < counts[here]
        return jnp.where(more, box, box + 1), jnp.where(more, chunk + 1, 0)

    def gather(table, sources):
        tiles = [
            jnp.where(low, table[sources[2 * j]], table[sources[2 * j + 1]])
            for j in range(len(sources) // 2)
        ]
        return jnp.concatenate(tiles, axis=1)

    def work(state):
        step, box, chunk = state
        slot = step % 2
        last = 1 - slot
        for j in range(STEP):
            kernel = ks[last, j]
            here = place[last * STEP * 9 + j * 9]
            sources = [place[last * STEP * 9 + j * 9 + 1 + c] for c in range(8)]
            acc[here] += nt(gather(qt, sources), kernel)
        for j in range(STEP):
            target = jnp.minimum(box, BOXES)
            here = jnp.minimum(box, BOXES - 1)
            used = counts[here]
            sources = []
            for c in range(8):
                n = chunk * 8 + c
                g = ids[here, jnp.minimum(n, NEAR - 1)] - first
                sources.append(jnp.where((n < used) & (box < BOXES), g, total))
            place[slot * STEP * 9 + j * 9] = target
            for c in range(8):
                place[slot * STEP * 9 + j * 9 + 1 + c] = sources[c]
            d = nn(at[target], gather(yt, sources))
            ks[slot, j] = lax.rsqrt(d).astype(BF16)
            box, chunk = advance(box, chunk)
        return step + 1, box, chunk

    for j in range(STEP):
        place[STEP * 9 + j * 9] = BOXES
        for c in range(8):
            place[STEP * 9 + j * 9 + 1 + c] = total
        ks[1, j] = jnp.zeros((64, 512), BF16)
    step, _, _ = lax.while_loop(lambda s: s[1] < BOXES, work, (0, 0, 0))
    last = 1 - step % 2
    for j in range(STEP):
        here = place[last * STEP * 9 + j * 9]
        sources = [place[last * STEP * 9 + j * 9 + 1 + c] for c in range(8)]
        acc[here] += nt(gather(qt, sources), ks[last, j])
    lane8 = iota((8, 128), 1) // 16
    for g in range(BOXES // 8):
        rows = jnp.concatenate([acc[g * 8 + c] for c in range(8)], axis=0)
        sums[...] = rows.T
        tiles = [sums[pl.ds(s, 8, stride=8), :] for s in range(8)]
        for c in range(8):
            total_tile = None
            for s in range(8):
                moved = tiles[s] if s == c else pltpu.roll(tiles[s], (16 * (s - c)) % 128, 1)
                total_tile = moved if total_tile is None else jnp.where(lane8 == s, moved, total_tile)
            out_ref[pl.ds(g * 8 + c, 8, stride=BOXES), :] = total_tile


def couple(table, w_ref, ids, base, first, boxes, offsets, low):
    quads = offsets // 4

    def body(k, total):
        rows = []
        for b in range(boxes):
            g = [ids[base + b, k * 4 + j] - first for j in range(4)]
            rows.append(
                jnp.concatenate(
                    [jnp.where(low, table[g[0]], table[g[1]]), jnp.where(low, table[g[2]], table[g[3]])],
                    axis=1,
                )
            )
        lhs = jnp.concatenate(rows, axis=0)
        return total + nt(lhs, w_ref[:, pl.ds(pl.multiple_of(k * 256, 256), 256)])

    return lax.fori_loop(0, quads, body, jnp.zeros((boxes * 16, 64), F32))


GROUP = 16


def field_kernel(
    info, ids, pids, su_ref, rd1_ref, rd2_ref, bp_ref, bm_ref, wl_ref, wu_ref, xv_ref, xe_ref, near_ref,
    out_ref, st, ut, halo, fs, ps,
):
    first = info[0]
    first_parent = info[1]
    sub = info[2]
    low = iota((16, 128), 1) < 64

    @pl.when(sub == 0)
    def _():
        halo[0] = bp_ref[:S_ROWS]
        halo[1] = rd1_ref[:S_ROWS]

    @pl.when(sub == 1)
    def _():
        halo[0] = rd1_ref[:S_ROWS]
        halo[1] = rd2_ref[:S_ROWS]

    @pl.when(sub == 2)
    def _():
        halo[0] = rd2_ref[:S_ROWS]
        halo[1] = rd1_ref[:S_ROWS]

    @pl.when(sub == 3)
    def _():
        halo[0] = rd1_ref[:S_ROWS]
        halo[1] = bm_ref[:S_ROWS]

    spread_pairs(halo.at[0], S_ROWS, st, 0)
    spread_pairs(su_ref, S_ROWS, st, BOXES)
    spread_pairs(halo.at[1], S_ROWS, st, 2 * BOXES)

    def parents(ref, row, group, flip):
        wide = nn(ref[row : row + U_ROWS], dup_matrix()).astype(BF16)
        at = group * 4 * PARENTS + (sub ^ flip) * PARENTS
        for u in range(PARENTS // 2):
            ut[at + 2 * u] = wide[u * 16 : u * 16 + 16, :128]
            ut[at + 2 * u + 1] = wide[u * 16 : u * 16 + 16, 128:]

    for group, ref in ((0, bp_ref), (2, bm_ref)):
        for j, flip in enumerate((3, 2, 0, 1)):
            parents(ref, S_ROWS + j * U_ROWS, group, flip)
    parents(su_ref, S_ROWS, 1, 0)
    parents(rd1_ref, S_ROWS, 1, 1)
    parents(rd2_ref, S_ROWS, 1, 3)
    parents(rd2_ref, S_ROWS + U_ROWS, 1, 2)

    upper = couple(ut, wu_ref, pids, 0, first_parent, PARENTS, UPPER, low)
    r64 = iota((64, 128), 0)
    c64 = iota((64, 128), 1)
    natural = onehot((c64 % 64) == 2 * (r64 % 32) + r64 // 32)
    upper2 = nn(upper.astype(BF16), natural)
    lane16 = iota((16, 128), 1)
    for p in range(PARENTS):
        u = upper2[p * 16 : p * 16 + 16]
        lhs = jnp.concatenate([jnp.where(low, u, 0.0), jnp.where(low, 0.0, u)], axis=0).astype(BF16)
        down = nt(lhs, xe_ref[p * 256 : (p + 1) * 256])
        for c in range(8):
            tile = down[:, (c // 4) * 128 : (c // 4) * 128 + 128]
            at = (c % 4) * 32
            a = tile[:16] if at == 0 else pltpu.roll(tile[:16], 128 - at, 1)
            b = tile[16:] if at == 32 else pltpu.roll(tile[16:], (160 - at) % 128, 1)
            fs[(p * 8 + c) * 16 : (p * 8 + c + 1) * 16] = jnp.where(lane16 < 32, a, b)
    lane8 = iota((8, 128), 1) // 32
    low64 = iota((16, 128), 1) < 64
    for h in range(BOXES // GROUP):
        part = couple(st, wl_ref, ids, h * GROUP, first, GROUP, OFFSETS, low)
        field = (part + fs[h * GROUP * 16 : (h + 1) * GROUP * 16, :64]).astype(BF16)
        wide = nn(field, natural)
        for q in range(GROUP // 4):
            parts = []
            for c in range(4):
                f = wide[(q * 4 + c) * 16 : (q * 4 + c + 1) * 16]
                parts += [jnp.where(low64, f, 0.0), jnp.where(low64, 0.0, f)]
            weights = jnp.concatenate(parts, axis=0).astype(BF16)
            g = h * (GROUP // 4) + q
            far = nt(xv_ref[g * 128 : (g + 1) * 128], weights)
            for c in range(4):
                tile = None
                for m in range(4):
                    piece = far[c * 32 + m * 8 : c * 32 + m * 8 + 8]
                    if m != c:
                        piece = pltpu.roll(piece, (32 * (m - c)) % 128, 1)
                    tile = piece if tile is None else jnp.where(lane8 == m, piece, tile)
                rows = pl.ds(g * 4 + c, 8, stride=BOXES)
                ps[rows, :] = tile
    for i in range(8):
        rows = slice(i * BOXES, (i + 1) * BOXES)
        out_ref[:, i * 128 : (i + 1) * 128] = near_ref[rows] + ps[rows]


VM = pl.BlockSpec(memory_space=pltpu.VMEM)
SM = pl.BlockSpec(memory_space=pltpu.SMEM)


def params():
    return pltpu.CompilerParams(vmem_limit_bytes=VMEM_LIMIT)


def run_skeleton(charges, basis, transfer):
    return pl.pallas_call(
        skeleton_kernel,
        out_shape=(
            jax.ShapeDtypeStruct((S_ROWS + U_ROWS, 128), BF16),
            jax.ShapeDtypeStruct((BOXES * 32, 128), BF16),
            jax.ShapeDtypeStruct((BOXES * 32, 128), BF16),
        ),
        in_specs=[VM] * 3,
        out_specs=(VM,) * 3,
        scratch_shapes=[
            pltpu.VMEM((8 * BOXES, 128), F32),
            pltpu.VMEM((32 * BOXES, 128), F32),
            pltpu.VMEM((32 * BOXES, 128), F32),
        ],
        compiler_params=params(),
        name="skeleton",
    )(charges, basis, transfer)


def run_pack(charges, coords):
    return pl.pallas_call(
        pack_kernel,
        out_shape=jax.ShapeDtypeStruct((S_ROWS + 2 * BOXES, 128), BF16),
        in_specs=[VM] * 2,
        out_specs=VM,
        scratch_shapes=[pltpu.VMEM((8 * BOXES, 128), F32)],
        compiler_params=params(),
        name="pack",
    )(charges, coords)


def run_tables(leaf_table, upper_table):
    return pl.pallas_call(
        table_kernel,
        out_shape=(
            jax.ShapeDtypeStruct((64, OFFSETS * 64), BF16),
            jax.ShapeDtypeStruct((64, UPPER * 64), BF16),
        ),
        in_specs=[VM] * 2,
        out_specs=(VM,) * 2,
        scratch_shapes=[pltpu.VMEM((32 * OFFSETS, 128), F32)],
        compiler_params=params(),
        name="tables",
    )(leaf_table, upper_table)


def run_near(info, near_ids, near_count, own, before, after, coords):
    return pl.pallas_call(
        near_kernel,
        out_shape=jax.ShapeDtypeStruct((8 * BOXES, 128), F32),
        in_specs=[SM] * 3 + [VM] * 4,
        out_specs=VM,
        scratch_shapes=[
            pltpu.VMEM((3 * BOXES + 1, 16, 128), BF16),
            pltpu.VMEM((3 * BOXES + 1, 16, 128), BF16),
            pltpu.VMEM((BOXES + 1, 64, 16), BF16),
            pltpu.VMEM((2, STEP, 64, 512), BF16),
            pltpu.VMEM((16 * BOXES, 128), F32),
            pltpu.VMEM((BOXES + 1, 16, 64), F32),
            pltpu.SMEM((2 * STEP * 9,), jnp.int32),
            pltpu.VMEM((64, 128), F32),
        ],
        compiler_params=params(),
        name="near",
    )(info, near_ids, near_count, own, before, after, coords)


def run_field(info, leaf_ids, parent_ids, su, rd1, rd2, bp, bm, wl, wu, xv, xe, near):
    return pl.pallas_call(
        field_kernel,
        out_shape=jax.ShapeDtypeStruct((BOXES, 1024), F32),
        in_specs=[SM] * 3 + [VM] * 10,
        out_specs=VM,
        scratch_shapes=[
            pltpu.VMEM((3 * BOXES, 16, 128), BF16),
            pltpu.VMEM((12 * PARENTS, 16, 128), BF16),
            pltpu.VMEM((2, S_ROWS, 128), BF16),
            pltpu.VMEM((BOXES * 16, 128), F32),
            pltpu.VMEM((8 * BOXES, 128), F32),
        ],
        compiler_params=params(),
        name="field",
    )(info, leaf_ids, parent_ids, su, rd1, rd2, bp, bm, wl, wu, xv, xe, near)


def local(
    charges, coords, basis, transfer, leaf_table, upper_table, near_ids, near_count, leaf_ids, parent_ids
):
    flat = ("box", "sub")
    boxes = lax.axis_size("box")
    subs = lax.axis_size("sub")
    chain = boxes * subs
    sub = lax.axis_index("sub")
    info = jnp.stack(
        [
            (lax.axis_index(flat) - 1) * BOXES,
            (lax.axis_index("box") - 1) * PARENTS * subs,
            sub,
        ]
    ).astype(jnp.int32)
    su, xv, xe = run_skeleton(charges, basis, transfer)
    rd1 = lax.ppermute(su, "sub", [(i, i ^ 1) for i in range(subs)])
    own = run_pack(charges, coords)
    before = lax.ppermute(own, flat, [(i, i + 1) for i in range(chain - 1)])
    after = lax.ppermute(own, flat, [(i + 1, i) for i in range(chain - 1)])
    wl, wu = run_tables(leaf_table, upper_table)
    rd2 = lax.ppermute(
        jnp.concatenate([su, rd1[S_ROWS:]], axis=0), "sub", [(i, i ^ 3) for i in range(subs)]
    )
    edge = jnp.concatenate([rd2, su[S_ROWS:], rd1[S_ROWS:]], axis=0)
    bp = lax.ppermute(edge, "box", [(i, i + 1) for i in range(boxes - 1)])
    bm = lax.ppermute(edge, "box", [(i + 1, i) for i in range(boxes - 1)])
    near = run_near(info, near_ids, near_count, own, before, after, coords)
    return run_field(info, leaf_ids, parent_ids, su, rd1, rd2, bp, bm, wl, wu, xv, xe, near)


def solution(mesh):
    rows = P(("box", "sub"), None)
    placed = (rows, rows, rows, rows, P(), P(), rows, P(("box", "sub")), rows, rows)
    return jax.shard_map(
        local, mesh=mesh, in_specs=placed, out_specs=P(("box", "sub"), None), check_vma=False
    )
```

time: 277 us -> 82.4 us (0.30)
  local copies, waits for them, and re-layouts: 140 us -> 3.72 us
  matrix products: 54.1 us -> 0 us
  Pallas kernels: 0 us -> 36 us
  other arithmetic: 28.5 us -> 0.1 us
  waiting for transfers between devices: 0.02 us -> 12.8 us
  blocking collectives: 11.9 us -> 0 us
  starting transfers between devices: 39.6 us -> 29.1 us
    dot_general x13 -> x0, matrix products: 54.1 us -> none  [the longest x3 32.7 us: near_part(): jnp.einsum('bim,bmr->bir', kernel, source_q, preferred_element_type=jnp.f...]
    gather x20 -> x0, local copies, waits for them, and re-layouts: 52.5 us -> none  [the longest x6 27.4 us: near_part(): jnp.take(charge_rim, source_ids, axis=0)]
    pallas_call x0 -> x5, Pallas kernels: none -> 36 us  [the longest x1 22 us: run_field(): pl.pallas_call(field_kernel, out_shape=jax.ShapeDtypeStruct((BOXES, 1024)...]
    broadcast_in_dim x42 -> x0, local copies, waits for them, and re-layouts: 35.7 us -> none  [the longest x24 30.6 us: add_offsets(): jnp.take(skeleton_rim, source_ids, axis=0)]
    select_n x17 -> x0, local copies, waits for them, and re-layouts: 28.2 us -> none  [the longest x12 25.2 us: add_offsets(): jnp.take(skeleton_rim, source_ids, axis=0)]
    select_n x19 -> x0, other arithmetic: 16.5 us -> none  [the longest x12 12.4 us: add_offsets(): jnp.take(skeleton_rim, source_ids, axis=0)]
    ppermute x8 -> x6, waiting for transfers between devices: 0.02 us -> 12.8 us  [the longest x1 6.24 us: local(): before = lax.ppermute(own, flat, [(i, i + 1) for i in range(chain - 1)])]
    all_gather x1 -> x0, blocking collectives: 11.9 us -> none  [local(): gathered = lax.all_gather(upper_skeleton, 'sub', axis=0, tiled=True)]
  transfers between devices with their start and end apart: 8 -> 6, of which waited for: 0 -> 3; matrix products, arithmetic and copies ran while one was open for 40% -> 0% of each run, Pallas kernels for 0% -> 13%
where the time goes in v1:
time: 82.4 us; the launch traced here: 82 us
  Pallas kernels  36 us (44%)
  starting transfers between devices  29.1 us (35%)
  waiting for transfers between devices  12.8 us (16%)
  local copies, waits for them, and re-layouts  3.72 us (5%)
    pallas_call x1, Pallas kernels, run_field(): pl.pallas_call(field_kernel, out_shape=jax.ShapeDtypeStruct((BOXES, 1024)...  22 us
    ppermute x1, starting transfers between devices, local(): bm = lax.ppermute(edge, 'box', [(i + 1, i) for i in range(boxes - 1)])  9 us
    pallas_call x1, Pallas kernels, run_near(): pl.pallas_call(near_kernel, out_shape=jax.ShapeDtypeStruct((8 * BOXES, 12...  8.5 us
    ppermute x1, starting transfers between devices, local(): after = lax.ppermute(own, flat, [(i + 1, i) for i in range(chain - 1)])  8.09 us
    ppermute x1, waiting for transfers between devices, local(): before = lax.ppermute(own, flat, [(i, i + 1) for i in range(chain - 1)])  6.24 us
    ppermute x1, starting transfers between devices, local(): lax.ppermute(jnp.concatenate([su, rd1[S_ROWS:]], axis=0), 'sub', [(i, i ^...  4.67 us
    unnamed x21, local copies, waits for them, and re-layouts  3.72 us
    ppermute x1, starting transfers between devices, local(): rd1 = lax.ppermute(su, 'sub', [(i, i ^ 1) for i in range(subs)])  3.53 us
  transfers between devices with their start and end apart: 6, of which 3 were waited for; matrix products, arithmetic and copies ran while one was open for 0% of the time, Pallas kernels for 13%

profile of v1, /device:TPU:24, one launch (start us, length us, event | category | flops | bytes accessed | tf_op | source)
XLA Modules:
  0.0 82.0 jit_solution(16859277505298267830)
XLA Ops:
  0.0 0.0 copy-start
  0.0 0.0 copy-start.2
  0.0 1.1 %copy-done.2 = bf16[48,4096]{1,0:T(8,128)(2,1)S(1)} copy-done((bf16[48,4096]{1,0:T(8,128)(2,1)S(1)}, bf16[48,4096]{1,0:T(8,128)(2,1)}, u32[]{:S(2)}) %copy-start.2) | copy-done | bytes 393240
  1.1 0.0 copy-start.3
  1.1 1.0 %copy-done.3 = bf16[48,4096]{1,0:T(8,128)(2,1)S(1)} copy-done((bf16[48,4096]{1,0:T(8,128)(2,1)S(1)}, bf16[48,4096]{1,0:T(8,128)(2,1)}, u32[]{:S(2)}) %copy-start.3) | copy-done | bytes 393240
  2.1 0.0 copy-start.4
  2.1 0.9 %copy-done.4 = bf16[48,1024]{1,0:T(8,128)(2,1)S(1)} copy-done((bf16[48,1024]{1,0:T(8,128)(2,1)S(1)}, bf16[48,1024]{1,0:T(8,128)(2,1)}, u32[]{:S(2)}) %copy-start.4) | copy-done | bytes 98328
  3.0 2.9 %skeleton.1 = (bf16[432,128]{1,0:T(8,128)(2,1)S(1)}, bf16[1536,128]{1,0:T(8,128)(2,1)S(1)}, bf16[1536,128]{1,0:T(8,128)(2,1)S(1)}) custom-call(bf16[48,1024]{1,0:T(8,128)(2,1)S(1)} %copy-done.4, bf16[48,4096]{1,0:T(8,128)(2,1)S(1)} %copy-done.2, bf16[48,4096]{1,0:T(8,128)(2,1)S(1)} %copy-done.3), custom_call_target="tpu_custom_call" | custom-call | tf_op jit(solution)/shard_map/skeleton/pallas_call | solution.py:393
  5.9 0.0 copy-start.1
  5.9 3.5 %collective-permute-start = (bf16[432,128]{1,0:T(8,128)(2,1)S(1)}, bf16[432,128]{1,0:T(8,128)(2,1)S(1)}, u32[]{:S(2)}, u32[]{:S(2)}) collective-permute-start(bf16[432,128]{1,0:T(8,128)(2,1)S(1)} %get-tuple-element.10.su_ref), channel_id=1, source_target_pairs={{0,1},{1,0},{2,3},{3,2},{4,5},{5,4},{6,7},{7,6},{8,9},{9,8},{10,11... | collective-permute-start | bytes 331784 | tf_op jit(solution)/shard_map/ppermute | solution.py:494
  9.4 3.3 %collective-permute-done.rd1_ref = bf16[432,128]{1,0:T(8,128)(2,1)S(1)} collective-permute-done((bf16[432,128]{1,0:T(8,128)(2,1)S(1)}, bf16[432,128]{1,0:T(8,128)(2,1)S(1)}, u32[]{:S(2)}, u32[]{:S(2)}) %collective-permute-start) | collective-permute-done | bytes 110624 | tf_op jit(solution)/shard_map/ppermute | solution.py:494
  12.7 4.7 %collective-permute-start.1 = (bf16[480,128]{1,0:T(8,128)(2,1)S(1)}, bf16[480,128]{1,0:T(8,128)(2,1)S(1)}, u32[]{:S(2)}, u32[]{:S(2)}) collective-permute-start(bf16[480,128]{1,0:T(8,128)(2,1)S(1)} %pad_maximum_fusion.1), channel_id=1, source_target_pairs={{0,3},{1,2},{2,1},{3,0},{4,7},{5,6},{6,5},{7,4},{8,11},{9,10},{10,... | collective-permute-start | bytes 368648 | tf_op jit(solution)/shard_map/ppermute | solution.py:499
  17.4 0.0 copy-start.5
  17.4 3.3 %collective-permute-done.1.rd2_ref = bf16[480,128]{1,0:T(8,128)(2,1)S(1)} collective-permute-done((bf16[480,128]{1,0:T(8,128)(2,1)S(1)}, bf16[480,128]{1,0:T(8,128)(2,1)S(1)}, u32[]{:S(2)}, u32[]{:S(2)}) %collective-permute-start.1) | collective-permute-done | bytes 122912 | tf_op jit(solution)/shard_map/ppermute | solution.py:499
  20.7 9.0 %collective-permute-start.3 = (bf16[576,128]{1,0:T(8,128)(2,1)S(1)}, bf16[576,128]{1,0:T(8,128)(2,1)S(1)}, u32[]{:S(2)}, u32[]{:S(2)}) collective-permute-start(bf16[576,128]{1,0:T(8,128)(2,1)S(1)} %pad_maximum_fusion), channel_id=1, source_target_pairs={{4,0},{8,4},{12,8},{16,12},{20,16},{24,20},{28,24},{32,28},{36,32}... | collective-permute-start | bytes 442376 | tf_op jit(solution)/shard_map/ppermute | solution.py:504
  29.7 1.9 %collective-permute-start.2 = (bf16[576,128]{1,0:T(8,128)(2,1)S(1)}, bf16[576,128]{1,0:T(8,128)(2,1)S(1)}, u32[]{:S(2)}, u32[]{:S(2)}) collective-permute-start(bf16[576,128]{1,0:T(8,128)(2,1)S(1)} %pad_maximum_fusion), channel_id=1, source_target_pairs={{0,4},{4,8},{8,12},{12,16},{16,20},{20,24},{24,28},{28,32},{32,36}... | collective-permute-start | bytes 442376 | tf_op jit(solution)/shard_map/ppermute | solution.py:503
  31.7 0.0 copy-done.5
  31.7 0.5 pack.1.own_ref
  32.2 0.0 copy-start.9
  32.2 8.1 %collective-permute-start.5 = (bf16[480,128]{1,0:T(8,128)(2,1)S(1)}, bf16[480,128]{1,0:T(8,128)(2,1)S(1)}, u32[]{:S(2)}, u32[]{:S(2)}) collective-permute-start(bf16[480,128]{1,0:T(8,128)(2,1)S(1)} %pack.1.own_ref), channel_id=1, source_target_pairs={{1,0},{2,1},{3,2},{4,3},{5,4},{6,5},{7,6},{8,7},{9,8},{10,9},{11,1... | collective-permute-start | bytes 368648 | tf_op jit(solution)/shard_map/ppermute | solution.py:497
  40.3 1.9 %collective-permute-start.4 = (bf16[480,128]{1,0:T(8,128)(2,1)S(1)}, bf16[480,128]{1,0:T(8,128)(2,1)S(1)}, u32[]{:S(2)}, u32[]{:S(2)}) collective-permute-start(bf16[480,128]{1,0:T(8,128)(2,1)S(1)} %pack.1.own_ref), channel_id=1, source_target_pairs={{0,1},{1,2},{2,3},{3,4},{4,5},{5,6},{6,7},{7,8},{8,9},{9,10},{10,1... | collective-permute-start | bytes 368648 | tf_op jit(solution)/shard_map/ppermute | solution.py:496
  42.2 0.0 copy-done.9
  42.2 0.1 copy.11.ids
  42.3 0.0 copy-done
  42.3 0.0 copy-done.1
  42.3 2.0 %tables.1 = (bf16[64,6144]{1,0:T(8,128)(2,1)S(1)}, bf16[64,4096]{1,0:T(8,128)(2,1)S(1)}) custom-call(bf16[96,4096]{1,0:T(8,128)(2,1)S(1)} %copy-done, bf16[64,4096]{1,0:T(8,128)(2,1)S(1)} %copy-done.1), custom_call_target="tpu_custom_call" | custom-call | tf_op jit(solution)/shard_map/tables/pallas_call | solution.py:425
  44.4 0.0 copy-start.8
  44.4 0.1 pad_add_fusion.info
  44.5 0.0 collective-permute-done.5.next_ref
  44.5 6.2 %collective-permute-done.4.prev_ref = bf16[480,128]{1,0:T(8,128)(2,1)S(1)} collective-permute-done((bf16[480,128]{1,0:T(8,128)(2,1)S(1)}, bf16[480,128]{1,0:T(8,128)(2,1)S(1)}, u32[]{:S(2)}, u32[]{:S(2)}) %collective-permute-start.4) | collective-permute-done | bytes 122912 | tf_op jit(solution)/shard_map/ppermute | solution.py:496
  50.7 0.0 copy-done.8
  50.7 0.0 copy-start.6
  50.7 8.5 %near.1.near_ref = f32[384,128]{1,0:T(8,128)S(1)} custom-call(s32[3]{0:T(128)S(1)} %pad_add_fusion.info, s32[48,27]{1,0:T(8,128)S(1)} %copy.11.ids, s32[48]{0:T(128)S(1)} %copy-done.8, bf16[480,128]{1,0:T(8,128)(2,1)S(1)} %pack.1.own_ref, bf16[480,128]{1,0:T(8,128)(2,1)S(1)} %collective-permute-done.4.prev_ref, ...), custom_call_target="tpu_custom_call" | custom-call | tf_op jit(solution)/shard_map/near/pallas_call | solution.py:440
  59.2 0.0 copy-start.7
  59.2 0.0 collective-permute-done.3.bm_ref
  59.2 0.0 collective-permute-done.2.bp_ref
  59.3 0.0 copy-done.6
  59.3 0.6 copy-done.7
  59.9 22.0 %field.1 = f32[48,1024]{1,0:T(8,128)} custom-call(s32[3]{0:T(128)S(1)} %pad_add_fusion.info, s32[48,96]{1,0:T(8,128)S(1)} %copy-done.6, s32[6,64]{1,0:T(8,128)S(1)} %copy-done.7, bf16[432,128]{1,0:T(8,128)(2,1)S(1)} %get-tuple-element.10.su_ref, bf16[432,128]{1,0:T(8,128)(2,1)S(1)} %collective-permute-done.rd1_ref, ...), custom_call_target="tpu_custom_call" | custom-call | tf_op jit(solution)/shard_map/field/pallas_call | solution.py:461
  (4 shorter events, 0.0 us)
Async XLA Ops:
  0.0 42.3 %copy-start = (bf16[96,4096]{1,0:T(8,128)(2,1)S(1)}, bf16[96,4096]{1,0:T(8,128)(2,1)}, u32[]{:S(2)}) copy-start(bf16[96,4096]{1,0:T(8,128)(2,1)} %leaf_ref.1) | copy-start | bytes 2359300
  0.0 1.1 %copy-start.2 = (bf16[48,4096]{1,0:T(8,128)(2,1)S(1)}, bf16[48,4096]{1,0:T(8,128)(2,1)}, u32[]{:S(2)}) copy-start(bf16[48,4096]{1,0:T(8,128)(2,1)} %v_ref.1) | copy-start | bytes 1179652
  1.1 1.0 %copy-start.3 = (bf16[48,4096]{1,0:T(8,128)(2,1)S(1)}, bf16[48,4096]{1,0:T(8,128)(2,1)}, u32[]{:S(2)}) copy-start(bf16[48,4096]{1,0:T(8,128)(2,1)} %e_ref.1) | copy-start | bytes 1179652
  2.1 0.9 %copy-start.4 = (bf16[48,1024]{1,0:T(8,128)(2,1)S(1)}, bf16[48,1024]{1,0:T(8,128)(2,1)}, u32[]{:S(2)}) copy-start(bf16[48,1024]{1,0:T(8,128)(2,1)} %q_ref.3) | copy-start | bytes 294916
  5.9 36.4 %copy-start.1 = (bf16[64,4096]{1,0:T(8,128)(2,1)S(1)}, bf16[64,4096]{1,0:T(8,128)(2,1)}, u32[]{:S(2)}) copy-start(bf16[64,4096]{1,0:T(8,128)(2,1)} %upper_ref.1) | copy-start | bytes 1572868
  5.9 6.8 %collective-permute-start = (bf16[432,128]{1,0:T(8,128)(2,1)S(1)}, bf16[432,128]{1,0:T(8,128)(2,1)S(1)}, u32[]{:S(2)}, u32[]{:S(2)}) collective-permute-start(bf16[432,128]{1,0:T(8,128)(2,1)S(1)} %get-tuple-element.10.su_ref), channel_id=1, source_target_pairs={{0,1},{1,0},{2,3},{3,2},{4,5},{5,4},{6,7},{7,6},{8,9},{9,8},{10,11... | collective-permute-start | bytes 331784 | tf_op jit(solution)/shard_map/ppermute | solution.py:494
  12.7 8.0 %collective-permute-start.1 = (bf16[480,128]{1,0:T(8,128)(2,1)S(1)}, bf16[480,128]{1,0:T(8,128)(2,1)S(1)}, u32[]{:S(2)}, u32[]{:S(2)}) collective-permute-start(bf16[480,128]{1,0:T(8,128)(2,1)S(1)} %pad_maximum_fusion.1), channel_id=1, source_target_pairs={{0,3},{1,2},{2,1},{3,0},{4,7},{5,6},{6,5},{7,4},{8,11},{9,10},{10,... | collective-permute-start | bytes 368648 | tf_op jit(solution)/shard_map/ppermute | solution.py:499
  17.4 14.2 %copy-start.5 = (f32[48,192]{1,0:T(8,128)S(1)}, f32[48,192]{1,0:T(8,128)}, u32[]{:S(2)}) copy-start(f32[48,192]{1,0:T(8,128)} %x_ref.3) | copy-start | bytes 110596
  20.7 38.5 %collective-permute-start.3 = (bf16[576,128]{1,0:T(8,128)(2,1)S(1)}, bf16[576,128]{1,0:T(8,128)(2,1)S(1)}, u32[]{:S(2)}, u32[]{:S(2)}) collective-permute-start(bf16[576,128]{1,0:T(8,128)(2,1)S(1)} %pad_maximum_fusion), channel_id=1, source_target_pairs={{4,0},{8,4},{12,8},{16,12},{20,16},{24,20},{28,24},{32,28},{36,32}... | collective-permute-start | bytes 442376 | tf_op jit(solution)/shard_map/ppermute | solution.py:504
  29.7 29.5 %collective-permute-start.2 = (bf16[576,128]{1,0:T(8,128)(2,1)S(1)}, bf16[576,128]{1,0:T(8,128)(2,1)S(1)}, u32[]{:S(2)}, u32[]{:S(2)}) collective-permute-start(bf16[576,128]{1,0:T(8,128)(2,1)S(1)} %pad_maximum_fusion), channel_id=1, source_target_pairs={{0,4},{4,8},{8,12},{12,16},{16,20},{20,24},{24,28},{28,32},{32,36}... | collective-permute-start | bytes 442376 | tf_op jit(solution)/shard_map/ppermute | solution.py:503
  32.2 10.0 %copy-start.9 = (s32[48,27]{0,1:T(8,128)S(1)}, s32[48,27]{0,1:T(8,128)}, u32[]{:S(2)}) copy-start(s32[48,27]{0,1:T(8,128)} %param.16) | copy-start | bytes 15556
  32.2 12.3 %collective-permute-start.5 = (bf16[480,128]{1,0:T(8,128)(2,1)S(1)}, bf16[480,128]{1,0:T(8,128)(2,1)S(1)}, u32[]{:S(2)}, u32[]{:S(2)}) collective-permute-start(bf16[480,128]{1,0:T(8,128)(2,1)S(1)} %pack.1.own_ref), channel_id=1, source_target_pairs={{1,0},{2,1},{3,2},{4,3},{5,4},{6,5},{7,6},{8,7},{9,8},{10,9},{11,1... | collective-permute-start | bytes 368648 | tf_op jit(solution)/shard_map/ppermute | solution.py:497
  40.3 10.4 %collective-permute-start.4 = (bf16[480,128]{1,0:T(8,128)(2,1)S(1)}, bf16[480,128]{1,0:T(8,128)(2,1)S(1)}, u32[]{:S(2)}, u32[]{:S(2)}) collective-permute-start(bf16[480,128]{1,0:T(8,128)(2,1)S(1)} %pack.1.own_ref), channel_id=1, source_target_pairs={{0,1},{1,2},{2,3},{3,4},{4,5},{5,6},{6,7},{7,8},{8,9},{9,10},{10,1... | collective-permute-start | bytes 368648 | tf_op jit(solution)/shard_map/ppermute | solution.py:496
  44.4 6.3 %copy-start.8 = (s32[48]{0:T(128)S(1)}, s32[48]{0:T(128)}, u32[]{:S(2)}) copy-start(s32[48]{0:T(128)} %counts.1) | copy-start | bytes 580
  50.7 8.5 %copy-start.6 = (s32[48,96]{1,0:T(8,128)S(1)}, s32[48,96]{1,0:T(8,128)}, u32[]{:S(2)}) copy-start(s32[48,96]{1,0:T(8,128)} %ids.2) | copy-start | bytes 55300
  59.2 0.7 copy-start.7

commit v2 on v1

--- a/solution.py
+++ b/solution.py
@@ -20,7 +20,7 @@
 PARENTS = 6
 S_ROWS = PAIRS * 16
 U_ROWS = PARENTS // 2 * 16
-VMEM_LIMIT = 48 * 1024 * 1024
+VMEM_LIMIT = 60 * 1024 * 1024
 
 
 def nn(a, b):
@@ -127,7 +127,7 @@
     ).astype(BF16)
 
 
-def table_kernel(leaf_ref, upper_ref, wl_ref, wu_ref, ts):
+def table_kernel(leaf_ref, upper_ref, after_ref, wl_ref, wu_ref, ts):
     low = iota((32, 128), 1) < 64
     for ref, out, count in ((leaf_ref, wl_ref, OFFSETS), (upper_ref, wu_ref, UPPER)):
         for t in range(32):
@@ -160,17 +160,14 @@
         dst_ref[base + 2 * u + 1] = wide[u * 16 : u * 16 + 16, 128:]
 
 
-STEP = 4
-
-
-def near_kernel(
-    info, ids, counts, own_ref, prev_ref, next_ref, x_ref, out_ref, qt, yt, at, ks, bs, acc, place, sums
-):
-    first = info[0]
+STEP = 8
+TOTAL = 3 * BOXES
+
+
+def near_tables_kernel(own_ref, prev_ref, next_ref, x_ref, after_ref, qt, yt, at, bs):
     for side, ref in enumerate((prev_ref, own_ref, next_ref)):
         spread_pairs(ref, S_ROWS, qt, side * BOXES)
-    qt[3 * BOXES] = jnp.zeros((16, 128), BF16)
-    total = 3 * BOXES
+    qt[TOTAL] = jnp.zeros((16, 128), BF16)
     lanes = iota((BOXES, 128), 1) < 64
 
     def dup3(xy, z):
@@ -185,10 +182,10 @@
         y0, y1, y2 = dup3(xy, z)
         n = split3(SCALE * (y0 * y0 + y1 * y1 + y2 * y2))
         for k, v in enumerate((y0, y0, y0, y1, y1, y1, y2, y2, y2, *n, ones, ones, ones, zeros)):
-            bs[k * BOXES : (k + 1) * BOXES] = v
+            bs[side, k * BOXES : (k + 1) * BOXES] = v
         for b in range(BOXES):
-            yt[side * BOXES + b] = bs[pl.ds(b, 16, stride=BOXES), :].astype(BF16)
-    yt[total] = onehot(iota((16, 128), 0) >= 12)
+            yt[side * BOXES + b] = bs[side, pl.ds(b, 16, stride=BOXES), :].astype(BF16)
+    yt[TOTAL] = onehot(iota((16, 128), 0) >= 12)
     zx = jnp.concatenate([x_ref[:, 128:], jnp.zeros((BOXES, 64), F32)], axis=1)
     x0, x1, x2 = dup3(x_ref[:, :128], zx)
     n = split3(SCALE * (x0 * x0 + x1 * x1 + x2 * x2 + SOFT))
@@ -196,69 +193,67 @@
     for x in (x0, x1, x2):
         cols += list(split3((-2.0 * SCALE) * x))
     for k, v in enumerate((*cols, ones, ones, ones, *n, zeros)):
-        bs[k * BOXES : (k + 1) * BOXES] = v
+        bs[3, k * BOXES : (k + 1) * BOXES] = v
     eye = onehot((iota((64, 128), 0) == iota((64, 128), 1)))
     for b in range(BOXES):
-        at[b] = nt(eye, bs[pl.ds(b, 16, stride=BOXES), :].astype(BF16)).astype(BF16)
+        at[b] = nt(eye, bs[3, pl.ds(b, 16, stride=BOXES), :].astype(BF16)).astype(BF16)
+    at[BOXES] = jnp.zeros((64, 16), BF16) + onehot(iota((64, 16), 1) == 12)
+
+
+def near_kernel(info, ids_ref, count_ref, qt, yt, at, after_ref, out_ref, slot_v, slot_s, ks, qs, acc, place, sums, sem):
+    first = info[0]
+    r48 = iota((BOXES, BOXES), 0)
+    counts = jnp.sum(
+        jnp.where(r48 == iota((BOXES, BOXES), 1), jnp.broadcast_to(count_ref[...], (BOXES, BOXES)), 0),
+        axis=1,
+        keepdims=True,
+    )
+    slot_v[...] = jnp.full((BOXES + 8, 128), TOTAL, jnp.int32)
+    slot_v[:BOXES, :NEAR] = jnp.where(iota((BOXES, NEAR), 1) < counts, ids_ref[...] - first, TOTAL)
+    slot_v[:BOXES, 32:33] = counts
+    slot_v[BOXES : BOXES + 8, 32:33] = jnp.zeros((8, 1), jnp.int32)
+    copy = pltpu.make_async_copy(slot_v, slot_s, sem)
+    copy.start()
+    for b in range(BOXES + 1):
         acc[b] = jnp.zeros((16, 64), F32)
-    acc[BOXES] = jnp.zeros((16, 64), F32)
-    at[BOXES] = jnp.zeros((64, 16), BF16) + onehot(iota((64, 16), 1) == 12)
     low = iota((16, 128), 1) < 64
-
-    def advance(box, chunk):
-        here = jnp.minimum(box, BOXES - 1)
-        more = (chunk + 1) * 8 < counts[here]
-        return jnp.where(more, box, box + 1), jnp.where(more, chunk + 1, 0)
-
-    def gather(table, sources):
-        tiles = [
-            jnp.where(low, table[sources[2 * j]], table[sources[2 * j + 1]])
-            for j in range(len(sources) // 2)
-        ]
-        return jnp.concatenate(tiles, axis=1)
+    for j in range(STEP):
+        place[STEP + j] = BOXES
+        ks[1, j] = jnp.zeros((64, 512), BF16)
+        qs[1, j] = jnp.zeros((16, 512), BF16)
+    copy.wait()
+
+    def finish(last):
+        for j in range(STEP):
+            here = place[last * STEP + j]
+            acc[here] += nt(qs[last, j], ks[last, j])
 
     def work(state):
         step, box, chunk = state
         slot = step % 2
-        last = 1 - slot
+        finish(1 - slot)
         for j in range(STEP):
-            kernel = ks[last, j]
-            here = place[last * STEP * 9 + j * 9]
-            sources = [place[last * STEP * 9 + j * 9 + 1 + c] for c in range(8)]
-            acc[here] += nt(gather(qt, sources), kernel)
-        for j in range(STEP):
-            target = jnp.minimum(box, BOXES)
-            here = jnp.minimum(box, BOXES - 1)
-            used = counts[here]
-            sources = []
-            for c in range(8):
-                n = chunk * 8 + c
-                g = ids[here, jnp.minimum(n, NEAR - 1)] - first
-                sources.append(jnp.where((n < used) & (box < BOXES), g, total))
-            place[slot * STEP * 9 + j * 9] = target
-            for c in range(8):
-                place[slot * STEP * 9 + j * 9 + 1 + c] = sources[c]
-            d = nn(at[target], gather(yt, sources))
+            place[slot * STEP + j] = box
+            ys = []
+            for c in range(4):
+                one = slot_s[box, chunk + 2 * c]
+                two = slot_s[box, chunk + 2 * c + 1]
+                ys.append(jnp.where(low, yt[one], yt[two]))
+                qs[slot, j, :, c * 128 : (c + 1) * 128] = jnp.where(low, qt[one], qt[two])
+            d = nn(at[box], jnp.concatenate(ys, axis=1))
             ks[slot, j] = lax.rsqrt(d).astype(BF16)
-            box, chunk = advance(box, chunk)
+            more = chunk + 8 < slot_s[box, 32]
+            box = jnp.where(more, box, jnp.minimum(box + 1, BOXES))
+            chunk = jnp.where(more, chunk + 8, 0)
         return step + 1, box, chunk
 
-    for j in range(STEP):
-        place[STEP * 9 + j * 9] = BOXES
-        for c in range(8):
-            place[STEP * 9 + j * 9 + 1 + c] = total
-        ks[1, j] = jnp.zeros((64, 512), BF16)
     step, _, _ = lax.while_loop(lambda s: s[1] < BOXES, work, (0, 0, 0))
-    last = 1 - step % 2
-    for j in range(STEP):
-        here = place[last * STEP * 9 + j * 9]
-        sources = [place[last * STEP * 9 + j * 9 + 1 + c] for c in range(8)]
-        acc[here] += nt(gather(qt, sources), ks[last, j])
+    finish(1 - step % 2)
     lane8 = iota((8, 128), 1) // 16
     for g in range(BOXES // 8):
         rows = jnp.concatenate([acc[g * 8 + c] for c in range(8)], axis=0)
-        sums[...] = rows.T
-        tiles = [sums[pl.ds(s, 8, stride=8), :] for s in range(8)]
+        sums[g] = rows.T
+        tiles = [sums[g, pl.ds(s, 8, stride=8), :] for s in range(8)]
         for c in range(8):
             total_tile = None
             for s in range(8):
@@ -267,35 +262,31 @@
             out_ref[pl.ds(g * 8 + c, 8, stride=BOXES), :] = total_tile
 
 
-def couple(table, w_ref, ids, base, first, boxes, offsets, low):
-    quads = offsets // 4
-
-    def body(k, total):
-        rows = []
-        for b in range(boxes):
-            g = [ids[base + b, k * 4 + j] - first for j in range(4)]
-            rows.append(
-                jnp.concatenate(
-                    [jnp.where(low, table[g[0]], table[g[1]]), jnp.where(low, table[g[2]], table[g[3]])],
-                    axis=1,
-                )
-            )
-        lhs = jnp.concatenate(rows, axis=0)
-        return total + nt(lhs, w_ref[:, pl.ds(pl.multiple_of(k * 256, 256), 256)])
-
-    return lax.fori_loop(0, quads, body, jnp.zeros((boxes * 16, 64), F32))
-
-
-GROUP = 16
+def couple(table, w_ref, ids, boxes, offsets, low):
+    rows = []
+    for b in range(boxes):
+        tiles = []
+        for o in range(0, offsets, 2):
+            one = table[ids[b, o]]
+            two = table[ids[b, o + 1]]
+            tiles.append(jnp.where(low, one, two))
+        rows.append(jnp.concatenate(tiles, axis=1))
+    lhs = jnp.concatenate(rows, axis=0)
+    return nt(lhs, w_ref[...])
 
 
 def field_kernel(
-    info, ids, pids, su_ref, rd1_ref, rd2_ref, bp_ref, bm_ref, wl_ref, wu_ref, xv_ref, xe_ref, near_ref,
-    out_ref, st, ut, halo, fs, ps,
+    info, leaf_ref, pid_ref, su_ref, rd1_ref, rd2_ref, bp_ref, bm_ref, wl_ref, wu_ref, xv_ref, xe_ref, near_ref,
+    out_ref, st, ut, halo, fs, ps, ids_v, ids, pids_v, pids, sems,
 ):
     first = info[0]
     first_parent = info[1]
     sub = info[2]
+    ids_v[:, :OFFSETS] = leaf_ref[...] - first
+    pids_v[:PARENTS, :UPPER] = pid_ref[...] - first_parent
+    copies = [pltpu.make_async_copy(ids_v, ids, sems.at[0]), pltpu.make_async_copy(pids_v, pids, sems.at[1])]
+    for copy in copies:
+        copy.start()
     low = iota((16, 128), 1) < 64
 
     @pl.when(sub == 0)
@@ -337,7 +328,9 @@
     parents(rd2_ref, S_ROWS, 1, 3)
     parents(rd2_ref, S_ROWS + U_ROWS, 1, 2)
 
-    upper = couple(ut, wu_ref, pids, 0, first_parent, PARENTS, UPPER, low)
+    for copy in copies:
+        copy.wait()
+    upper = couple(ut, wu_ref, pids, PARENTS, UPPER, low)
     r64 = iota((64, 128), 0)
     c64 = iota((64, 128), 1)
     natural = onehot((c64 % 64) == 2 * (r64 % 32) + r64 // 32)
@@ -355,27 +348,24 @@
             fs[(p * 8 + c) * 16 : (p * 8 + c + 1) * 16] = jnp.where(lane16 < 32, a, b)
     lane8 = iota((8, 128), 1) // 32
     low64 = iota((16, 128), 1) < 64
-    for h in range(BOXES // GROUP):
-        part = couple(st, wl_ref, ids, h * GROUP, first, GROUP, OFFSETS, low)
-        field = (part + fs[h * GROUP * 16 : (h + 1) * GROUP * 16, :64]).astype(BF16)
-        wide = nn(field, natural)
-        for q in range(GROUP // 4):
-            parts = []
-            for c in range(4):
-                f = wide[(q * 4 + c) * 16 : (q * 4 + c + 1) * 16]
-                parts += [jnp.where(low64, f, 0.0), jnp.where(low64, 0.0, f)]
-            weights = jnp.concatenate(parts, axis=0).astype(BF16)
-            g = h * (GROUP // 4) + q
-            far = nt(xv_ref[g * 128 : (g + 1) * 128], weights)
-            for c in range(4):
-                tile = None
-                for m in range(4):
-                    piece = far[c * 32 + m * 8 : c * 32 + m * 8 + 8]
-                    if m != c:
-                        piece = pltpu.roll(piece, (32 * (m - c)) % 128, 1)
-                    tile = piece if tile is None else jnp.where(lane8 == m, piece, tile)
-                rows = pl.ds(g * 4 + c, 8, stride=BOXES)
-                ps[rows, :] = tile
+    part = couple(st, wl_ref, ids, BOXES, OFFSETS, low)
+    field = (part + fs[:, :64]).astype(BF16)
+    wide = nn(field, natural)
+    for g in range(BOXES // 4):
+        parts = []
+        for c in range(4):
+            f = wide[(g * 4 + c) * 16 : (g * 4 + c + 1) * 16]
+            parts += [jnp.where(low64, f, 0.0), jnp.where(low64, 0.0, f)]
+        weights = jnp.concatenate(parts, axis=0).astype(BF16)
+        far = nt(xv_ref[g * 128 : (g + 1) * 128], weights)
+        for c in range(4):
+            tile = None
+            for m in range(4):
+                piece = far[c * 32 + m * 8 : c * 32 + m * 8 + 8]
+                if m != c:
+                    piece = pltpu.roll(piece, (32 * (m - c)) % 128, 1)
+                tile = piece if tile is None else jnp.where(lane8 == m, piece, tile)
+            ps[pl.ds(g * 4 + c, 8, stride=BOXES), :] = tile
     for i in range(8):
         rows = slice(i * BOXES, (i + 1) * BOXES)
         out_ref[:, i * 128 : (i + 1) * 128] = near_ref[rows] + ps[rows]
@@ -385,18 +375,26 @@
 SM = pl.BlockSpec(memory_space=pltpu.SMEM)
 
 
+HB = pl.BlockSpec(memory_space=pl.ANY)
+PEAK = 1.0e15
+
+
 def params():
     return pltpu.CompilerParams(vmem_limit_bytes=VMEM_LIMIT)
+
+
+def cost(us):
+    return pl.CostEstimate(flops=int(us * 1e-6 * PEAK), bytes_accessed=1 << 20, transcendentals=0)
+
+
+def shape(*dims, dtype=BF16):
+    return jax.ShapeDtypeStruct(dims, dtype)
 
 
 def run_skeleton(charges, basis, transfer):
     return pl.pallas_call(
         skeleton_kernel,
-        out_shape=(
-            jax.ShapeDtypeStruct((S_ROWS + U_ROWS, 128), BF16),
-            jax.ShapeDtypeStruct((BOXES * 32, 128), BF16),
-            jax.ShapeDtypeStruct((BOXES * 32, 128), BF16),
-        ),
+        out_shape=(shape(S_ROWS + U_ROWS, 128), shape(BOXES * 32, 128), shape(BOXES * 32, 128)),
         in_specs=[VM] * 3,
         out_specs=(VM,) * 3,
         scratch_shapes=[
@@ -405,6 +403,7 @@
             pltpu.VMEM((32 * BOXES, 128), F32),
         ],
         compiler_params=params(),
+        cost_estimate=cost(4.0),
         name="skeleton",
     )(charges, basis, transfer)
 
@@ -412,56 +411,69 @@
 def run_pack(charges, coords):
     return pl.pallas_call(
         pack_kernel,
-        out_shape=jax.ShapeDtypeStruct((S_ROWS + 2 * BOXES, 128), BF16),
+        out_shape=shape(S_ROWS + 2 * BOXES, 128),
         in_specs=[VM] * 2,
         out_specs=VM,
         scratch_shapes=[pltpu.VMEM((8 * BOXES, 128), F32)],
         compiler_params=params(),
+        cost_estimate=cost(2.0),
         name="pack",
     )(charges, coords)
 
 
-def run_tables(leaf_table, upper_table):
+def run_tables(leaf_table, upper_table, su):
     return pl.pallas_call(
         table_kernel,
-        out_shape=(
-            jax.ShapeDtypeStruct((64, OFFSETS * 64), BF16),
-            jax.ShapeDtypeStruct((64, UPPER * 64), BF16),
-        ),
-        in_specs=[VM] * 2,
+        out_shape=(shape(64, OFFSETS * 64), shape(64, UPPER * 64)),
+        in_specs=[VM] * 2 + [HB],
         out_specs=(VM,) * 2,
         scratch_shapes=[pltpu.VMEM((32 * OFFSETS, 128), F32)],
         compiler_params=params(),
+        cost_estimate=cost(4.0),
         name="tables",
-    )(leaf_table, upper_table)
-
-
-def run_near(info, near_ids, near_count, own, before, after, coords):
+    )(leaf_table, upper_table, su)
+
+
+def run_near_tables(own, before, after, coords, wl):
+    return pl.pallas_call(
+        near_tables_kernel,
+        out_shape=(shape(TOTAL + 1, 16, 128), shape(TOTAL + 1, 16, 128), shape(BOXES + 1, 64, 16)),
+        in_specs=[VM] * 4 + [HB],
+        out_specs=(VM,) * 3,
+        scratch_shapes=[pltpu.VMEM((4, 16 * BOXES, 128), F32)],
+        compiler_params=params(),
+        cost_estimate=cost(4.0),
+        name="near_tables",
+    )(own, before, after, coords, wl)
+
+
+def run_near(info, near_ids, near_count, qt, yt, at, rd2):
     return pl.pallas_call(
         near_kernel,
-        out_shape=jax.ShapeDtypeStruct((8 * BOXES, 128), F32),
-        in_specs=[SM] * 3 + [VM] * 4,
+        out_shape=shape(8 * BOXES, 128, dtype=F32),
+        in_specs=[SM] + [VM] * 5 + [HB],
         out_specs=VM,
         scratch_shapes=[
-            pltpu.VMEM((3 * BOXES + 1, 16, 128), BF16),
-            pltpu.VMEM((3 * BOXES + 1, 16, 128), BF16),
-            pltpu.VMEM((BOXES + 1, 64, 16), BF16),
+            pltpu.VMEM((BOXES + 8, 128), jnp.int32),
+            pltpu.SMEM((BOXES + 8, 128), jnp.int32),
             pltpu.VMEM((2, STEP, 64, 512), BF16),
-            pltpu.VMEM((16 * BOXES, 128), F32),
+            pltpu.VMEM((2, STEP, 16, 512), BF16),
             pltpu.VMEM((BOXES + 1, 16, 64), F32),
-            pltpu.SMEM((2 * STEP * 9,), jnp.int32),
-            pltpu.VMEM((64, 128), F32),
+            pltpu.SMEM((2 * STEP,), jnp.int32),
+            pltpu.VMEM((BOXES // 8, 64, 128), F32),
+            pltpu.SemaphoreType.DMA,
         ],
         compiler_params=params(),
+        cost_estimate=cost(7.0),
         name="near",
-    )(info, near_ids, near_count, own, before, after, coords)
+    )(info, near_ids, near_count.reshape(1, BOXES), qt, yt, at, rd2)
 
 
 def run_field(info, leaf_ids, parent_ids, su, rd1, rd2, bp, bm, wl, wu, xv, xe, near):
     return pl.pallas_call(
         field_kernel,
-        out_shape=jax.ShapeDtypeStruct((BOXES, 1024), F32),
-        in_specs=[SM] * 3 + [VM] * 10,
+        out_shape=shape(BOXES, 1024, dtype=F32),
+        in_specs=[SM] + [VM] * 12,
         out_specs=VM,
         scratch_shapes=[
             pltpu.VMEM((3 * BOXES, 16, 128), BF16),
@@ -469,8 +481,14 @@
             pltpu.VMEM((2, S_ROWS, 128), BF16),
             pltpu.VMEM((BOXES * 16, 128), F32),
             pltpu.VMEM((8 * BOXES, 128), F32),
+            pltpu.VMEM((BOXES, 128), jnp.int32),
+            pltpu.SMEM((BOXES, 128), jnp.int32),
+            pltpu.VMEM((8, 128), jnp.int32),
+            pltpu.SMEM((8, 128), jnp.int32),
+            pltpu.SemaphoreType.DMA((2,)),
         ],
         compiler_params=params(),
+        cost_estimate=cost(9.0),
         name="field",
     )(info, leaf_ids, parent_ids, su, rd1, rd2, bp, bm, wl, wu, xv, xe, near)
 
@@ -490,19 +508,20 @@
             sub,
         ]
     ).astype(jnp.int32)
-    su, xv, xe = run_skeleton(charges, basis, transfer)
-    rd1 = lax.ppermute(su, "sub", [(i, i ^ 1) for i in range(subs)])
     own = run_pack(charges, coords)
     before = lax.ppermute(own, flat, [(i, i + 1) for i in range(chain - 1)])
     after = lax.ppermute(own, flat, [(i + 1, i) for i in range(chain - 1)])
-    wl, wu = run_tables(leaf_table, upper_table)
+    su, xv, xe = run_skeleton(charges, basis, transfer)
+    rd1 = lax.ppermute(su, "sub", [(i, i ^ 1) for i in range(subs)])
+    wl, wu = run_tables(leaf_table, upper_table, su)
     rd2 = lax.ppermute(
         jnp.concatenate([su, rd1[S_ROWS:]], axis=0), "sub", [(i, i ^ 3) for i in range(subs)]
     )
+    qt, yt, at = run_near_tables(own, before, after, coords, wl)
     edge = jnp.concatenate([rd2, su[S_ROWS:], rd1[S_ROWS:]], axis=0)
     bp = lax.ppermute(edge, "box", [(i, i + 1) for i in range(boxes - 1)])
     bm = lax.ppermute(edge, "box", [(i + 1, i) for i in range(boxes - 1)])
-    near = run_near(info, near_ids, near_count, own, before, after, coords)
+    near = run_near(info, near_ids, near_count, qt, yt, at, rd2)
     return run_field(info, leaf_ids, parent_ids, su, rd1, rd2, bp, bm, wl, wu, xv, xe, near)
 
 

time: 82.4 us -> 65.6 us (0.80)
  waiting for transfers between devices: 12.8 us -> 2.37 us
  Pallas kernels: 36 us -> 31.3 us
  starting transfers between devices: 29.1 us -> 26.6 us
    ppermute x1, waiting for transfers between devices: 6.24 us -> 0.01 us  [local(): before = lax.ppermute(own, flat, [(i, i + 1) for i in range(chain - 1)])]
    pallas_call x5 -> x6, Pallas kernels: 36 us -> 31.3 us  [the longest x1 8.81 us: run_field(): pl.pallas_call(field_kernel, out_shape=shape(BOXES, 1024, dtype=F32), in_...]
    ppermute x1, starting transfers between devices: 8.09 us -> 11.7 us  [local(): after = lax.ppermute(own, flat, [(i + 1, i) for i in range(chain - 1)])]
    ppermute x1, waiting for transfers between devices: 3.29 us -> 0.01 us  [local(): rd1 = lax.ppermute(su, 'sub', [(i, i ^ 1) for i in range(subs)])]
    ppermute x1, starting transfers between devices: 9 us -> 5.75 us  [local(): bm = lax.ppermute(edge, 'box', [(i + 1, i) for i in range(boxes - 1)])]
    ppermute x1, starting transfers between devices: 4.67 us -> 1.91 us  [local(): lax.ppermute(jnp.concatenate([su, rd1[S_ROWS:]], axis=0), 'sub', [(i, i ^...]
    ppermute x1, starting transfers between devices: 3.53 us -> 1.91 us  [local(): rd1 = lax.ppermute(su, 'sub', [(i, i ^ 1) for i in range(subs)])]
    ppermute x1, starting transfers between devices: 1.92 us -> 3.39 us  [local(): before = lax.ppermute(own, flat, [(i, i + 1) for i in range(chain - 1)])]
  transfers between devices with their start and end apart: 6 -> 6, of which waited for: 3 -> 1; matrix products, arithmetic and copies ran while one was open for 0% -> 2% of each run, Pallas kernels for 13% -> 32%
where the time goes in v2:
time: 65.6 us; the launch traced here: 64.6 us
  Pallas kernels  31.3 us (48%)
  starting transfers between devices  26.6 us (41%)
  local copies, waits for them, and re-layouts  3.44 us (5%)
  waiting for transfers between devices  2.37 us (4%)
    ppermute x1, starting transfers between devices, local(): after = lax.ppermute(own, flat, [(i + 1, i) for i in range(chain - 1)])  11.7 us
    pallas_call x1, Pallas kernels, run_field(): pl.pallas_call(field_kernel, out_shape=shape(BOXES, 1024, dtype=F32), in_...  8.81 us
    pallas_call x1, Pallas kernels, run_near(): pl.pallas_call(near_kernel, out_shape=shape(8 * BOXES, 128, dtype=F32), i...  8.53 us
    ppermute x1, starting transfers between devices, local(): bm = lax.ppermute(edge, 'box', [(i + 1, i) for i in range(boxes - 1)])  5.75 us
    pallas_call x1, Pallas kernels, run_skeleton(): pl.pallas_call(skeleton_kernel, out_shape=(shape(S_ROWS + U_ROWS, 128), s...  4.75 us
    pallas_call x1, Pallas kernels, run_tables(): pl.pallas_call(table_kernel, out_shape=(shape(64, OFFSETS * 64), shape(64...  4.14 us
    unnamed x17, local copies, waits for them, and re-layouts  3.43 us
    ppermute x1, starting transfers between devices, local(): before = lax.ppermute(own, flat, [(i, i + 1) for i in range(chain - 1)])  3.39 us
  transfers between devices with their start and end apart: 6, of which 1 were waited for; matrix products, arithmetic and copies ran while one was open for 2% of the time, Pallas kernels for 32%

profile of v2, /device:TPU:24, one launch (start us, length us, event | category | flops | bytes accessed | tf_op | source)
XLA Modules:
  0.0 64.6 jit_solution(5280713651010541543)
XLA Ops:
  0.0 2.1 %pack.1.own_ref = bf16[480,128]{1,0:T(8,128)(2,1)} custom-call(bf16[48,1024]{1,0:T(8,128)(2,1)} %q_ref.3, f32[48,192]{1,0:T(8,128)} %x_ref.3), custom_call_target="tpu_custom_call" | custom-call | flops 2000000000 | bytes 1048576 | tf_op jit(solution)/shard_map/pack/pallas_call | solution.py:412
  2.1 3.4 %collective-permute-start.4 = (bf16[480,128]{1,0:T(8,128)(2,1)}, bf16[480,128]{1,0:T(8,128)(2,1)S(1)}, u32[]{:S(2)}, u32[]{:S(2)}) collective-permute-start(bf16[480,128]{1,0:T(8,128)(2,1)} %pack.1.own_ref), channel_id=1, source_target_pairs={{0,1},{1,2},{2,3},{3,4},{4,5},{5,6},{6,7},{7,8},{8,9},{9,10},{10,1... | collective-permute-start | bytes 368648 | tf_op jit(solution)/shard_map/ppermute | solution.py:512
  5.5 11.7 %collective-permute-start.5 = (bf16[480,128]{1,0:T(8,128)(2,1)}, bf16[480,128]{1,0:T(8,128)(2,1)S(1)}, u32[]{:S(2)}, u32[]{:S(2)}) collective-permute-start(bf16[480,128]{1,0:T(8,128)(2,1)} %pack.1.own_ref), channel_id=1, source_target_pairs={{1,0},{2,1},{3,2},{4,3},{5,4},{6,5},{7,6},{8,7},{9,8},{10,9},{11,1... | collective-permute-start | bytes 368648 | tf_op jit(solution)/shard_map/ppermute | solution.py:513
  17.2 4.7 %skeleton.1 = (bf16[432,128]{1,0:T(8,128)(2,1)}, bf16[1536,128]{1,0:T(8,128)(2,1)}, bf16[1536,128]{1,0:T(8,128)(2,1)}) custom-call(bf16[48,1024]{1,0:T(8,128)(2,1)} %q_ref.3, bf16[48,4096]{1,0:T(8,128)(2,1)} %v_ref.1, bf16[48,4096]{1,0:T(8,128)(2,1)} %e_ref.1), custom_call_target="tpu_custom_call" | custom-call | flops 4000000000 | bytes 1048576 | tf_op jit(solution)/shard_map/skeleton/pallas_call | solution.py:395
  22.0 1.9 %collective-permute-start = (bf16[432,128]{1,0:T(8,128)(2,1)}, bf16[432,128]{1,0:T(8,128)(2,1)S(1)}, u32[]{:S(2)}, u32[]{:S(2)}) collective-permute-start(bf16[432,128]{1,0:T(8,128)(2,1)} %get-tuple-element.13.after_ref.su_ref), channel_id=1, source_target_pairs={{0,1},{1,0},{2,3},{3,2},{4,5},{5,4},{6,7},{7,6},{8,9},{9,8},{10,11... | collective-permute-start | bytes 331784 | tf_op jit(solution)/shard_map/ppermute | solution.py:515
  23.9 0.0 copy-start
  23.9 4.1 %tables.1 = (bf16[64,6144]{1,0:T(8,128)(2,1)}, bf16[64,4096]{1,0:T(8,128)(2,1)}) custom-call(bf16[96,4096]{1,0:T(8,128)(2,1)} %leaf_ref.2, bf16[64,4096]{1,0:T(8,128)(2,1)} %upper_ref.1, bf16[432,128]{1,0:T(8,128)(2,1)} %get-tuple-element.13.after_ref.su_ref), custom_call_target="tpu_custom_call" | custom-call | flops 4000000000 | bytes 1048576 | tf_op jit(solution)/shard_map/tables/pallas_call | solution.py:425
  28.0 0.0 copy-start.2
  28.0 0.6 pad_add_fusion.info
  28.6 0.0 copy-done
  28.6 0.1 copy-done.2
  28.8 0.7 %copy.11.ids_ref = s32[48,27]{1,0:T(8,128)} copy(s32[48,27]{0,1:T(8,128)S(1)} %copy-done.2) | data formatting | bytes 10368 | tf_op args[6]
  29.4 0.0 collective-permute-done.rd1_ref
  29.5 0.0 copy-start.3
  29.5 0.6 copy-done.3
  30.1 1.9 %collective-permute-start.1 = (bf16[480,128]{1,0:T(8,128)(2,1)S(1)}, bf16[480,128]{1,0:T(8,128)(2,1)S(1)}, u32[]{:S(2)}, u32[]{:S(2)}) collective-permute-start(bf16[480,128]{1,0:T(8,128)(2,1)S(1)} %pad_maximum_fusion.1), channel_id=1, source_target_pairs={{0,3},{1,2},{2,1},{3,0},{4,7},{5,6},{6,5},{7,4},{8,11},{9,10},{10,... | collective-permute-start | bytes 368648 | tf_op jit(solution)/shard_map/ppermute | solution.py:517
  32.0 0.0 collective-permute-done.4.prev_ref
  32.0 0.0 copy-start.6
  32.0 0.0 collective-permute-done.5.next_ref
  32.0 0.0 copy-start.7
  32.0 0.6 copy-done.6
  32.7 0.1 copy-done.7
  32.7 3.0 %near_tables.1 = (bf16[145,16,128]{2,1,0:T(8,128)(2,1)}, bf16[145,16,128]{2,1,0:T(8,128)(2,1)}, bf16[49,64,16]{2,1,0:T(8,128)(2,1)}) custom-call(bf16[480,128]{1,0:T(8,128)(2,1)} %pack.1.own_ref, bf16[480,128]{1,0:T(8,128)(2,1)} %copy-done.6, bf16[480,128]{1,0:T(8,128)(2,1)} %copy-done.7, f32[48,192]{1,0:T(8,128)} %x_ref.3, ...), custom_call_target="tpu_custom_call" | custom-call | flops 4000000000 | bytes 1048576 | tf_op jit(solution)/shard_map/near_tables/pallas_call | solution.py:438
  35.7 2.4 %collective-permute-done.1.after_ref.rd2_ref = bf16[480,128]{1,0:T(8,128)(2,1)S(1)} collective-permute-done((bf16[480,128]{1,0:T(8,128)(2,1)S(1)}, bf16[480,128]{1,0:T(8,128)(2,1)S(1)}, u32[]{:S(2)}, u32[]{:S(2)}) %collective-permute-start.1) | collective-permute-done | bytes 122912 | tf_op jit(solution)/shard_map/ppermute | solution.py:517
  38.1 0.0 copy-start.1
  38.1 0.6 copy-done.1
  38.7 1.9 %collective-permute-start.2 = (bf16[576,128]{1,0:T(8,128)(2,1)S(1)}, bf16[576,128]{1,0:T(8,128)(2,1)S(1)}, u32[]{:S(2)}, u32[]{:S(2)}) collective-permute-start(bf16[576,128]{1,0:T(8,128)(2,1)S(1)} %pad_maximum_fusion), channel_id=1, source_target_pairs={{0,4},{4,8},{8,12},{12,16},{16,20},{20,24},{24,28},{28,32},{32,36}... | collective-permute-start | bytes 442376 | tf_op jit(solution)/shard_map/ppermute | solution.py:522
  40.6 5.8 %collective-permute-start.3 = (bf16[576,128]{1,0:T(8,128)(2,1)S(1)}, bf16[576,128]{1,0:T(8,128)(2,1)S(1)}, u32[]{:S(2)}, u32[]{:S(2)}) collective-permute-start(bf16[576,128]{1,0:T(8,128)(2,1)S(1)} %pad_maximum_fusion), channel_id=1, source_target_pairs={{4,0},{8,4},{12,8},{16,12},{20,16},{24,20},{28,24},{32,28},{36,32}... | collective-permute-start | bytes 442376 | tf_op jit(solution)/shard_map/ppermute | solution.py:523
  46.4 8.5 %near.1.near_ref = f32[384,128]{1,0:T(8,128)} custom-call(s32[3]{0:T(128)} %pad_add_fusion.info, s32[48,27]{1,0:T(8,128)} %copy.11.ids_ref, s32[1,48]{1,0:T(1,128)} %bitcast.4, bf16[145,16,128]{2,1,0:T(8,128)(2,1)} %get-tuple-element.18.qt, bf16[145,16,128]{2,1,0:T(8,128)(2,1)} %get-tuple-element.19.yt, bf16[49,64,16]{2,1,0:T(8,128)(2,1)} %get-tuple-element.20.at, ...), custom_call_target="tpu_custom_call" | custom-call | flops 7000000000 | bytes 1048576 | tf_op jit(solution)/shard_map/near/pallas_call | solution.py:451
  54.9 0.0 collective-permute-done.2.bp_ref
  54.9 0.0 copy-start.4
  54.9 0.0 collective-permute-done.3.bm_ref
  55.0 0.0 copy-start.5
  55.0 0.6 copy-done.4
  55.6 0.1 copy-done.5
  55.6 8.8 %field.1 = f32[48,1024]{1,0:T(8,128)} custom-call(s32[3]{0:T(128)} %pad_add_fusion.info, s32[48,96]{1,0:T(8,128)} %leaf_ref.3, s32[6,64]{1,0:T(8,128)} %pid_ref.1, bf16[432,128]{1,0:T(8,128)(2,1)} %get-tuple-element.13.after_ref.su_ref, bf16[432,128]{1,0:T(8,128)(2,1)} %copy-done.3, bf16[480,128]{1,0:T(8,128)(2,1)} %copy-done.1, bf16[576,128]{1,0:T(8,128)(2,1)} %copy-done.4, ...), custom_call_target="tpu_custom_call" | custom-call | flops 8999999488 | bytes 1048576 | tf_op jit(solution)/shard_map/field/pallas_call | solution.py:473
  (4 shorter events, 0.0 us)
Async XLA Ops:
  2.1 29.9 %collective-permute-start.4 = (bf16[480,128]{1,0:T(8,128)(2,1)}, bf16[480,128]{1,0:T(8,128)(2,1)S(1)}, u32[]{:S(2)}, u32[]{:S(2)}) collective-permute-start(bf16[480,128]{1,0:T(8,128)(2,1)} %pack.1.own_ref), channel_id=1, source_target_pairs={{0,1},{1,2},{2,3},{3,4},{4,5},{5,6},{6,7},{7,8},{8,9},{9,10},{10,1... | collective-permute-start | bytes 368648 | tf_op jit(solution)/shard_map/ppermute | solution.py:512
  5.5 26.6 %collective-permute-start.5 = (bf16[480,128]{1,0:T(8,128)(2,1)}, bf16[480,128]{1,0:T(8,128)(2,1)S(1)}, u32[]{:S(2)}, u32[]{:S(2)}) collective-permute-start(bf16[480,128]{1,0:T(8,128)(2,1)} %pack.1.own_ref), channel_id=1, source_target_pairs={{1,0},{2,1},{3,2},{4,3},{5,4},{6,5},{7,6},{8,7},{9,8},{10,9},{11,1... | collective-permute-start | bytes 368648 | tf_op jit(solution)/shard_map/ppermute | solution.py:513
  22.0 7.5 %collective-permute-start = (bf16[432,128]{1,0:T(8,128)(2,1)}, bf16[432,128]{1,0:T(8,128)(2,1)S(1)}, u32[]{:S(2)}, u32[]{:S(2)}) collective-permute-start(bf16[432,128]{1,0:T(8,128)(2,1)} %get-tuple-element.13.after_ref.su_ref), channel_id=1, source_target_pairs={{0,1},{1,0},{2,3},{3,2},{4,5},{5,4},{6,7},{7,6},{8,9},{9,8},{10,11... | collective-permute-start | bytes 331784 | tf_op jit(solution)/shard_map/ppermute | solution.py:515
  23.9 4.7 %copy-start = (bf16[432,128]{1,0:T(8,128)(2,1)S(1)}, bf16[432,128]{1,0:T(8,128)(2,1)}, u32[]{:S(2)}) copy-start(bf16[432,128]{1,0:T(8,128)(2,1)} %get-tuple-element.13.after_ref.su_ref) | copy-start | bytes 331780
  28.0 0.7 %copy-start.2 = (s32[48,27]{0,1:T(8,128)S(1)}, s32[48,27]{0,1:T(8,128)}, u32[]{:S(2)}) copy-start(s32[48,27]{0,1:T(8,128)} %param.16) | copy-start | bytes 15556
  29.5 0.6 copy-start.3
  30.1 8.0 %collective-permute-start.1 = (bf16[480,128]{1,0:T(8,128)(2,1)S(1)}, bf16[480,128]{1,0:T(8,128)(2,1)S(1)}, u32[]{:S(2)}, u32[]{:S(2)}) collective-permute-start(bf16[480,128]{1,0:T(8,128)(2,1)S(1)} %pad_maximum_fusion.1), channel_id=1, source_target_pairs={{0,3},{1,2},{2,1},{3,0},{4,7},{5,6},{6,5},{7,4},{8,11},{9,10},{10,... | collective-permute-start | bytes 368648 | tf_op jit(solution)/shard_map/ppermute | solution.py:517
  32.0 0.7 %copy-start.6 = (bf16[480,128]{1,0:T(8,128)(2,1)}, bf16[480,128]{1,0:T(8,128)(2,1)S(1)}, u32[]{:S(2)}) copy-start(bf16[480,128]{1,0:T(8,128)(2,1)S(1)} %collective-permute-done.4.prev_ref) | copy-start | bytes 368644
  32.0 0.7 %copy-start.7 = (bf16[480,128]{1,0:T(8,128)(2,1)}, bf16[480,128]{1,0:T(8,128)(2,1)S(1)}, u32[]{:S(2)}) copy-start(bf16[480,128]{1,0:T(8,128)(2,1)S(1)} %collective-permute-done.5.next_ref) | copy-start | bytes 368644
  38.1 0.6 %copy-start.1 = (bf16[480,128]{1,0:T(8,128)(2,1)}, bf16[480,128]{1,0:T(8,128)(2,1)S(1)}, u32[]{:S(2)}) copy-start(bf16[480,128]{1,0:T(8,128)(2,1)S(1)} %collective-permute-done.1.after_ref.rd2_ref) | copy-start | bytes 368644
  38.7 16.2 %collective-permute-start.2 = (bf16[576,128]{1,0:T(8,128)(2,1)S(1)}, bf16[576,128]{1,0:T(8,128)(2,1)S(1)}, u32[]{:S(2)}, u32[]{:S(2)}) collective-permute-start(bf16[576,128]{1,0:T(8,128)(2,1)S(1)} %pad_maximum_fusion), channel_id=1, source_target_pairs={{0,4},{4,8},{8,12},{12,16},{16,20},{20,24},{24,28},{28,32},{32,36}... | collective-permute-start | bytes 442376 | tf_op jit(solution)/shard_map/ppermute | solution.py:522
  40.6 14.3 %collective-permute-start.3 = (bf16[576,128]{1,0:T(8,128)(2,1)S(1)}, bf16[576,128]{1,0:T(8,128)(2,1)S(1)}, u32[]{:S(2)}, u32[]{:S(2)}) collective-permute-start(bf16[576,128]{1,0:T(8,128)(2,1)S(1)} %pad_maximum_fusion), channel_id=1, source_target_pairs={{4,0},{8,4},{12,8},{16,12},{20,16},{24,20},{28,24},{32,28},{36,32}... | collective-permute-start | bytes 442376 | tf_op jit(solution)/shard_map/ppermute | solution.py:523
  54.9 0.7 %copy-start.4 = (bf16[576,128]{1,0:T(8,128)(2,1)}, bf16[576,128]{1,0:T(8,128)(2,1)S(1)}, u32[]{:S(2)}) copy-start(bf16[576,128]{1,0:T(8,128)(2,1)S(1)} %collective-permute-done.2.bp_ref) | copy-start | bytes 442372
  55.0 0.7 %copy-start.5 = (bf16[576,128]{1,0:T(8,128)(2,1)}, bf16[576,128]{1,0:T(8,128)(2,1)S(1)}, u32[]{:S(2)}) copy-start(bf16[576,128]{1,0:T(8,128)(2,1)S(1)} %collective-permute-done.3.bm_ref) | copy-start | bytes 442372

commit v3 on v2

--- a/solution.py
+++ b/solution.py
@@ -20,7 +20,12 @@
 PARENTS = 6
 S_ROWS = PAIRS * 16
 U_ROWS = PARENTS // 2 * 16
-VMEM_LIMIT = 60 * 1024 * 1024
+Q_ROW = S_ROWS
+XY_ROW = 2 * S_ROWS
+Z_ROW = XY_ROW + BOXES
+UP_ROW = Z_ROW + BOXES
+ALL_ROWS = UP_ROW + U_ROWS
+VMEM_LIMIT = 24 * 1024 * 1024
 
 
 def nn(a, b):
@@ -43,11 +48,30 @@
     return pltpu.roll(x, 64, 1)
 
 
-def skeleton_kernel(q_ref, v_ref, e_ref, su_ref, xv_ref, xe_ref, qs, vs, es):
+def skeleton_kernel(
+    q_hbm, x_hbm, v_hbm, e_hbm, su_ref, up_ref, xv_ref, xe_ref, q_ref, x_ref, v_ref, e_ref, qs, vs, es, sems
+):
+    loads = [
+        pltpu.make_async_copy(q_hbm, q_ref, sems.at[0]),
+        pltpu.make_async_copy(v_hbm, v_ref, sems.at[1]),
+        pltpu.make_async_copy(x_hbm, x_ref, sems.at[2]),
+        pltpu.make_async_copy(e_hbm, e_ref, sems.at[3]),
+    ]
+    for load in loads:
+        load.start()
+    loads[0].wait()
     for i in range(8):
         qs[i * BOXES : (i + 1) * BOXES] = q_ref[:, i * 128 : (i + 1) * 128].astype(F32)
+    pack_charges(qs, su_ref)
+    loads[2].wait()
+    su_ref[XY_ROW : XY_ROW + BOXES] = x_ref[:, :128].astype(BF16)
+    su_ref[Z_ROW : Z_ROW + BOXES] = jnp.concatenate(
+        [x_ref[:, 128:], jnp.zeros((BOXES, 64), F32)], axis=1
+    ).astype(BF16)
+    loads[1].wait()
     for t in range(32):
         vs[t * BOXES : (t + 1) * BOXES] = v_ref[:, t * 128 : (t + 1) * 128].astype(F32)
+    loads[3].wait()
     for t in range(32):
         es[t * BOXES : (t + 1) * BOXES] = e_ref[:, t * 128 : (t + 1) * 128].astype(F32)
     row = iota((32, 128), 0)
@@ -104,13 +128,12 @@
             lifted = z[:16] + half_swap(z[16:])
         else:
             other = half_swap(z[:16]) + z[16:]
-            r = S_ROWS + (p // 2) * 16
+            r = UP_ROW + (p // 2) * 16
             su_ref[r : r + 16] = jnp.where(low, lifted, other).astype(BF16)
-
-
-def pack_kernel(q_ref, x_ref, out_ref, qs):
-    for i in range(8):
-        qs[i * BOXES : (i + 1) * BOXES] = q_ref[:, i * 128 : (i + 1) * 128].astype(F32)
+    up_ref[...] = su_ref[UP_ROW:]
+
+
+def pack_charges(qs, out_ref):
     own = iota((8, 128), 0) == iota((8, 128), 1) // 16
     pick = onehot((iota((16, 128), 1) % 16) == iota((16, 128), 0))
     for u in range(PAIRS):
@@ -120,11 +143,8 @@
             for i in range(8):
                 parts.append(jnp.where(own, jnp.broadcast_to(rows[i : i + 1], (8, 128)), 0.0))
         weights = jnp.concatenate(parts, axis=0).astype(BF16)
-        out_ref[u * 16 : u * 16 + 16] = nt(pick, weights).astype(BF16)
-    out_ref[S_ROWS : S_ROWS + BOXES] = x_ref[:, :128].astype(BF16)
-    out_ref[S_ROWS + BOXES : S_ROWS + 2 * BOXES] = jnp.concatenate(
-        [x_ref[:, 128:], jnp.zeros((BOXES, 64), F32)], axis=1
-    ).astype(BF16)
+        r = Q_ROW + u * 16
+        out_ref[r : r + 16] = nt(pick, weights).astype(BF16)
 
 
 def table_kernel(leaf_ref, upper_ref, after_ref, wl_ref, wu_ref, ts):
@@ -153,8 +173,8 @@
     return onehot((r // 64 == c // 128) & (r % 64 == c % 64))
 
 
-def spread_pairs(src_ref, rows, dst_ref, base):
-    wide = nn(src_ref[:rows], dup_matrix()).astype(BF16)
+def spread_pairs(src_ref, row, rows, dst_ref, base):
+    wide = nn(src_ref[row : row + rows], dup_matrix()).astype(BF16)
     for u in range(rows // 16):
         dst_ref[base + 2 * u] = wide[u * 16 : u * 16 + 16, :128]
         dst_ref[base + 2 * u + 1] = wide[u * 16 : u * 16 + 16, 128:]
@@ -164,9 +184,15 @@
 TOTAL = 3 * BOXES
 
 
-def near_tables_kernel(own_ref, prev_ref, next_ref, x_ref, after_ref, qt, yt, at, bs):
-    for side, ref in enumerate((prev_ref, own_ref, next_ref)):
-        spread_pairs(ref, S_ROWS, qt, side * BOXES)
+def leaf_sides(own_ref, ev_ref, od_ref):
+    odd = lax.axis_index("sub") % 2
+    return ((1, own_ref), (2 - 2 * odd, ev_ref), (2 * odd, od_ref))
+
+
+def near_tables_kernel(own_ref, ev_ref, od_ref, x_ref, after_ref, qt, yt, at, bs):
+    sides = leaf_sides(own_ref, ev_ref, od_ref)
+    for side, ref in sides:
+        spread_pairs(ref, Q_ROW, S_ROWS, qt, side * BOXES)
     qt[TOTAL] = jnp.zeros((16, 128), BF16)
     lanes = iota((BOXES, 128), 1) < 64
 
@@ -176,15 +202,15 @@
 
     ones = jnp.ones((BOXES, 128), F32)
     zeros = jnp.zeros((BOXES, 128), F32)
-    for side, ref in enumerate((prev_ref, own_ref, next_ref)):
-        xy = ref[S_ROWS : S_ROWS + BOXES].astype(F32)
-        z = ref[S_ROWS + BOXES : S_ROWS + 2 * BOXES].astype(F32)
+    for j, (side, ref) in enumerate(sides):
+        xy = ref[XY_ROW : XY_ROW + BOXES].astype(F32)
+        z = ref[Z_ROW : Z_ROW + BOXES].astype(F32)
         y0, y1, y2 = dup3(xy, z)
         n = split3(SCALE * (y0 * y0 + y1 * y1 + y2 * y2))
         for k, v in enumerate((y0, y0, y0, y1, y1, y1, y2, y2, y2, *n, ones, ones, ones, zeros)):
-            bs[side, k * BOXES : (k + 1) * BOXES] = v
+            bs[j, k * BOXES : (k + 1) * BOXES] = v
         for b in range(BOXES):
-            yt[side * BOXES + b] = bs[side, pl.ds(b, 16, stride=BOXES), :].astype(BF16)
+            yt[side * BOXES + b] = bs[j, pl.ds(b, 16, stride=BOXES), :].astype(BF16)
     yt[TOTAL] = onehot(iota((16, 128), 0) >= 12)
     zx = jnp.concatenate([x_ref[:, 128:], jnp.zeros((BOXES, 64), F32)], axis=1)
     x0, x1, x2 = dup3(x_ref[:, :128], zx)
@@ -200,18 +226,13 @@
     at[BOXES] = jnp.zeros((64, 16), BF16) + onehot(iota((64, 16), 1) == 12)
 
 
-def near_kernel(info, ids_ref, count_ref, qt, yt, at, after_ref, out_ref, slot_v, slot_s, ks, qs, acc, place, sums, sem):
-    first = info[0]
-    r48 = iota((BOXES, BOXES), 0)
-    counts = jnp.sum(
-        jnp.where(r48 == iota((BOXES, BOXES), 1), jnp.broadcast_to(count_ref[...], (BOXES, BOXES)), 0),
-        axis=1,
-        keepdims=True,
-    )
-    slot_v[...] = jnp.full((BOXES + 8, 128), TOTAL, jnp.int32)
-    slot_v[:BOXES, :NEAR] = jnp.where(iota((BOXES, NEAR), 1) < counts, ids_ref[...] - first, TOTAL)
-    slot_v[:BOXES, 32:33] = counts
-    slot_v[BOXES : BOXES + 8, 32:33] = jnp.zeros((8, 1), jnp.int32)
+def near_kernel(ids_ref, count_ref, qt, yt, at, after_ref, out_ref, slot_v, slot_s, ks, qs, acc, place, sums, sem):
+    first = (lax.axis_index(("box", "sub")) - 1) * BOXES
+    counts = count_ref[...]
+    slot_v[...] = jnp.full((40, 128), TOTAL, jnp.int32)
+    slot_v[:NEAR, :BOXES] = jnp.where(iota((NEAR, BOXES), 0) < counts, ids_ref[...] - first, TOTAL)
+    slot_v[32:33] = jnp.zeros((1, 128), jnp.int32)
+    slot_v[32:33, :BOXES] = counts
     copy = pltpu.make_async_copy(slot_v, slot_s, sem)
     copy.start()
     for b in range(BOXES + 1):
@@ -236,13 +257,13 @@
             place[slot * STEP + j] = box
             ys = []
             for c in range(4):
-                one = slot_s[box, chunk + 2 * c]
-                two = slot_s[box, chunk + 2 * c + 1]
+                one = slot_s[chunk + 2 * c, box]
+                two = slot_s[chunk + 2 * c + 1, box]
                 ys.append(jnp.where(low, yt[one], yt[two]))
                 qs[slot, j, :, c * 128 : (c + 1) * 128] = jnp.where(low, qt[one], qt[two])
             d = nn(at[box], jnp.concatenate(ys, axis=1))
             ks[slot, j] = lax.rsqrt(d).astype(BF16)
-            more = chunk + 8 < slot_s[box, 32]
+            more = chunk + 8 < slot_s[32, box]
             box = jnp.where(more, box, jnp.minimum(box + 1, BOXES))
             chunk = jnp.where(more, chunk + 8, 0)
         return step + 1, box, chunk
@@ -276,12 +297,12 @@
 
 
 def field_kernel(
-    info, leaf_ref, pid_ref, su_ref, rd1_ref, rd2_ref, bp_ref, bm_ref, wl_ref, wu_ref, xv_ref, xe_ref, near_ref,
-    out_ref, st, ut, halo, fs, ps, ids_v, ids, pids_v, pids, sems,
+    leaf_ref, pid_ref, su_ref, ev_ref, od_ref, x3_ref, be_ref, bo_ref, wl_ref, wu_ref, xv_ref, xe_ref, near_ref,
+    out_ref, st, ut, fs, ps, ids_v, ids, pids_v, pids, sems,
 ):
-    first = info[0]
-    first_parent = info[1]
-    sub = info[2]
+    first = (lax.axis_index(("box", "sub")) - 1) * BOXES
+    first_parent = (lax.axis_index("box") - 1) * 4 * PARENTS
+    sub = lax.axis_index("sub")
     ids_v[:, :OFFSETS] = leaf_ref[...] - first
     pids_v[:PARENTS, :UPPER] = pid_ref[...] - first_parent
     copies = [pltpu.make_async_copy(ids_v, ids, sems.at[0]), pltpu.make_async_copy(pids_v, pids, sems.at[1])]
@@ -289,45 +310,20 @@
         copy.start()
     low = iota((16, 128), 1) < 64
 
-    @pl.when(sub == 0)
-    def _():
-        halo[0] = bp_ref[:S_ROWS]
-        halo[1] = rd1_ref[:S_ROWS]
-
-    @pl.when(sub == 1)
-    def _():
-        halo[0] = rd1_ref[:S_ROWS]
-        halo[1] = rd2_ref[:S_ROWS]
-
-    @pl.when(sub == 2)
-    def _():
-        halo[0] = rd2_ref[:S_ROWS]
-        halo[1] = rd1_ref[:S_ROWS]
-
-    @pl.when(sub == 3)
-    def _():
-        halo[0] = rd1_ref[:S_ROWS]
-        halo[1] = bm_ref[:S_ROWS]
-
-    spread_pairs(halo.at[0], S_ROWS, st, 0)
-    spread_pairs(su_ref, S_ROWS, st, BOXES)
-    spread_pairs(halo.at[1], S_ROWS, st, 2 * BOXES)
+    for side, ref in leaf_sides(su_ref, ev_ref, od_ref):
+        spread_pairs(ref, 0, S_ROWS, st, side * BOXES)
+    odd = lax.axis_index("box") % 2
 
     def parents(ref, row, group, flip):
-        wide = nn(ref[row : row + U_ROWS], dup_matrix()).astype(BF16)
-        at = group * 4 * PARENTS + (sub ^ flip) * PARENTS
-        for u in range(PARENTS // 2):
-            ut[at + 2 * u] = wide[u * 16 : u * 16 + 16, :128]
-            ut[at + 2 * u + 1] = wide[u * 16 : u * 16 + 16, 128:]
-
-    for group, ref in ((0, bp_ref), (2, bm_ref)):
-        for j, flip in enumerate((3, 2, 0, 1)):
-            parents(ref, S_ROWS + j * U_ROWS, group, flip)
-    parents(su_ref, S_ROWS, 1, 0)
-    parents(rd1_ref, S_ROWS, 1, 1)
-    parents(rd2_ref, S_ROWS, 1, 3)
-    parents(rd2_ref, S_ROWS + U_ROWS, 1, 2)
-
+        spread_pairs(ref, row, U_ROWS, ut, (group * 4 + (sub ^ flip)) * PARENTS)
+
+    for group, ref in ((2 - 2 * odd, be_ref), (2 * odd, bo_ref)):
+        for j, flip in enumerate((0, 1, 3, 2)):
+            parents(ref, j * U_ROWS, group, flip)
+    parents(su_ref, UP_ROW, 1, 0)
+    parents(ev_ref, UP_ROW, 1, 1)
+    parents(x3_ref, 0, 1, 3)
+    parents(x3_ref, U_ROWS, 1, 2)
     for copy in copies:
         copy.wait()
     upper = couple(ut, wu_ref, pids, PARENTS, UPPER, low)
@@ -379,8 +375,8 @@
 PEAK = 1.0e15
 
 
-def params():
-    return pltpu.CompilerParams(vmem_limit_bytes=VMEM_LIMIT)
+def params(limit=VMEM_LIMIT):
+    return pltpu.CompilerParams(vmem_limit_bytes=limit)
 
 
 def cost(us):
@@ -391,34 +387,26 @@
     return jax.ShapeDtypeStruct(dims, dtype)
 
 
-def run_skeleton(charges, basis, transfer):
+def run_skeleton(charges, coords, basis, transfer):
     return pl.pallas_call(
         skeleton_kernel,
-        out_shape=(shape(S_ROWS + U_ROWS, 128), shape(BOXES * 32, 128), shape(BOXES * 32, 128)),
-        in_specs=[VM] * 3,
-        out_specs=(VM,) * 3,
+        out_shape=(shape(ALL_ROWS, 128), shape(U_ROWS, 128), shape(BOXES * 32, 128), shape(BOXES * 32, 128)),
+        in_specs=[pl.BlockSpec(memory_space=pltpu.HBM)] * 4,
+        out_specs=(VM,) * 4,
         scratch_shapes=[
+            pltpu.VMEM((BOXES, 1024), BF16),
+            pltpu.VMEM((BOXES, 192), F32),
+            pltpu.VMEM((BOXES, 4096), BF16),
+            pltpu.VMEM((BOXES, 4096), BF16),
             pltpu.VMEM((8 * BOXES, 128), F32),
             pltpu.VMEM((32 * BOXES, 128), F32),
             pltpu.VMEM((32 * BOXES, 128), F32),
+            pltpu.SemaphoreType.DMA((4,)),
         ],
-        compiler_params=params(),
+        compiler_params=params(60 << 20),
         cost_estimate=cost(4.0),
         name="skeleton",
-    )(charges, basis, transfer)
-
-
-def run_pack(charges, coords):
-    return pl.pallas_call(
-        pack_kernel,
-        out_shape=shape(S_ROWS + 2 * BOXES, 128),
-        in_specs=[VM] * 2,
-        out_specs=VM,
-        scratch_shapes=[pltpu.VMEM((8 * BOXES, 128), F32)],
-        compiler_params=params(),
-        cost_estimate=cost(2.0),
-        name="pack",
-    )(charges, coords)
+    )(charges, coords, basis, transfer)
 
 
 def run_tables(leaf_table, upper_table, su):
@@ -429,12 +417,12 @@
         out_specs=(VM,) * 2,
         scratch_shapes=[pltpu.VMEM((32 * OFFSETS, 128), F32)],
         compiler_params=params(),
-        cost_estimate=cost(4.0),
+        cost_estimate=cost(2.0),
         name="tables",
     )(leaf_table, upper_table, su)
 
 
-def run_near_tables(own, before, after, coords, wl):
+def run_near_tables(su, ev, od, coords, wl):
     return pl.pallas_call(
         near_tables_kernel,
         out_shape=(shape(TOTAL + 1, 16, 128), shape(TOTAL + 1, 16, 128), shape(BOXES + 1, 64, 16)),
@@ -442,20 +430,20 @@
         out_specs=(VM,) * 3,
         scratch_shapes=[pltpu.VMEM((4, 16 * BOXES, 128), F32)],
         compiler_params=params(),
-        cost_estimate=cost(4.0),
+        cost_estimate=cost(1.0),
         name="near_tables",
-    )(own, before, after, coords, wl)
-
-
-def run_near(info, near_ids, near_count, qt, yt, at, rd2):
+    )(su, ev, od, coords, wl)
+
+
+def run_near(near_ids, near_count, qt, yt, at, x3):
     return pl.pallas_call(
         near_kernel,
         out_shape=shape(8 * BOXES, 128, dtype=F32),
-        in_specs=[SM] + [VM] * 5 + [HB],
+        in_specs=[VM] * 5 + [HB],
         out_specs=VM,
         scratch_shapes=[
-            pltpu.VMEM((BOXES + 8, 128), jnp.int32),
-            pltpu.SMEM((BOXES + 8, 128), jnp.int32),
+            pltpu.VMEM((40, 128), jnp.int32),
+            pltpu.SMEM((40, 128), jnp.int32),
             pltpu.VMEM((2, STEP, 64, 512), BF16),
             pltpu.VMEM((2, STEP, 16, 512), BF16),
             pltpu.VMEM((BOXES + 1, 16, 64), F32),
@@ -466,19 +454,18 @@
         compiler_params=params(),
         cost_estimate=cost(7.0),
         name="near",
-    )(info, near_ids, near_count.reshape(1, BOXES), qt, yt, at, rd2)
-
-
-def run_field(info, leaf_ids, parent_ids, su, rd1, rd2, bp, bm, wl, wu, xv, xe, near):
+    )(near_ids.T, near_count.reshape(1, BOXES), qt, yt, at, x3)
+
+
+def run_field(leaf_ids, parent_ids, su, ev, od, x3, be, bo, wl, wu, xv, xe, near):
     return pl.pallas_call(
         field_kernel,
         out_shape=shape(BOXES, 1024, dtype=F32),
-        in_specs=[SM] + [VM] * 12,
+        in_specs=[VM] * 13,
         out_specs=VM,
         scratch_shapes=[
             pltpu.VMEM((3 * BOXES, 16, 128), BF16),
             pltpu.VMEM((12 * PARENTS, 16, 128), BF16),
-            pltpu.VMEM((2, S_ROWS, 128), BF16),
             pltpu.VMEM((BOXES * 16, 128), F32),
             pltpu.VMEM((8 * BOXES, 128), F32),
             pltpu.VMEM((BOXES, 128), jnp.int32),
@@ -490,7 +477,7 @@
         compiler_params=params(),
         cost_estimate=cost(9.0),
         name="field",
-    )(info, leaf_ids, parent_ids, su, rd1, rd2, bp, bm, wl, wu, xv, xe, near)
+    )(leaf_ids, parent_ids, su, ev, od, x3, be, bo, wl, wu, xv, xe, near)
 
 
 def local(
@@ -500,29 +487,18 @@
     boxes = lax.axis_size("box")
     subs = lax.axis_size("sub")
     chain = boxes * subs
-    sub = lax.axis_index("sub")
-    info = jnp.stack(
-        [
-            (lax.axis_index(flat) - 1) * BOXES,
-            (lax.axis_index("box") - 1) * PARENTS * subs,
-            sub,
-        ]
-    ).astype(jnp.int32)
-    own = run_pack(charges, coords)
-    before = lax.ppermute(own, flat, [(i, i + 1) for i in range(chain - 1)])
-    after = lax.ppermute(own, flat, [(i + 1, i) for i in range(chain - 1)])
-    su, xv, xe = run_skeleton(charges, basis, transfer)
-    rd1 = lax.ppermute(su, "sub", [(i, i ^ 1) for i in range(subs)])
+    su, up, xv, xe = run_skeleton(charges, coords, basis, transfer)
+    ev = lax.ppermute(su, "sub", [(i, i ^ 1) for i in range(subs)])
+    od = lax.ppermute(su, flat, [(i, ((i + 1) ^ 1) - 1) for i in range(1, chain - 1)])
     wl, wu = run_tables(leaf_table, upper_table, su)
-    rd2 = lax.ppermute(
-        jnp.concatenate([su, rd1[S_ROWS:]], axis=0), "sub", [(i, i ^ 3) for i in range(subs)]
-    )
-    qt, yt, at = run_near_tables(own, before, after, coords, wl)
-    edge = jnp.concatenate([rd2, su[S_ROWS:], rd1[S_ROWS:]], axis=0)
-    bp = lax.ppermute(edge, "box", [(i, i + 1) for i in range(boxes - 1)])
-    bm = lax.ppermute(edge, "box", [(i + 1, i) for i in range(boxes - 1)])
-    near = run_near(info, near_ids, near_count, qt, yt, at, rd2)
-    return run_field(info, leaf_ids, parent_ids, su, rd1, rd2, bp, bm, wl, wu, xv, xe, near)
+    pair = jnp.concatenate([up, ev[UP_ROW:]], axis=0)
+    x3 = lax.ppermute(pair, "sub", [(i, i ^ 3) for i in range(subs)])
+    qt, yt, at = run_near_tables(su, ev, od, coords, wl)
+    branch = jnp.concatenate([pair, x3], axis=0)
+    be = lax.ppermute(branch, "box", [(i, i ^ 1) for i in range(boxes)])
+    bo = lax.ppermute(branch, "box", [(i, ((i + 1) ^ 1) - 1) for i in range(1, boxes - 1)])
+    near = run_near(near_ids, near_count, qt, yt, at, x3)
+    return run_field(leaf_ids, parent_ids, su, ev, od, x3, be, bo, wl, wu, xv, xe, near)
 
 
 def solution(mesh):

time: 65.6 us -> 52.4 us (0.80)
  Pallas kernels: 31.3 us -> 22.3 us
  starting transfers between devices: 26.6 us -> 22.5 us
  waiting for transfers between devices: 2.37 us -> 4.09 us
  local copies, waits for them, and re-layouts: 3.44 us -> 2.27 us
    ppermute x6 -> x5, starting transfers between devices: 26.6 us -> 22.5 us  [the longest x1 12.3 us: local(): lax.ppermute(su, flat, [(i, (i + 1 ^ 1) - 1) for i in range(1, chain - 1)])]
    pallas_call x1, Pallas kernels: 2.98 us -> 0.87 us  [run_near_tables(): pl.pallas_call(near_tables_kernel, out_shape=(shape(TOTAL + 1, 16, 128),...]
    pallas_call x1, Pallas kernels: 4.14 us -> 2.04 us  [run_tables(): pl.pallas_call(table_kernel, out_shape=(shape(64, OFFSETS * 64), shape(64...]
    pallas_call x1, Pallas kernels: 8.53 us -> 6.72 us  [run_near(): pl.pallas_call(near_kernel, out_shape=shape(8 * BOXES, 128, dtype=F32), i...]
    ppermute x6 -> x5, waiting for transfers between devices: 2.37 us -> 4.09 us  [the longest x1 4.08 us: local(): x3 = lax.ppermute(pair, 'sub', [(i, i ^ 3) for i in range(subs)])]
    pallas_call x1, Pallas kernels: 8.81 us -> 7.33 us  [run_field(): pl.pallas_call(field_kernel, out_shape=shape(BOXES, 1024, dtype=F32), in_...]
    pallas_call x2 -> x1, Pallas kernels: 6.83 us -> 5.39 us  [run_skeleton(): pl.pallas_call(skeleton_kernel, out_shape=(shape(ALL_ROWS, 128), shape(U_...]
    unnamed x17 -> x24, local copies, waits for them, and re-layouts: 3.43 us -> 2.27 us
  transfers between devices with their start and end apart: 6 -> 5, of which waited for: 1 -> 1; matrix products, arithmetic and copies ran while one was open for 2% -> 0% of each run, Pallas kernels for 32% -> 19%
where the time goes in v3:
time: 52.4 us; the launch traced here: 51.5 us
  starting transfers between devices  22.5 us (43%)
  Pallas kernels  22.3 us (43%)
  waiting for transfers between devices  4.09 us (8%)
  local copies, waits for them, and re-layouts  2.27 us (4%)
    ppermute x1, starting transfers between devices, local(): lax.ppermute(su, flat, [(i, (i + 1 ^ 1) - 1) for i in range(1, chain - 1)])  12.3 us
    pallas_call x1, Pallas kernels, run_field(): pl.pallas_call(field_kernel, out_shape=shape(BOXES, 1024, dtype=F32), in_...  7.33 us
    pallas_call x1, Pallas kernels, run_near(): pl.pallas_call(near_kernel, out_shape=shape(8 * BOXES, 128, dtype=F32), i...  6.72 us
    pallas_call x1, Pallas kernels, run_skeleton(): pl.pallas_call(skeleton_kernel, out_shape=(shape(ALL_ROWS, 128), shape(U_...  5.39 us
    ppermute x1, waiting for transfers between devices, local(): x3 = lax.ppermute(pair, 'sub', [(i, i ^ 3) for i in range(subs)])  4.08 us
    ppermute x1, starting transfers between devices, local(): ev = lax.ppermute(su, 'sub', [(i, i ^ 1) for i in range(subs)])  3.4 us
    ppermute x1, starting transfers between devices, local(): lax.ppermute(branch, 'box', [(i, (i + 1 ^ 1) - 1) for i in range(1, boxes...  3.02 us
    unnamed x24, local copies, waits for them, and re-layouts  2.27 us
  transfers between devices with their start and end apart: 5, of which 1 were waited for; matrix products, arithmetic and copies ran while one was open for 0% of the time, Pallas kernels for 19%

profile of v3, /device:TPU:24, one launch (start us, length us, event | category | flops | bytes accessed | tf_op | source)
XLA Modules:
  0.0 51.5 jit_solution(7169944315510721709)
XLA Ops:
  0.0 0.0 copy-start
  0.0 0.0 copy-start.1
  0.0 5.4 %skeleton.1 = (bf16[912,128]{1,0:T(8,128)(2,1)}, bf16[48,128]{1,0:T(8,128)(2,1)}, bf16[1536,128]{1,0:T(8,128)(2,1)}, bf16[1536,128]{1,0:T(8,128)(2,1)}) custom-call(bf16[48,1024]{1,0:T(8,128)(2,1)} %q_hbm.1, f32[48,192]{1,0:T(8,128)} %x_ref.1, bf16[48,4096]{1,0:T(8,128)(2,1)} %v_hbm.1, bf16[48,4096]{1,0:T(8,128)(2,1)} %e_hbm.1), custom_call_target="tpu_custom_call" | custom-call | flops 4000000000 | bytes 1048576 | tf_op jit(solution)/shard_map/skeleton/pallas_call | solution.py:391
  5.4 3.4 %collective-permute-start = (bf16[912,128]{1,0:T(8,128)(2,1)}, bf16[912,128]{1,0:T(8,128)(2,1)S(1)}, u32[]{:S(2)}, u32[]{:S(2)}) collective-permute-start(bf16[912,128]{1,0:T(8,128)(2,1)} %get-tuple-element.14.after_ref.own_ref.su_ref), channel_id=1, source_target_pairs={{0,1},{1,0},{2,3},{3,2},{4,5},{5,4},{6,7},{7,6},{8,9},{9,8},{10,11... | collective-permute-start | bytes 700424 | tf_op jit(solution)/shard_map/ppermute | solution.py:491
  8.8 12.3 %collective-permute-start.1 = (bf16[912,128]{1,0:T(8,128)(2,1)}, bf16[912,128]{1,0:T(8,128)(2,1)S(1)}, u32[]{:S(2)}, u32[]{:S(2)}) collective-permute-start(bf16[912,128]{1,0:T(8,128)(2,1)} %get-tuple-element.14.after_ref.own_ref.su_ref), channel_id=1, source_target_pairs={{1,2},{2,1},{3,4},{4,3},{5,6},{6,5},{7,8},{8,7},{9,10},{10,9},{11,... | collective-permute-start | bytes 700424 | tf_op jit(solution)/shard_map/ppermute | solution.py:492
  21.1 0.0 copy-done
  21.1 0.0 copy-done.1
  21.1 0.0 copy-start.2
  21.1 1.0 %copy-done.2 = bf16[912,128]{1,0:T(8,128)(2,1)S(1)} copy-done((bf16[912,128]{1,0:T(8,128)(2,1)S(1)}, bf16[912,128]{1,0:T(8,128)(2,1)}, u32[]{:S(2)}) %copy-start.2) | copy-done | bytes 233496
  22.1 0.0 copy-start.11
  22.1 0.0 copy-start.3
  22.1 2.0 %tables.1 = (bf16[64,6144]{1,0:T(8,128)(2,1)S(1)}, bf16[64,4096]{1,0:T(8,128)(2,1)S(1)}) custom-call(bf16[96,4096]{1,0:T(8,128)(2,1)S(1)} %copy-done, bf16[64,4096]{1,0:T(8,128)(2,1)S(1)} %copy-done.1, bf16[912,128]{1,0:T(8,128)(2,1)S(1)} %copy-done.2), custom_call_target="tpu_custom_call" | custom-call | flops 2000000000 | bytes 1048576 | tf_op jit(solution)/shard_map/tables/pallas_call | solution.py:413
  24.1 0.0 copy-start.4
  24.1 0.0 collective-permute-done.ev_ref
  24.1 0.0 copy-done.11
  24.2 1.9 %collective-permute-start.2 = (bf16[96,128]{1,0:T(8,128)(2,1)S(1)}, bf16[96,128]{1,0:T(8,128)(2,1)S(1)}, u32[]{:S(2)}, u32[]{:S(2)}) collective-permute-start(bf16[96,128]{1,0:T(8,128)(2,1)S(1)} %pad_maximum_fusion.1), channel_id=1, source_target_pairs={{0,3},{1,2},{2,1},{3,0},{4,7},{5,6},{6,5},{7,4},{8,11},{9,10},{10,... | collective-permute-start | bytes 73736 | tf_op jit(solution)/shard_map/ppermute | solution.py:495
  26.1 0.0 collective-permute-done.1.od_ref
  26.1 0.0 copy-done.3
  26.1 0.0 copy-done.4
  26.1 0.9 %near_tables.1 = (bf16[145,16,128]{2,1,0:T(8,128)(2,1)S(1)}, bf16[145,16,128]{2,1,0:T(8,128)(2,1)S(1)}, bf16[49,64,16]{2,1,0:T(8,128)(2,1)S(1)}) custom-call(bf16[912,128]{1,0:T(8,128)(2,1)S(1)} %copy-done.3, bf16[912,128]{1,0:T(8,128)(2,1)S(1)} %collective-permute-done.ev_ref, bf16[912,128]{1,0:T(8,128)(2,1)S(1)} %collective-permute-done.1.od_ref, ...), custom_call_target="tpu_custom_call" | custom-call | flops 1000000000 | bytes 1048576 | tf_op jit(solution)/shard_map/near_tables/pallas_call | solution.py:426
  27.0 0.0 copy-start.6
  27.0 4.1 %collective-permute-done.2.after_ref.x3_ref = bf16[96,128]{1,0:T(8,128)(2,1)S(1)} collective-permute-done((bf16[96,128]{1,0:T(8,128)(2,1)S(1)}, bf16[96,128]{1,0:T(8,128)(2,1)S(1)}, u32[]{:S(2)}, u32[]{:S(2)}) %collective-permute-start.2) | collective-permute-done | bytes 24608 | tf_op jit(solution)/shard_map/ppermute | solution.py:495
  31.1 1.9 %collective-permute-start.3 = (bf16[192,128]{1,0:T(8,128)(2,1)S(1)}, bf16[192,128]{1,0:T(8,128)(2,1)S(1)}, u32[]{:S(2)}, u32[]{:S(2)}) collective-permute-start(bf16[192,128]{1,0:T(8,128)(2,1)S(1)} %pad_maximum_fusion), channel_id=1, source_target_pairs={{0,4},{4,0},{8,12},{12,8},{16,20},{20,16},{24,28},{28,24},{32,36},... | collective-permute-start | bytes 147464 | tf_op jit(solution)/shard_map/ppermute | solution.py:498
  33.0 3.0 %collective-permute-start.4 = (bf16[192,128]{1,0:T(8,128)(2,1)S(1)}, bf16[192,128]{1,0:T(8,128)(2,1)S(1)}, u32[]{:S(2)}, u32[]{:S(2)}) collective-permute-start(bf16[192,128]{1,0:T(8,128)(2,1)S(1)} %pad_maximum_fusion), channel_id=1, source_target_pairs={{4,8},{8,4},{12,16},{16,12},{20,24},{24,20},{28,32},{32,28},{36,40... | collective-permute-start | bytes 147464 | tf_op jit(solution)/shard_map/ppermute | solution.py:499
  36.1 0.0 copy-start.8
  36.1 0.0 copy-done.6
  36.1 0.6 %copy-done.8 = s32[48]{0:T(128)S(1)} copy-done((s32[48]{0:T(128)S(1)}, s32[48]{0:T(128)}, u32[]{:S(2)}) %copy-start.8) | copy-done | bytes 216
  36.7 0.0 copy-start.5
  36.7 0.0 copy-start.9
  36.7 0.0 copy-start.10
  36.7 6.7 %near.1.near_ref = f32[384,128]{1,0:T(8,128)S(1)} custom-call(s32[27,48]{1,0:T(8,128)S(1)} %bitcast.2, s32[1,48]{1,0:T(1,128)S(1)} %bitcast.3, bf16[145,16,128]{2,1,0:T(8,128)(2,1)S(1)} %get-tuple-element.20.qt, bf16[145,16,128]{2,1,0:T(8,128)(2,1)S(1)} %get-tuple-element.21.yt, bf16[49,64,16]{2,1,0:T(8,128)(2,1)S(1)} %get-tuple-element.22.at, ...), custom_call_target="tpu_custom_call" | custom-call | flops 7000000000 | bytes 1048576 | tf_op jit(solution)/shard_map/near/pallas_call | solution.py:439
  43.4 0.0 copy-start.7
  43.5 0.0 collective-permute-done.3.be_ref
  43.5 0.0 collective-permute-done.4.bo_ref
  43.5 0.0 copy-done.5
  43.5 0.0 copy-done.9
  43.5 0.0 copy-done.10
  43.5 0.6 %copy-done.7 = s32[6,64]{1,0:T(8,128)S(1)} copy-done((s32[6,64]{1,0:T(8,128)S(1)}, s32[6,64]{1,0:T(8,128)}, u32[]{:S(2)}) %copy-start.7) | copy-done | bytes 1560
  44.1 7.3 %field.1 = f32[48,1024]{1,0:T(8,128)} custom-call(s32[48,96]{1,0:T(8,128)S(1)} %copy-done.5, s32[6,64]{1,0:T(8,128)S(1)} %copy-done.7, bf16[912,128]{1,0:T(8,128)(2,1)S(1)} %copy-done.3, bf16[912,128]{1,0:T(8,128)(2,1)S(1)} %collective-permute-done.ev_ref, bf16[912,128]{1,0:T(8,128)(2,1)S(1)} %collective-permute-done.1.od_ref, ...), custom_call_target="tpu_custom_call" | custom-call | flops 8999999488 | bytes 1048576 | tf_op jit(solution)/shard_map/field/pallas_call | solution.py:461
  (3 shorter events, 0.0 us)
Async XLA Ops:
  0.0 21.1 %copy-start = (bf16[96,4096]{1,0:T(8,128)(2,1)S(1)}, bf16[96,4096]{1,0:T(8,128)(2,1)}, u32[]{:S(2)}) copy-start(bf16[96,4096]{1,0:T(8,128)(2,1)} %leaf_ref.2) | copy-start | bytes 2359300
  0.0 21.1 %copy-start.1 = (bf16[64,4096]{1,0:T(8,128)(2,1)S(1)}, bf16[64,4096]{1,0:T(8,128)(2,1)}, u32[]{:S(2)}) copy-start(bf16[64,4096]{1,0:T(8,128)(2,1)} %upper_ref.1) | copy-start | bytes 1572868
  5.4 18.7 %collective-permute-start = (bf16[912,128]{1,0:T(8,128)(2,1)}, bf16[912,128]{1,0:T(8,128)(2,1)S(1)}, u32[]{:S(2)}, u32[]{:S(2)}) collective-permute-start(bf16[912,128]{1,0:T(8,128)(2,1)} %get-tuple-element.14.after_ref.own_ref.su_ref), channel_id=1, source_target_pairs={{0,1},{1,0},{2,3},{3,2},{4,5},{5,4},{6,7},{7,6},{8,9},{9,8},{10,11... | collective-permute-start | bytes 700424 | tf_op jit(solution)/shard_map/ppermute | solution.py:491
  8.8 17.3 %collective-permute-start.1 = (bf16[912,128]{1,0:T(8,128)(2,1)}, bf16[912,128]{1,0:T(8,128)(2,1)S(1)}, u32[]{:S(2)}, u32[]{:S(2)}) collective-permute-start(bf16[912,128]{1,0:T(8,128)(2,1)} %get-tuple-element.14.after_ref.own_ref.su_ref), channel_id=1, source_target_pairs={{1,2},{2,1},{3,4},{4,3},{5,6},{6,5},{7,8},{8,7},{9,10},{10,9},{11,... | collective-permute-start | bytes 700424 | tf_op jit(solution)/shard_map/ppermute | solution.py:492
  21.1 1.0 %copy-start.2 = (bf16[912,128]{1,0:T(8,128)(2,1)S(1)}, bf16[912,128]{1,0:T(8,128)(2,1)}, u32[]{:S(2)}) copy-start(bf16[912,128]{1,0:T(8,128)(2,1)} %get-tuple-element.14.after_ref.own_ref.su_ref) | copy-start | bytes 700420
  22.1 2.1 %copy-start.11 = (bf16[48,128]{1,0:T(8,128)(2,1)S(1)}, bf16[48,128]{1,0:T(8,128)(2,1)}, u32[]{:S(2)}) copy-start(bf16[48,128]{1,0:T(8,128)(2,1)} %get-tuple-element.15) | copy-start | bytes 36868
  22.1 4.0 %copy-start.3 = (bf16[912,128]{1,0:T(8,128)(2,1)S(1)}, bf16[912,128]{1,0:T(8,128)(2,1)}, u32[]{:S(2)}) copy-start(bf16[912,128]{1,0:T(8,128)(2,1)} %get-tuple-element.14.after_ref.own_ref.su_ref) | copy-start | bytes 700420
  24.1 2.0 %copy-start.4 = (f32[48,192]{1,0:T(8,128)S(1)}, f32[48,192]{1,0:T(8,128)}, u32[]{:S(2)}) copy-start(f32[48,192]{1,0:T(8,128)} %x_ref.1) | copy-start | bytes 110596
  24.2 6.9 %collective-permute-start.2 = (bf16[96,128]{1,0:T(8,128)(2,1)S(1)}, bf16[96,128]{1,0:T(8,128)(2,1)S(1)}, u32[]{:S(2)}, u32[]{:S(2)}) collective-permute-start(bf16[96,128]{1,0:T(8,128)(2,1)S(1)} %pad_maximum_fusion.1), channel_id=1, source_target_pairs={{0,3},{1,2},{2,1},{3,0},{4,7},{5,6},{6,5},{7,4},{8,11},{9,10},{10,... | collective-permute-start | bytes 73736 | tf_op jit(solution)/shard_map/ppermute | solution.py:495
  27.0 9.1 %copy-start.6 = (s32[48,27]{0,1:T(8,128)S(1)}, s32[48,27]{0,1:T(8,128)}, u32[]{:S(2)}) copy-start(s32[48,27]{0,1:T(8,128)} %param.16) | copy-start | bytes 15556
  31.1 12.4 %collective-permute-start.3 = (bf16[192,128]{1,0:T(8,128)(2,1)S(1)}, bf16[192,128]{1,0:T(8,128)(2,1)S(1)}, u32[]{:S(2)}, u32[]{:S(2)}) collective-permute-start(bf16[192,128]{1,0:T(8,128)(2,1)S(1)} %pad_maximum_fusion), channel_id=1, source_target_pairs={{0,4},{4,0},{8,12},{12,8},{16,20},{20,16},{24,28},{28,24},{32,36},... | collective-permute-start | bytes 147464 | tf_op jit(solution)/shard_map/ppermute | solution.py:498
  33.0 10.4 %collective-permute-start.4 = (bf16[192,128]{1,0:T(8,128)(2,1)S(1)}, bf16[192,128]{1,0:T(8,128)(2,1)S(1)}, u32[]{:S(2)}, u32[]{:S(2)}) collective-permute-start(bf16[192,128]{1,0:T(8,128)(2,1)S(1)} %pad_maximum_fusion), channel_id=1, source_target_pairs={{4,8},{8,4},{12,16},{16,12},{20,24},{24,20},{28,32},{32,28},{36,40... | collective-permute-start | bytes 147464 | tf_op jit(solution)/shard_map/ppermute | solution.py:499
  36.1 0.7 %copy-start.8 = (s32[48]{0:T(128)S(1)}, s32[48]{0:T(128)}, u32[]{:S(2)}) copy-start(s32[48]{0:T(128)} %param.17) | copy-start | bytes 580
  36.7 6.8 %copy-start.5 = (s32[48,96]{1,0:T(8,128)S(1)}, s32[48,96]{1,0:T(8,128)}, u32[]{:S(2)}) copy-start(s32[48,96]{1,0:T(8,128)} %leaf_ref.3) | copy-start | bytes 55300
  36.7 6.8 %copy-start.9 = (bf16[1536,128]{1,0:T(8,128)(2,1)S(1)}, bf16[1536,128]{1,0:T(8,128)(2,1)}, u32[]{:S(2)}) copy-start(bf16[1536,128]{1,0:T(8,128)(2,1)} %get-tuple-element.18.xv_ref) | copy-start | bytes 1179652
  36.7 6.8 %copy-start.10 = (bf16[1536,128]{1,0:T(8,128)(2,1)S(1)}, bf16[1536,128]{1,0:T(8,128)(2,1)}, u32[]{:S(2)}) copy-start(bf16[1536,128]{1,0:T(8,128)(2,1)} %get-tuple-element.19.xe_ref) | copy-start | bytes 1179652
  43.4 0.7 %copy-start.7 = (s32[6,64]{1,0:T(8,128)S(1)}, s32[6,64]{1,0:T(8,128)}, u32[]{:S(2)}) copy-start(s32[6,64]{1,0:T(8,128)} %pid_ref.1) | copy-start | bytes 4612

commit v4 on v3

--- a/solution.py
+++ b/solution.py
@@ -13,6 +13,7 @@
 F32 = jnp.float32
 BF16 = jnp.bfloat16
 BOXES = 48
+VP = 52
 PAIRS = BOXES // 2
 NEAR = 27
 OFFSETS = 96
@@ -20,6 +21,7 @@
 PARENTS = 6
 S_ROWS = PAIRS * 16
 U_ROWS = PARENTS // 2 * 16
+TOTAL = 3 * BOXES
 Q_ROW = S_ROWS
 XY_ROW = 2 * S_ROWS
 Z_ROW = XY_ROW + BOXES
@@ -48,32 +50,77 @@
     return pltpu.roll(x, 64, 1)
 
 
-def skeleton_kernel(
-    q_hbm, x_hbm, v_hbm, e_hbm, su_ref, up_ref, xv_ref, xe_ref, q_ref, x_ref, v_ref, e_ref, qs, vs, es, sems
-):
-    loads = [
-        pltpu.make_async_copy(q_hbm, q_ref, sems.at[0]),
-        pltpu.make_async_copy(v_hbm, v_ref, sems.at[1]),
-        pltpu.make_async_copy(x_hbm, x_ref, sems.at[2]),
-        pltpu.make_async_copy(e_hbm, e_ref, sems.at[3]),
-    ]
+IN_SHAPES = (
+    ((BOXES, 1024), BF16),
+    ((BOXES, 192), F32),
+    ((NEAR, BOXES), jnp.int32),
+    ((1, BOXES), jnp.int32),
+    ((BOXES, OFFSETS), jnp.int32),
+    ((PARENTS, UPPER), jnp.int32),
+    ((BOXES, 4096), BF16),
+    ((BOXES, 4096), BF16),
+)
+SLOT_ROWS = 40
+LEAF_ROW = SLOT_ROWS
+PID_ROW = LEAF_ROW + BOXES
+INT_ROWS = PID_ROW + 8
+OUT_SHAPES = (
+    ((INT_ROWS, 128), jnp.int32),
+    ((BOXES * 32, 128), BF16),
+    ((2 * S_ROWS + 2 * BOXES + U_ROWS, 128), BF16),
+    ((U_ROWS, 128), BF16),
+    ((BOXES * 32, 128), BF16),
+)
+
+
+def prepare_kernel(*refs):
+    n, m = len(IN_SHAPES), len(OUT_SHAPES)
+    sources, targets = refs[:n], refs[n : n + m]
+    ins, outs = refs[n + m : 2 * n + m], refs[2 * n + m : 2 * n + 2 * m]
+    qs, vs, es, in_sems, out_sems = refs[2 * n + 2 * m :]
+    loads = [pltpu.make_async_copy(sources[j], ins[j], in_sems.at[j]) for j in range(n)]
+    stores = [pltpu.make_async_copy(outs[j], targets[j], out_sems.at[j]) for j in range(m)]
+    q_ref, x_ref, near_ref, count_ref, leaf_ref, pid_ref, v_ref, e_ref = ins
+    int_ref, xv_ref, su_ref, up_ref, xe_ref = outs
     for load in loads:
         load.start()
     loads[0].wait()
     for i in range(8):
-        qs[i * BOXES : (i + 1) * BOXES] = q_ref[:, i * 128 : (i + 1) * 128].astype(F32)
+        qs[i * VP : i * VP + BOXES] = q_ref[:, i * 128 : (i + 1) * 128].astype(F32)
     pack_charges(qs, su_ref)
-    loads[2].wait()
+    loads[1].wait()
     su_ref[XY_ROW : XY_ROW + BOXES] = x_ref[:, :128].astype(BF16)
     su_ref[Z_ROW : Z_ROW + BOXES] = jnp.concatenate(
         [x_ref[:, 128:], jnp.zeros((BOXES, 64), F32)], axis=1
     ).astype(BF16)
-    loads[1].wait()
+    for j in range(2, 6):
+        loads[j].wait()
+    first = (lax.axis_index(("box", "sub")) - 1) * BOXES
+    counts = count_ref[...]
+    int_ref[...] = jnp.full((INT_ROWS, 128), TOTAL, jnp.int32)
+    int_ref[:NEAR, :BOXES] = jnp.where(iota((NEAR, BOXES), 0) < counts, near_ref[...] - first, TOTAL)
+    int_ref[32:33] = jnp.zeros((1, 128), jnp.int32)
+    int_ref[32:33, :BOXES] = counts
+    int_ref[LEAF_ROW : LEAF_ROW + BOXES, :OFFSETS] = leaf_ref[...] - first
+    int_ref[PID_ROW : PID_ROW + PARENTS, :UPPER] = pid_ref[...] - (lax.axis_index("box") - 1) * 4 * PARENTS
+    stores[0].start()
+    loads[6].wait()
     for t in range(32):
-        vs[t * BOXES : (t + 1) * BOXES] = v_ref[:, t * 128 : (t + 1) * 128].astype(F32)
-    loads[3].wait()
+        vs[t * VP : t * VP + BOXES] = v_ref[:, t * 128 : (t + 1) * 128].astype(F32)
+    make_skeletons(qs, vs, xv_ref, su_ref)
+    stores[1].start()
+    loads[7].wait()
     for t in range(32):
-        es[t * BOXES : (t + 1) * BOXES] = e_ref[:, t * 128 : (t + 1) * 128].astype(F32)
+        es[t * VP : t * VP + BOXES] = e_ref[:, t * 128 : (t + 1) * 128].astype(F32)
+    make_parents(es, xe_ref, su_ref)
+    up_ref[...] = su_ref[UP_ROW:]
+    for j in range(2, 5):
+        stores[j].start()
+    for store in stores:
+        store.wait()
+
+
+def make_skeletons(qs, vs, xv_ref, su_ref):
     row = iota((32, 128), 0)
     lane = iota((32, 128), 1)
     pick = onehot((lane % 32) == row)
@@ -85,7 +132,7 @@
         parts = []
         for c in range(4):
             b = g * 4 + c
-            rows = qs[pl.ds(b, 8, stride=BOXES), :]
+            rows = qs[pl.ds(b, 8, stride=VP), :]
             parts += [jnp.where(lane8 == m, rows, 0.0) for m in range(4)]
         weights = jnp.concatenate(parts, axis=0).astype(BF16)
         q2 = nt(pick, weights)
@@ -93,7 +140,7 @@
         vb = []
         for c in range(4):
             b = g * 4 + c
-            vb += [vs[pl.ds(m * BOXES + b, 8, stride=4 * BOXES), :] for m in range(4)]
+            vb += [vs[pl.ds(m * VP + b, 8, stride=4 * VP), :] for m in range(4)]
         xv = jnp.concatenate(vb, axis=0).astype(BF16)
         xv_ref[g * 128 : (g + 1) * 128] = xv
         z = nn(lhs, xv)
@@ -103,6 +150,10 @@
             odd = half_swap(z[o + 32 : o + 48]) + z[o + 48 : o + 64]
             r = (g * 2 + u) * 16
             su_ref[r : r + 16] = jnp.where(low, even, odd).astype(BF16)
+
+
+def make_parents(es, xe_ref, su_ref):
+    low = iota((16, 128), 1) < 64
     prow = iota((256, 256), 0)
     pcol = iota((256, 256), 1)
     spread = onehot(
@@ -119,7 +170,7 @@
             moved = nn(wide, spread)
             lhs.append(jnp.concatenate([moved[:, :128], moved[:, 128:]], axis=0))
             for c in range(4):
-                xe.append(es[pl.ds(g * 4 + c, 32, stride=BOXES), :])
+                xe.append(es[pl.ds(g * 4 + c, 32, stride=VP), :])
         lhs = jnp.concatenate(lhs, axis=1).astype(BF16)
         xe = jnp.concatenate(xe, axis=0).astype(BF16)
         xe_ref[p * 256 : (p + 1) * 256] = xe
@@ -130,7 +181,6 @@
             other = half_swap(z[:16]) + z[16:]
             r = UP_ROW + (p // 2) * 16
             su_ref[r : r + 16] = jnp.where(low, lifted, other).astype(BF16)
-    up_ref[...] = su_ref[UP_ROW:]
 
 
 def pack_charges(qs, out_ref):
@@ -139,7 +189,7 @@
     for u in range(PAIRS):
         parts = []
         for c in range(2):
-            rows = qs[pl.ds(u * 2 + c, 8, stride=BOXES), :]
+            rows = qs[pl.ds(u * 2 + c, 8, stride=VP), :]
             for i in range(8):
                 parts.append(jnp.where(own, jnp.broadcast_to(rows[i : i + 1], (8, 128)), 0.0))
         weights = jnp.concatenate(parts, axis=0).astype(BF16)
@@ -147,17 +197,22 @@
         out_ref[r : r + 16] = nt(pick, weights).astype(BF16)
 
 
-def table_kernel(leaf_ref, upper_ref, after_ref, wl_ref, wu_ref, ts):
+def turn_table(ref, out, ts, count):
     low = iota((32, 128), 1) < 64
-    for ref, out, count in ((leaf_ref, wl_ref, OFFSETS), (upper_ref, wu_ref, UPPER)):
-        for t in range(32):
-            ts[t * count : (t + 1) * count] = ref[:, t * 128 : (t + 1) * 128].astype(F32)
-        for u in range(count // 2):
-            first = ts[pl.ds(2 * u, 32, stride=count), :]
-            second = ts[pl.ds(2 * u + 1, 32, stride=count), :]
-            even = jnp.where(low, first, half_swap(second))
-            odd = jnp.where(low, half_swap(first), second)
-            out[:, u * 128 : (u + 1) * 128] = jnp.concatenate([even, odd], axis=0).astype(BF16)
+    pitch = count + 4
+    for t in range(32):
+        ts[t * pitch : t * pitch + count] = ref[:, t * 128 : (t + 1) * 128].astype(F32)
+    for u in range(count // 2):
+        first = ts[pl.ds(2 * u, 32, stride=pitch), :]
+        second = ts[pl.ds(2 * u + 1, 32, stride=pitch), :]
+        even = jnp.where(low, first, half_swap(second))
+        odd = jnp.where(low, half_swap(first), second)
+        out[:, u * 128 : (u + 1) * 128] = jnp.concatenate([even, odd], axis=0).astype(BF16)
+
+
+def table_kernel(leaf_ref, upper_ref, after_ref, wl_ref, wu_ref, tl, tu):
+    turn_table(leaf_ref, wl_ref, tl, OFFSETS)
+    turn_table(upper_ref, wu_ref, tu, UPPER)
 
 
 def split3(x):
@@ -181,7 +236,6 @@
 
 
 STEP = 8
-TOTAL = 3 * BOXES
 
 
 def leaf_sides(own_ref, ev_ref, od_ref):
@@ -189,7 +243,7 @@
     return ((1, own_ref), (2 - 2 * odd, ev_ref), (2 * odd, od_ref))
 
 
-def near_tables_kernel(own_ref, ev_ref, od_ref, x_ref, after_ref, qt, yt, at, bs):
+def near_tables_kernel(own_ref, ev_ref, od_ref, x_ref, qt, yt, at, bs):
     sides = leaf_sides(own_ref, ev_ref, od_ref)
     for side, ref in sides:
         spread_pairs(ref, Q_ROW, S_ROWS, qt, side * BOXES)
@@ -208,9 +262,9 @@
         y0, y1, y2 = dup3(xy, z)
         n = split3(SCALE * (y0 * y0 + y1 * y1 + y2 * y2))
         for k, v in enumerate((y0, y0, y0, y1, y1, y1, y2, y2, y2, *n, ones, ones, ones, zeros)):
-            bs[j, k * BOXES : (k + 1) * BOXES] = v
+            bs[j, k * VP : k * VP + BOXES] = v
         for b in range(BOXES):
-            yt[side * BOXES + b] = bs[j, pl.ds(b, 16, stride=BOXES), :].astype(BF16)
+            yt[side * BOXES + b] = bs[j, pl.ds(b, 16, stride=VP), :].astype(BF16)
     yt[TOTAL] = onehot(iota((16, 128), 0) >= 12)
     zx = jnp.concatenate([x_ref[:, 128:], jnp.zeros((BOXES, 64), F32)], axis=1)
     x0, x1, x2 = dup3(x_ref[:, :128], zx)
@@ -219,21 +273,15 @@
     for x in (x0, x1, x2):
         cols += list(split3((-2.0 * SCALE) * x))
     for k, v in enumerate((*cols, ones, ones, ones, *n, zeros)):
-        bs[3, k * BOXES : (k + 1) * BOXES] = v
+        bs[3, k * VP : k * VP + BOXES] = v
     eye = onehot((iota((64, 128), 0) == iota((64, 128), 1)))
     for b in range(BOXES):
-        at[b] = nt(eye, bs[3, pl.ds(b, 16, stride=BOXES), :].astype(BF16)).astype(BF16)
+        at[b] = nt(eye, bs[3, pl.ds(b, 16, stride=VP), :].astype(BF16)).astype(BF16)
     at[BOXES] = jnp.zeros((64, 16), BF16) + onehot(iota((64, 16), 1) == 12)
 
 
-def near_kernel(ids_ref, count_ref, qt, yt, at, after_ref, out_ref, slot_v, slot_s, ks, qs, acc, place, sums, sem):
-    first = (lax.axis_index(("box", "sub")) - 1) * BOXES
-    counts = count_ref[...]
-    slot_v[...] = jnp.full((40, 128), TOTAL, jnp.int32)
-    slot_v[:NEAR, :BOXES] = jnp.where(iota((NEAR, BOXES), 0) < counts, ids_ref[...] - first, TOTAL)
-    slot_v[32:33] = jnp.zeros((1, 128), jnp.int32)
-    slot_v[32:33, :BOXES] = counts
-    copy = pltpu.make_async_copy(slot_v, slot_s, sem)
+def near_kernel(int_ref, qt, yt, at, after_ref, out_ref, slot_s, ks, qs, acc, place, sums, sem):
+    copy = pltpu.make_async_copy(int_ref.at[:SLOT_ROWS], slot_s, sem)
     copy.start()
     for b in range(BOXES + 1):
         acc[b] = jnp.zeros((16, 64), F32)
@@ -280,7 +328,7 @@
             for s in range(8):
                 moved = tiles[s] if s == c else pltpu.roll(tiles[s], (16 * (s - c)) % 128, 1)
                 total_tile = moved if total_tile is None else jnp.where(lane8 == s, moved, total_tile)
-            out_ref[pl.ds(g * 8 + c, 8, stride=BOXES), :] = total_tile
+            out_ref[pl.ds(g * 8 + c, 8, stride=VP), :] = total_tile
 
 
 def couple(table, w_ref, ids, boxes, offsets, low):
@@ -296,22 +344,24 @@
     return nt(lhs, w_ref[...])
 
 
-def field_kernel(
-    leaf_ref, pid_ref, su_ref, ev_ref, od_ref, x3_ref, be_ref, bo_ref, wl_ref, wu_ref, xv_ref, xe_ref, near_ref,
-    out_ref, st, ut, fs, ps, ids_v, ids, pids_v, pids, sems,
-):
-    first = (lax.axis_index(("box", "sub")) - 1) * BOXES
-    first_parent = (lax.axis_index("box") - 1) * 4 * PARENTS
-    sub = lax.axis_index("sub")
-    ids_v[:, :OFFSETS] = leaf_ref[...] - first
-    pids_v[:PARENTS, :UPPER] = pid_ref[...] - first_parent
-    copies = [pltpu.make_async_copy(ids_v, ids, sems.at[0]), pltpu.make_async_copy(pids_v, pids, sems.at[1])]
-    for copy in copies:
-        copy.start()
+def leaf_kernel(int_ref, su_ref, ev_ref, od_ref, wl_ref, out_ref, st, ids, sem):
     low = iota((16, 128), 1) < 64
-
+    copy = pltpu.make_async_copy(int_ref.at[LEAF_ROW : LEAF_ROW + BOXES], ids, sem)
+    copy.start()
     for side, ref in leaf_sides(su_ref, ev_ref, od_ref):
         spread_pairs(ref, 0, S_ROWS, st, side * BOXES)
+    copy.wait()
+    out_ref[:, :64] = couple(st, wl_ref, ids, BOXES, OFFSETS, low)
+
+
+def field_kernel(
+    int_ref, up_ref, ev_ref, x3_ref, be_ref, bo_ref, wu_ref, xv_ref, xe_ref, part_ref, near_ref,
+    out_ref, ut, fs, ps, pids, sem,
+):
+    sub = lax.axis_index("sub")
+    copy = pltpu.make_async_copy(int_ref.at[PID_ROW:INT_ROWS], pids, sem)
+    copy.start()
+    low = iota((16, 128), 1) < 64
     odd = lax.axis_index("box") % 2
 
     def parents(ref, row, group, flip):
@@ -320,12 +370,11 @@
     for group, ref in ((2 - 2 * odd, be_ref), (2 * odd, bo_ref)):
         for j, flip in enumerate((0, 1, 3, 2)):
             parents(ref, j * U_ROWS, group, flip)
-    parents(su_ref, UP_ROW, 1, 0)
+    parents(up_ref, 0, 1, 0)
     parents(ev_ref, UP_ROW, 1, 1)
     parents(x3_ref, 0, 1, 3)
     parents(x3_ref, U_ROWS, 1, 2)
-    for copy in copies:
-        copy.wait()
+    copy.wait()
     upper = couple(ut, wu_ref, pids, PARENTS, UPPER, low)
     r64 = iota((64, 128), 0)
     c64 = iota((64, 128), 1)
@@ -344,8 +393,7 @@
             fs[(p * 8 + c) * 16 : (p * 8 + c + 1) * 16] = jnp.where(lane16 < 32, a, b)
     lane8 = iota((8, 128), 1) // 32
     low64 = iota((16, 128), 1) < 64
-    part = couple(st, wl_ref, ids, BOXES, OFFSETS, low)
-    field = (part + fs[:, :64]).astype(BF16)
+    field = (part_ref[:, :64] + fs[:, :64]).astype(BF16)
     wide = nn(field, natural)
     for g in range(BOXES // 4):
         parts = []
@@ -361,9 +409,9 @@
                 if m != c:
                     piece = pltpu.roll(piece, (32 * (m - c)) % 128, 1)
                 tile = piece if tile is None else jnp.where(lane8 == m, piece, tile)
-            ps[pl.ds(g * 4 + c, 8, stride=BOXES), :] = tile
+            ps[pl.ds(g * 4 + c, 8, stride=VP), :] = tile
     for i in range(8):
-        rows = slice(i * BOXES, (i + 1) * BOXES)
+        rows = slice(i * VP, i * VP + BOXES)
         out_ref[:, i * 128 : (i + 1) * 128] = near_ref[rows] + ps[rows]
 
 
@@ -387,63 +435,67 @@
     return jax.ShapeDtypeStruct(dims, dtype)
 
 
-def run_skeleton(charges, coords, basis, transfer):
+def run_prepare(charges, coords, near_ids, near_count, leaf_ids, parent_ids, basis, transfer):
+    hbm = pl.BlockSpec(memory_space=pltpu.HBM)
     return pl.pallas_call(
-        skeleton_kernel,
-        out_shape=(shape(ALL_ROWS, 128), shape(U_ROWS, 128), shape(BOXES * 32, 128), shape(BOXES * 32, 128)),
-        in_specs=[pl.BlockSpec(memory_space=pltpu.HBM)] * 4,
-        out_specs=(VM,) * 4,
+        prepare_kernel,
+        out_shape=tuple(jax.ShapeDtypeStruct(d, t) for d, t in OUT_SHAPES),
+        in_specs=[hbm] * len(IN_SHAPES),
+        out_specs=(hbm,) * len(OUT_SHAPES),
         scratch_shapes=[
-            pltpu.VMEM((BOXES, 1024), BF16),
-            pltpu.VMEM((BOXES, 192), F32),
-            pltpu.VMEM((BOXES, 4096), BF16),
-            pltpu.VMEM((BOXES, 4096), BF16),
-            pltpu.VMEM((8 * BOXES, 128), F32),
-            pltpu.VMEM((32 * BOXES, 128), F32),
-            pltpu.VMEM((32 * BOXES, 128), F32),
-            pltpu.SemaphoreType.DMA((4,)),
+            *(pltpu.VMEM(d, t) for d, t in IN_SHAPES),
+            *(pltpu.VMEM(d, t) for d, t in OUT_SHAPES),
+            pltpu.VMEM((8 * VP, 128), F32),
+            pltpu.VMEM((32 * VP, 128), F32),
+            pltpu.VMEM((32 * VP, 128), F32),
+            pltpu.SemaphoreType.DMA((len(IN_SHAPES),)),
+            pltpu.SemaphoreType.DMA((len(OUT_SHAPES),)),
         ],
         compiler_params=params(60 << 20),
-        cost_estimate=cost(4.0),
-        name="skeleton",
-    )(charges, coords, basis, transfer)
-
-
-def run_tables(leaf_table, upper_table, su):
+        cost_estimate=cost(5.0),
+        name="prepare",
+    )(
+        charges, coords, near_ids.T, near_count.reshape(1, BOXES), leaf_ids, parent_ids, basis, transfer
+    )
+
+
+def run_tables(leaf_table, upper_table, up):
     return pl.pallas_call(
         table_kernel,
         out_shape=(shape(64, OFFSETS * 64), shape(64, UPPER * 64)),
         in_specs=[VM] * 2 + [HB],
         out_specs=(VM,) * 2,
-        scratch_shapes=[pltpu.VMEM((32 * OFFSETS, 128), F32)],
+        scratch_shapes=[
+            pltpu.VMEM((32 * (OFFSETS + 4), 128), F32),
+            pltpu.VMEM((32 * (UPPER + 4), 128), F32),
+        ],
         compiler_params=params(),
-        cost_estimate=cost(2.0),
+        cost_estimate=cost(1.0),
         name="tables",
-    )(leaf_table, upper_table, su)
-
-
-def run_near_tables(su, ev, od, coords, wl):
+    )(leaf_table, upper_table, up)
+
+
+def run_near_tables(su, ev, od, coords):
     return pl.pallas_call(
         near_tables_kernel,
         out_shape=(shape(TOTAL + 1, 16, 128), shape(TOTAL + 1, 16, 128), shape(BOXES + 1, 64, 16)),
-        in_specs=[VM] * 4 + [HB],
+        in_specs=[VM] * 4,
         out_specs=(VM,) * 3,
-        scratch_shapes=[pltpu.VMEM((4, 16 * BOXES, 128), F32)],
+        scratch_shapes=[pltpu.VMEM((4, 16 * VP, 128), F32)],
         compiler_params=params(),
         cost_estimate=cost(1.0),
         name="near_tables",
-    )(su, ev, od, coords, wl)
-
-
-def run_near(near_ids, near_count, qt, yt, at, x3):
+    )(su, ev, od, coords)
+
+
+def run_near(ints, qt, yt, at, x3):
     return pl.pallas_call(
         near_kernel,
-        out_shape=shape(8 * BOXES, 128, dtype=F32),
-        in_specs=[VM] * 5 + [HB],
+        out_shape=shape(8 * VP, 128, dtype=F32),
+        in_specs=[VM] * 4 + [HB],
         out_specs=VM,
         scratch_shapes=[
-            pltpu.VMEM((40, 128), jnp.int32),
-            pltpu.SMEM((40, 128), jnp.int32),
+            pltpu.SMEM((SLOT_ROWS, 128), jnp.int32),
             pltpu.VMEM((2, STEP, 64, 512), BF16),
             pltpu.VMEM((2, STEP, 16, 512), BF16),
             pltpu.VMEM((BOXES + 1, 16, 64), F32),
@@ -454,30 +506,43 @@
         compiler_params=params(),
         cost_estimate=cost(7.0),
         name="near",
-    )(near_ids.T, near_count.reshape(1, BOXES), qt, yt, at, x3)
-
-
-def run_field(leaf_ids, parent_ids, su, ev, od, x3, be, bo, wl, wu, xv, xe, near):
+    )(ints, qt, yt, at, x3)
+
+
+def run_leaf(ints, su, ev, od, wl):
+    return pl.pallas_call(
+        leaf_kernel,
+        out_shape=shape(BOXES * 16, 128, dtype=F32),
+        in_specs=[VM] * 5,
+        out_specs=VM,
+        scratch_shapes=[
+            pltpu.VMEM((3 * BOXES, 16, 128), BF16),
+            pltpu.SMEM((BOXES, 128), jnp.int32),
+            pltpu.SemaphoreType.DMA,
+        ],
+        compiler_params=params(),
+        cost_estimate=cost(5.0),
+        name="leaf",
+    )(ints, su, ev, od, wl)
+
+
+def run_field(ints, up, ev, x3, be, bo, wu, xv, xe, part, near):
     return pl.pallas_call(
         field_kernel,
         out_shape=shape(BOXES, 1024, dtype=F32),
-        in_specs=[VM] * 13,
+        in_specs=[VM] * 11,
         out_specs=VM,
         scratch_shapes=[
-            pltpu.VMEM((3 * BOXES, 16, 128), BF16),
             pltpu.VMEM((12 * PARENTS, 16, 128), BF16),
             pltpu.VMEM((BOXES * 16, 128), F32),
-            pltpu.VMEM((8 * BOXES, 128), F32),
-            pltpu.VMEM((BOXES, 128), jnp.int32),
-            pltpu.SMEM((BOXES, 128), jnp.int32),
-            pltpu.VMEM((8, 128), jnp.int32),
+            pltpu.VMEM((8 * VP, 128), F32),
             pltpu.SMEM((8, 128), jnp.int32),
-            pltpu.SemaphoreType.DMA((2,)),
+            pltpu.SemaphoreType.DMA,
         ],
         compiler_params=params(),
-        cost_estimate=cost(9.0),
+        cost_estimate=cost(3.0),
         name="field",
-    )(leaf_ids, parent_ids, su, ev, od, x3, be, bo, wl, wu, xv, xe, near)
+    )(ints, up, ev, x3, be, bo, wu, xv, xe, part, near)
 
 
 def local(
@@ -487,18 +552,21 @@
     boxes = lax.axis_size("box")
     subs = lax.axis_size("sub")
     chain = boxes * subs
-    su, up, xv, xe = run_skeleton(charges, coords, basis, transfer)
+    ints, xv, su, up, xe = run_prepare(
+        charges, coords, near_ids, near_count, leaf_ids, parent_ids, basis, transfer
+    )
     ev = lax.ppermute(su, "sub", [(i, i ^ 1) for i in range(subs)])
     od = lax.ppermute(su, flat, [(i, ((i + 1) ^ 1) - 1) for i in range(1, chain - 1)])
-    wl, wu = run_tables(leaf_table, upper_table, su)
+    wl, wu = run_tables(leaf_table, upper_table, up)
     pair = jnp.concatenate([up, ev[UP_ROW:]], axis=0)
     x3 = lax.ppermute(pair, "sub", [(i, i ^ 3) for i in range(subs)])
-    qt, yt, at = run_near_tables(su, ev, od, coords, wl)
+    qt, yt, at = run_near_tables(su, ev, od, coords)
+    part = run_leaf(ints, su, ev, od, wl)
     branch = jnp.concatenate([pair, x3], axis=0)
     be = lax.ppermute(branch, "box", [(i, i ^ 1) for i in range(boxes)])
     bo = lax.ppermute(branch, "box", [(i, ((i + 1) ^ 1) - 1) for i in range(1, boxes - 1)])
-    near = run_near(near_ids, near_count, qt, yt, at, x3)
-    return run_field(leaf_ids, parent_ids, su, ev, od, x3, be, bo, wl, wu, xv, xe, near)
+    near = run_near(ints, qt, yt, at, x3)
+    return run_field(ints, up, ev, x3, be, bo, wu, xv, xe, part, near)
 
 
 def solution(mesh):

time: 52.4 us -> 49.1 us (0.937)
  waiting for transfers between devices: 4.09 us -> 0.65 us
  starting transfers between devices: 22.5 us -> 25.8 us
  Pallas kernels: 22.3 us -> 20.7 us
  local copies, waits for them, and re-layouts: 2.27 us -> 0.79 us
    pallas_call x2 -> x3, Pallas kernels: 12.1 us -> 16.6 us  [the longest x1 6.19 us: run_near(): pl.pallas_call(near_kernel, out_shape=shape(8 * VP, 128, dtype=F32), in_s...]
    pallas_call x1, Pallas kernels: 7.33 us -> 2.87 us  [run_field(): pl.pallas_call(field_kernel, out_shape=shape(BOXES, 1024, dtype=F32), in_...]
    ppermute x1, waiting for transfers between devices: 4.08 us -> 0.01 us  [local(): x3 = lax.ppermute(pair, 'sub', [(i, i ^ 3) for i in range(subs)])]
    ppermute x1, starting transfers between devices: 3.02 us -> 6.3 us  [local(): lax.ppermute(branch, 'box', [(i, (i + 1 ^ 1) - 1) for i in range(1, boxes...]
    unnamed x24 -> x18, local copies, waits for them, and re-layouts: 2.27 us -> 0.79 us
    pallas_call x1, Pallas kernels: 2.04 us -> 0.59 us  [run_tables(): pl.pallas_call(table_kernel, out_shape=(shape(64, OFFSETS * 64), shape(64...]
    ppermute x1, waiting for transfers between devices: 0.01 us -> 0.64 us  [local(): lax.ppermute(su, flat, [(i, (i + 1 ^ 1) - 1) for i in range(1, chain - 1)])]
  transfers between devices with their start and end apart: 5 -> 5, of which waited for: 1 -> 1; matrix products, arithmetic and copies ran while one was open for 0% -> 0% of each run, Pallas kernels for 19% -> 25%
where the time goes in v4:
time: 49.1 us; the launch traced here: 48.1 us
  starting transfers between devices  25.8 us (53%)
  Pallas kernels  20.7 us (42%)
  local copies, waits for them, and re-layouts  0.79 us (2%)
  waiting for transfers between devices  0.65 us (1%)
    ppermute x1, starting transfers between devices, local(): lax.ppermute(su, flat, [(i, (i + 1 ^ 1) - 1) for i in range(1, chain - 1)])  12.3 us
    ppermute x1, starting transfers between devices, local(): lax.ppermute(branch, 'box', [(i, (i + 1 ^ 1) - 1) for i in range(1, boxes...  6.3 us
    pallas_call x1, Pallas kernels, run_near(): pl.pallas_call(near_kernel, out_shape=shape(8 * VP, 128, dtype=F32), in_s...  6.19 us
    pallas_call x1, Pallas kernels, run_prepare(): pl.pallas_call(prepare_kernel, out_shape=tuple((jax.ShapeDtypeStruct(d, t...  5.65 us
    pallas_call x1, Pallas kernels, run_leaf(): pl.pallas_call(leaf_kernel, out_shape=shape(BOXES * 16, 128, dtype=F32),...  4.76 us
    ppermute x1, starting transfers between devices, local(): ev = lax.ppermute(su, 'sub', [(i, i ^ 1) for i in range(subs)])  3.4 us
    pallas_call x1, Pallas kernels, run_field(): pl.pallas_call(field_kernel, out_shape=shape(BOXES, 1024, dtype=F32), in_...  2.87 us
    ppermute x1, starting transfers between devices, local(): x3 = lax.ppermute(pair, 'sub', [(i, i ^ 3) for i in range(subs)])  1.92 us
  transfers between devices with their start and end apart: 5, of which 1 were waited for; matrix products, arithmetic and copies ran while one was open for 0% of the time, Pallas kernels for 25%

profile of v4, /device:TPU:24, one launch (start us, length us, event | category | flops | bytes accessed | tf_op | source)
XLA Modules:
  0.0 48.1 jit_solution(5497146126275710924)
XLA Ops:
  0.0 0.0 copy-start.2
  0.0 0.0 copy-start.3
  0.0 5.7 %prepare.1 = (s32[96,128]{1,0:T(8,128)}, bf16[1536,128]{1,0:T(8,128)(2,1)}, bf16[912,128]{1,0:T(8,128)(2,1)}, bf16[48,128]{1,0:T(8,128)(2,1)}, bf16[1536,128]{1,0:T(8,128)(2,1)}) custom-call(bf16[48,1024]{1,0:T(8,128)(2,1)} %refs_0_.1, f32[48,192]{1,0:T(8,128)} %x_ref.1, s32[27,48]{1,0:T(8,128)} %bitcast.2, s32[1,48]{1,0:T(1,128)} %bitcast.3, ...), custom_call_target="tpu_custom_call" | custom-call | flops 5000000000 | bytes 1048576 | tf_op jit(solution)/shard_map/prepare/pallas_call | solution.py:440
  5.7 3.4 %collective-permute-start = (bf16[912,128]{1,0:T(8,128)(2,1)}, bf16[912,128]{1,0:T(8,128)(2,1)S(1)}, u32[]{:S(2)}, u32[]{:S(2)}) collective-permute-start(bf16[912,128]{1,0:T(8,128)(2,1)} %get-tuple-element.17.su_ref.own_ref), channel_id=1, source_target_pairs={{0,1},{1,0},{2,3},{3,2},{4,5},{5,4},{6,7},{7,6},{8,9},{9,8},{10,11... | collective-permute-start | bytes 700424 | tf_op jit(solution)/shard_map/ppermute | solution.py:558
  9.1 12.3 %collective-permute-start.4 = (bf16[912,128]{1,0:T(8,128)(2,1)}, bf16[912,128]{1,0:T(8,128)(2,1)S(1)}, u32[]{:S(2)}, u32[]{:S(2)}) collective-permute-start(bf16[912,128]{1,0:T(8,128)(2,1)} %get-tuple-element.17.su_ref.own_ref), channel_id=1, source_target_pairs={{1,2},{2,1},{3,4},{4,3},{5,6},{6,5},{7,8},{8,7},{9,10},{10,9},{11,... | collective-permute-start | bytes 700424 | tf_op jit(solution)/shard_map/ppermute | solution.py:559
  21.4 0.0 copy-done.2
  21.4 0.0 copy-done.3
  21.4 0.0 copy-start
  21.4 0.7 %copy-done = bf16[48,128]{1,0:T(8,128)(2,1)S(1)} copy-done((bf16[48,128]{1,0:T(8,128)(2,1)S(1)}, bf16[48,128]{1,0:T(8,128)(2,1)}, u32[]{:S(2)}) %copy-start) | copy-done | bytes 12312
  22.1 0.0 copy-start.4
  22.1 0.6 %tables.1 = (bf16[64,6144]{1,0:T(8,128)(2,1)S(1)}, bf16[64,4096]{1,0:T(8,128)(2,1)S(1)}) custom-call(bf16[96,4096]{1,0:T(8,128)(2,1)S(1)} %copy-done.2, bf16[64,4096]{1,0:T(8,128)(2,1)S(1)} %copy-done.3, bf16[48,128]{1,0:T(8,128)(2,1)S(1)} %copy-done), custom_call_target="tpu_custom_call" | custom-call | flops 1000000000 | bytes 1048576 | tf_op jit(solution)/shard_map/tables/pallas_call | solution.py:463
  22.7 0.0 copy-start.8
  22.7 0.0 collective-permute-done.ev_ref
  22.7 1.9 %collective-permute-start.1 = (bf16[96,128]{1,0:T(8,128)(2,1)S(1)}, bf16[96,128]{1,0:T(8,128)(2,1)S(1)}, u32[]{:S(2)}, u32[]{:S(2)}) collective-permute-start(bf16[96,128]{1,0:T(8,128)(2,1)S(1)} %pad_maximum_fusion.1), channel_id=1, source_target_pairs={{0,3},{1,2},{2,1},{3,0},{4,7},{5,6},{6,5},{7,4},{8,11},{9,10},{10,... | collective-permute-start | bytes 73736 | tf_op jit(solution)/shard_map/ppermute | solution.py:562
  24.7 0.6 %collective-permute-done.4.od_ref = bf16[912,128]{1,0:T(8,128)(2,1)S(1)} collective-permute-done((bf16[912,128]{1,0:T(8,128)(2,1)}, bf16[912,128]{1,0:T(8,128)(2,1)S(1)}, u32[]{:S(2)}, u32[]{:S(2)}) %collective-permute-start.4) | collective-permute-done | bytes 233504 | tf_op jit(solution)/shard_map/ppermute | solution.py:559
  25.3 0.0 copy-done.4
  25.3 0.0 copy-done.8
  25.3 0.0 copy-start.5
  25.3 4.8 %leaf.1.part_ref = f32[768,128]{1,0:T(8,128)S(1)} custom-call(s32[96,128]{1,0:T(8,128)S(1)} %copy-done.8, bf16[912,128]{1,0:T(8,128)(2,1)S(1)} %copy-done.4, bf16[912,128]{1,0:T(8,128)(2,1)S(1)} %collective-permute-done.ev_ref, bf16[912,128]{1,0:T(8,128)(2,1)S(1)} %collective-permute-done.4.od_ref, bf16[64,6144]{1,0:T(8,128)(2,1)S(1)} %get-tuple-element.21.wl_ref), custom_call_target="tpu_custom_call" | custom-call | flops 5000000000 | bytes 1048576 | tf_op jit(solution)/shard_map/leaf/pallas_call | solution.py:513
  30.1 0.0 copy-done.5
  30.1 0.0 copy-start.1
  30.1 0.6 %near_tables.1 = (bf16[145,16,128]{2,1,0:T(8,128)(2,1)S(1)}, bf16[145,16,128]{2,1,0:T(8,128)(2,1)S(1)}, bf16[49,64,16]{2,1,0:T(8,128)(2,1)S(1)}) custom-call(bf16[912,128]{1,0:T(8,128)(2,1)S(1)} %copy-done.4, bf16[912,128]{1,0:T(8,128)(2,1)S(1)} %collective-permute-done.ev_ref, bf16[912,128]{1,0:T(8,128)(2,1)S(1)} %collective-permute-done.4.od_ref, ...), custom_call_target="tpu_custom_call" | custom-call | flops 1000000000 | bytes 1048576 | tf_op jit(solution)/shard_map/near_tables/pallas_call | solution.py:479
  30.7 0.0 collective-permute-done.1.after_ref.x3_ref
  30.7 0.1 copy-done.1
  30.8 1.9 %collective-permute-start.2 = (bf16[192,128]{1,0:T(8,128)(2,1)S(1)}, bf16[192,128]{1,0:T(8,128)(2,1)S(1)}, u32[]{:S(2)}, u32[]{:S(2)}) collective-permute-start(bf16[192,128]{1,0:T(8,128)(2,1)S(1)} %pad_maximum_fusion), channel_id=1, source_target_pairs={{0,4},{4,0},{8,12},{12,8},{16,20},{20,16},{24,28},{28,24},{32,36},... | collective-permute-start | bytes 147464 | tf_op jit(solution)/shard_map/ppermute | solution.py:566
  32.7 6.3 %collective-permute-start.3 = (bf16[192,128]{1,0:T(8,128)(2,1)S(1)}, bf16[192,128]{1,0:T(8,128)(2,1)S(1)}, u32[]{:S(2)}, u32[]{:S(2)}) collective-permute-start(bf16[192,128]{1,0:T(8,128)(2,1)S(1)} %pad_maximum_fusion), channel_id=1, source_target_pairs={{4,8},{8,4},{12,16},{16,12},{20,24},{24,20},{28,32},{32,28},{36,40... | collective-permute-start | bytes 147464 | tf_op jit(solution)/shard_map/ppermute | solution.py:567
  39.0 0.0 copy-start.6
  39.0 0.0 copy-start.7
  39.0 6.2 %near.1.near_ref = f32[416,128]{1,0:T(8,128)S(1)} custom-call(s32[96,128]{1,0:T(8,128)S(1)} %copy-done.8, bf16[145,16,128]{2,1,0:T(8,128)(2,1)S(1)} %get-tuple-element.22.qt, bf16[145,16,128]{2,1,0:T(8,128)(2,1)S(1)} %get-tuple-element.23.yt, bf16[49,64,16]{2,1,0:T(8,128)(2,1)S(1)} %get-tuple-element.24.at, ...), custom_call_target="tpu_custom_call" | custom-call | flops 7000000000 | bytes 1048576 | tf_op jit(solution)/shard_map/near/pallas_call | solution.py:492
  45.2 0.0 collective-permute-done.2.be_ref
  45.2 0.0 collective-permute-done.3.bo_ref
  45.3 0.0 copy-done.6
  45.3 0.0 copy-done.7
  45.3 2.9 %field.1 = f32[48,1024]{1,0:T(8,128)} custom-call(s32[96,128]{1,0:T(8,128)S(1)} %copy-done.8, bf16[48,128]{1,0:T(8,128)(2,1)S(1)} %copy-done.1, bf16[912,128]{1,0:T(8,128)(2,1)S(1)} %collective-permute-done.ev_ref, bf16[96,128]{1,0:T(8,128)(2,1)S(1)} %collective-permute-done.1.after_ref.x3_ref, bf16[192,128]{1,0:T(8,128)(2,1)S(1)} %collective-permute-done.2.be_ref, ...), custom_call_target="tpu_custom_call" | custom-call | flops 3000000000 | bytes 1048576 | tf_op jit(solution)/shard_map/field/pallas_call | solution.py:530
  (3 shorter events, 0.0 us)
Async XLA Ops:
  0.0 21.4 %copy-start.2 = (bf16[96,4096]{1,0:T(8,128)(2,1)S(1)}, bf16[96,4096]{1,0:T(8,128)(2,1)}, u32[]{:S(2)}) copy-start(bf16[96,4096]{1,0:T(8,128)(2,1)} %leaf_ref.1) | copy-start | bytes 2359300
  0.0 21.4 %copy-start.3 = (bf16[64,4096]{1,0:T(8,128)(2,1)S(1)}, bf16[64,4096]{1,0:T(8,128)(2,1)}, u32[]{:S(2)}) copy-start(bf16[64,4096]{1,0:T(8,128)(2,1)} %upper_ref.1) | copy-start | bytes 1572868
  5.7 17.0 %collective-permute-start = (bf16[912,128]{1,0:T(8,128)(2,1)}, bf16[912,128]{1,0:T(8,128)(2,1)S(1)}, u32[]{:S(2)}, u32[]{:S(2)}) collective-permute-start(bf16[912,128]{1,0:T(8,128)(2,1)} %get-tuple-element.17.su_ref.own_ref), channel_id=1, source_target_pairs={{0,1},{1,0},{2,3},{3,2},{4,5},{5,4},{6,7},{7,6},{8,9},{9,8},{10,11... | collective-permute-start | bytes 700424 | tf_op jit(solution)/shard_map/ppermute | solution.py:558
  9.1 16.2 %collective-permute-start.4 = (bf16[912,128]{1,0:T(8,128)(2,1)}, bf16[912,128]{1,0:T(8,128)(2,1)S(1)}, u32[]{:S(2)}, u32[]{:S(2)}) collective-permute-start(bf16[912,128]{1,0:T(8,128)(2,1)} %get-tuple-element.17.su_ref.own_ref), channel_id=1, source_target_pairs={{1,2},{2,1},{3,4},{4,3},{5,6},{6,5},{7,8},{8,7},{9,10},{10,9},{11,... | collective-permute-start | bytes 700424 | tf_op jit(solution)/shard_map/ppermute | solution.py:559
  21.4 0.7 %copy-start = (bf16[48,128]{1,0:T(8,128)(2,1)S(1)}, bf16[48,128]{1,0:T(8,128)(2,1)}, u32[]{:S(2)}) copy-start(bf16[48,128]{1,0:T(8,128)(2,1)} %get-tuple-element.16.after_ref.up_ref) | copy-start | bytes 36868
  22.1 3.2 %copy-start.4 = (bf16[912,128]{1,0:T(8,128)(2,1)S(1)}, bf16[912,128]{1,0:T(8,128)(2,1)}, u32[]{:S(2)}) copy-start(bf16[912,128]{1,0:T(8,128)(2,1)} %get-tuple-element.17.su_ref.own_ref) | copy-start | bytes 700420
  22.7 2.6 %copy-start.8 = (s32[96,128]{1,0:T(8,128)S(1)}, s32[96,128]{1,0:T(8,128)}, u32[]{:S(2)}) copy-start(s32[96,128]{1,0:T(8,128)} %get-tuple-element.15.int_ref) | copy-start | bytes 147460
  22.7 8.0 %collective-permute-start.1 = (bf16[96,128]{1,0:T(8,128)(2,1)S(1)}, bf16[96,128]{1,0:T(8,128)(2,1)S(1)}, u32[]{:S(2)}, u32[]{:S(2)}) collective-permute-start(bf16[96,128]{1,0:T(8,128)(2,1)S(1)} %pad_maximum_fusion.1), channel_id=1, source_target_pairs={{0,3},{1,2},{2,1},{3,0},{4,7},{5,6},{6,5},{7,4},{8,11},{9,10},{10,... | collective-permute-start | bytes 73736 | tf_op jit(solution)/shard_map/ppermute | solution.py:562
  25.3 4.8 %copy-start.5 = (f32[48,192]{1,0:T(8,128)S(1)}, f32[48,192]{1,0:T(8,128)}, u32[]{:S(2)}) copy-start(f32[48,192]{1,0:T(8,128)} %x_ref.1) | copy-start | bytes 110596
  30.1 0.7 %copy-start.1 = (bf16[48,128]{1,0:T(8,128)(2,1)S(1)}, bf16[48,128]{1,0:T(8,128)(2,1)}, u32[]{:S(2)}) copy-start(bf16[48,128]{1,0:T(8,128)(2,1)} %get-tuple-element.16.after_ref.up_ref) | copy-start | bytes 36868
  30.8 14.4 %collective-permute-start.2 = (bf16[192,128]{1,0:T(8,128)(2,1)S(1)}, bf16[192,128]{1,0:T(8,128)(2,1)S(1)}, u32[]{:S(2)}, u32[]{:S(2)}) collective-permute-start(bf16[192,128]{1,0:T(8,128)(2,1)S(1)} %pad_maximum_fusion), channel_id=1, source_target_pairs={{0,4},{4,0},{8,12},{12,8},{16,20},{20,16},{24,28},{28,24},{32,36},... | collective-permute-start | bytes 147464 | tf_op jit(solution)/shard_map/ppermute | solution.py:566
  32.7 12.5 %collective-permute-start.3 = (bf16[192,128]{1,0:T(8,128)(2,1)S(1)}, bf16[192,128]{1,0:T(8,128)(2,1)S(1)}, u32[]{:S(2)}, u32[]{:S(2)}) collective-permute-start(bf16[192,128]{1,0:T(8,128)(2,1)S(1)} %pad_maximum_fusion), channel_id=1, source_target_pairs={{4,8},{8,4},{12,16},{16,12},{20,24},{24,20},{28,32},{32,28},{36,40... | collective-permute-start | bytes 147464 | tf_op jit(solution)/shard_map/ppermute | solution.py:567
  39.0 6.2 %copy-start.6 = (bf16[1536,128]{1,0:T(8,128)(2,1)S(1)}, bf16[1536,128]{1,0:T(8,128)(2,1)}, u32[]{:S(2)}) copy-start(bf16[1536,128]{1,0:T(8,128)(2,1)} %get-tuple-element.19.xv_ref) | copy-start | bytes 1179652
  39.0 6.2 %copy-start.7 = (bf16[1536,128]{1,0:T(8,128)(2,1)S(1)}, bf16[1536,128]{1,0:T(8,128)(2,1)}, u32[]{:S(2)}) copy-start(bf16[1536,128]{1,0:T(8,128)(2,1)} %get-tuple-element.20.xe_ref) | copy-start | bytes 1179652

commit v5 on v4

--- a/solution.py
+++ b/solution.py
@@ -231,11 +231,11 @@
 def spread_pairs(src_ref, row, rows, dst_ref, base):
     wide = nn(src_ref[row : row + rows], dup_matrix()).astype(BF16)
     for u in range(rows // 16):
-        dst_ref[base + 2 * u] = wide[u * 16 : u * 16 + 16, :128]
-        dst_ref[base + 2 * u + 1] = wide[u * 16 : u * 16 + 16, 128:]
-
-
-STEP = 8
+        dst_ref[base + 2 * u, :16] = wide[u * 16 : u * 16 + 16, :128]
+        dst_ref[base + 2 * u + 1, :16] = wide[u * 16 : u * 16 + 16, 128:]
+
+
+STEP = 12
 
 
 def leaf_sides(own_ref, ev_ref, od_ref):
@@ -243,11 +243,11 @@
     return ((1, own_ref), (2 - 2 * odd, ev_ref), (2 * odd, od_ref))
 
 
-def near_tables_kernel(own_ref, ev_ref, od_ref, x_ref, qt, yt, at, bs):
+def near_tables_kernel(own_ref, ev_ref, od_ref, x_ref, tab, at, bs):
     sides = leaf_sides(own_ref, ev_ref, od_ref)
     for side, ref in sides:
-        spread_pairs(ref, Q_ROW, S_ROWS, qt, side * BOXES)
-    qt[TOTAL] = jnp.zeros((16, 128), BF16)
+        spread_pairs(ref, Q_ROW, S_ROWS, tab, side * BOXES)
+    tab[TOTAL, :16] = jnp.zeros((16, 128), BF16)
     lanes = iota((BOXES, 128), 1) < 64
 
     def dup3(xy, z):
@@ -264,8 +264,8 @@
         for k, v in enumerate((y0, y0, y0, y1, y1, y1, y2, y2, y2, *n, ones, ones, ones, zeros)):
             bs[j, k * VP : k * VP + BOXES] = v
         for b in range(BOXES):
-            yt[side * BOXES + b] = bs[j, pl.ds(b, 16, stride=VP), :].astype(BF16)
-    yt[TOTAL] = onehot(iota((16, 128), 0) >= 12)
+            tab[side * BOXES + b, 16:] = bs[j, pl.ds(b, 16, stride=VP), :].astype(BF16)
+    tab[TOTAL, 16:] = onehot(iota((16, 128), 0) >= 12)
     zx = jnp.concatenate([x_ref[:, 128:], jnp.zeros((BOXES, 64), F32)], axis=1)
     x0, x1, x2 = dup3(x_ref[:, :128], zx)
     n = split3(SCALE * (x0 * x0 + x1 * x1 + x2 * x2 + SOFT))
@@ -280,7 +280,7 @@
     at[BOXES] = jnp.zeros((64, 16), BF16) + onehot(iota((64, 16), 1) == 12)
 
 
-def near_kernel(int_ref, qt, yt, at, after_ref, out_ref, slot_s, ks, qs, acc, place, sums, sem):
+def near_kernel(int_ref, tab, at, after_ref, out_ref, slot_s, ks, qs, acc, place, sums, sem):
     copy = pltpu.make_async_copy(int_ref.at[:SLOT_ROWS], slot_s, sem)
     copy.start()
     for b in range(BOXES + 1):
@@ -307,8 +307,8 @@
             for c in range(4):
                 one = slot_s[chunk + 2 * c, box]
                 two = slot_s[chunk + 2 * c + 1, box]
-                ys.append(jnp.where(low, yt[one], yt[two]))
-                qs[slot, j, :, c * 128 : (c + 1) * 128] = jnp.where(low, qt[one], qt[two])
+                ys.append(jnp.where(low, tab[one, 16:], tab[two, 16:]))
+                qs[slot, j, :, c * 128 : (c + 1) * 128] = jnp.where(low, tab[one, :16], tab[two, :16])
             d = nn(at[box], jnp.concatenate(ys, axis=1))
             ks[slot, j] = lax.rsqrt(d).astype(BF16)
             more = chunk + 8 < slot_s[32, box]
@@ -478,9 +478,9 @@
 def run_near_tables(su, ev, od, coords):
     return pl.pallas_call(
         near_tables_kernel,
-        out_shape=(shape(TOTAL + 1, 16, 128), shape(TOTAL + 1, 16, 128), shape(BOXES + 1, 64, 16)),
+        out_shape=(shape(TOTAL + 1, 32, 128), shape(BOXES + 1, 64, 16)),
         in_specs=[VM] * 4,
-        out_specs=(VM,) * 3,
+        out_specs=(VM,) * 2,
         scratch_shapes=[pltpu.VMEM((4, 16 * VP, 128), F32)],
         compiler_params=params(),
         cost_estimate=cost(1.0),
@@ -488,11 +488,11 @@
     )(su, ev, od, coords)
 
 
-def run_near(ints, qt, yt, at, x3):
+def run_near(ints, tab, at, x3):
     return pl.pallas_call(
         near_kernel,
         out_shape=shape(8 * VP, 128, dtype=F32),
-        in_specs=[VM] * 4 + [HB],
+        in_specs=[VM] * 3 + [HB],
         out_specs=VM,
         scratch_shapes=[
             pltpu.SMEM((SLOT_ROWS, 128), jnp.int32),
@@ -506,7 +506,7 @@
         compiler_params=params(),
         cost_estimate=cost(7.0),
         name="near",
-    )(ints, qt, yt, at, x3)
+    )(ints, tab, at, x3)
 
 
 def run_leaf(ints, su, ev, od, wl):
@@ -560,12 +560,12 @@
     wl, wu = run_tables(leaf_table, upper_table, up)
     pair = jnp.concatenate([up, ev[UP_ROW:]], axis=0)
     x3 = lax.ppermute(pair, "sub", [(i, i ^ 3) for i in range(subs)])
-    qt, yt, at = run_near_tables(su, ev, od, coords)
+    tab, at = run_near_tables(su, ev, od, coords)
     part = run_leaf(ints, su, ev, od, wl)
     branch = jnp.concatenate([pair, x3], axis=0)
     be = lax.ppermute(branch, "box", [(i, i ^ 1) for i in range(boxes)])
     bo = lax.ppermute(branch, "box", [(i, ((i + 1) ^ 1) - 1) for i in range(1, boxes - 1)])
-    near = run_near(ints, qt, yt, at, x3)
+    near = run_near(ints, tab, at, x3)
     return run_field(ints, up, ev, x3, be, bo, wu, xv, xe, part, near)
 
 

time: 49.1 us -> 49.3 us (level); the launches traced: 48.1 us -> 49.1 us
  Pallas kernels: 20.7 us -> 21.7 us
    pallas_call x1, Pallas kernels: 6.19 us -> 7.17 us  [run_near(): pl.pallas_call(near_kernel, out_shape=shape(8 * VP, 128, dtype=F32), in_s...]
  transfers between devices with their start and end apart: 5 -> 5, of which waited for: 1 -> 1; matrix products, arithmetic and copies ran while one was open for 0% -> 0% of each run, Pallas kernels for 25% -> 27%
where the time goes in v5:
time: 49.3 us; the launch traced here: 49.1 us
  starting transfers between devices  25.8 us (52%)
  Pallas kernels  21.7 us (44%)
  local copies, waits for them, and re-layouts  0.79 us (2%)
  waiting for transfers between devices  0.66 us (1%)
    ppermute x1, starting transfers between devices, local(): lax.ppermute(su, flat, [(i, (i + 1 ^ 1) - 1) for i in range(1, chain - 1)])  12.3 us
    pallas_call x1, Pallas kernels, run_near(): pl.pallas_call(near_kernel, out_shape=shape(8 * VP, 128, dtype=F32), in_s...  7.17 us
    ppermute x1, starting transfers between devices, local(): lax.ppermute(branch, 'box', [(i, (i + 1 ^ 1) - 1) for i in range(1, boxes...  6.3 us
    pallas_call x1, Pallas kernels, run_prepare(): pl.pallas_call(prepare_kernel, out_shape=tuple((jax.ShapeDtypeStruct(d, t...  5.65 us
    pallas_call x1, Pallas kernels, run_leaf(): pl.pallas_call(leaf_kernel, out_shape=shape(BOXES * 16, 128, dtype=F32),...  4.76 us
    ppermute x1, starting transfers between devices, local(): ev = lax.ppermute(su, 'sub', [(i, i ^ 1) for i in range(subs)])  3.4 us
    pallas_call x1, Pallas kernels, run_field(): pl.pallas_call(field_kernel, out_shape=shape(BOXES, 1024, dtype=F32), in_...  2.87 us
    ppermute x1, starting transfers between devices, local(): x3 = lax.ppermute(pair, 'sub', [(i, i ^ 3) for i in range(subs)])  1.92 us
  transfers between devices with their start and end apart: 5, of which 1 were waited for; matrix products, arithmetic and copies ran while one was open for 0% of the time, Pallas kernels for 27%

profile of v5, /device:TPU:24, one launch (start us, length us, event | category | flops | bytes accessed | tf_op | source)
XLA Modules:
  0.0 49.1 jit_solution(17520902395026045682)
XLA Ops:
  0.0 0.0 copy-start.2
  0.0 0.0 copy-start.3
  0.0 5.7 %prepare.1 = (s32[96,128]{1,0:T(8,128)}, bf16[1536,128]{1,0:T(8,128)(2,1)}, bf16[912,128]{1,0:T(8,128)(2,1)}, bf16[48,128]{1,0:T(8,128)(2,1)}, bf16[1536,128]{1,0:T(8,128)(2,1)}) custom-call(bf16[48,1024]{1,0:T(8,128)(2,1)} %refs_0_.1, f32[48,192]{1,0:T(8,128)} %x_ref.1, s32[27,48]{1,0:T(8,128)} %bitcast.2, s32[1,48]{1,0:T(1,128)} %bitcast.3, ...), custom_call_target="tpu_custom_call" | custom-call | flops 5000000000 | bytes 1048576 | tf_op jit(solution)/shard_map/prepare/pallas_call | solution.py:440
  5.7 3.4 %collective-permute-start = (bf16[912,128]{1,0:T(8,128)(2,1)}, bf16[912,128]{1,0:T(8,128)(2,1)S(1)}, u32[]{:S(2)}, u32[]{:S(2)}) collective-permute-start(bf16[912,128]{1,0:T(8,128)(2,1)} %get-tuple-element.16.su_ref.own_ref), channel_id=1, source_target_pairs={{0,1},{1,0},{2,3},{3,2},{4,5},{5,4},{6,7},{7,6},{8,9},{9,8},{10,11... | collective-permute-start | bytes 700424 | tf_op jit(solution)/shard_map/ppermute | solution.py:558
  9.1 12.3 %collective-permute-start.4 = (bf16[912,128]{1,0:T(8,128)(2,1)}, bf16[912,128]{1,0:T(8,128)(2,1)S(1)}, u32[]{:S(2)}, u32[]{:S(2)}) collective-permute-start(bf16[912,128]{1,0:T(8,128)(2,1)} %get-tuple-element.16.su_ref.own_ref), channel_id=1, source_target_pairs={{1,2},{2,1},{3,4},{4,3},{5,6},{6,5},{7,8},{8,7},{9,10},{10,9},{11,... | collective-permute-start | bytes 700424 | tf_op jit(solution)/shard_map/ppermute | solution.py:559
  21.4 0.0 copy-done.2
  21.4 0.0 copy-done.3
  21.4 0.0 copy-start
  21.4 0.7 %copy-done = bf16[48,128]{1,0:T(8,128)(2,1)S(1)} copy-done((bf16[48,128]{1,0:T(8,128)(2,1)S(1)}, bf16[48,128]{1,0:T(8,128)(2,1)}, u32[]{:S(2)}) %copy-start) | copy-done | bytes 12312
  22.1 0.0 copy-start.4
  22.1 0.0 copy-start.8
  22.1 0.6 %tables.1 = (bf16[64,6144]{1,0:T(8,128)(2,1)S(1)}, bf16[64,4096]{1,0:T(8,128)(2,1)S(1)}) custom-call(bf16[96,4096]{1,0:T(8,128)(2,1)S(1)} %copy-done.2, bf16[64,4096]{1,0:T(8,128)(2,1)S(1)} %copy-done.3, bf16[48,128]{1,0:T(8,128)(2,1)S(1)} %copy-done), custom_call_target="tpu_custom_call" | custom-call | flops 1000000000 | bytes 1048576 | tf_op jit(solution)/shard_map/tables/pallas_call | solution.py:463
  22.7 0.0 collective-permute-done.ev_ref
  22.7 1.9 %collective-permute-start.1 = (bf16[96,128]{1,0:T(8,128)(2,1)S(1)}, bf16[96,128]{1,0:T(8,128)(2,1)S(1)}, u32[]{:S(2)}, u32[]{:S(2)}) collective-permute-start(bf16[96,128]{1,0:T(8,128)(2,1)S(1)} %pad_maximum_fusion.1), channel_id=1, source_target_pairs={{0,3},{1,2},{2,1},{3,0},{4,7},{5,6},{6,5},{7,4},{8,11},{9,10},{10,... | collective-permute-start | bytes 73736 | tf_op jit(solution)/shard_map/ppermute | solution.py:562
  24.6 0.6 %collective-permute-done.4.od_ref = bf16[912,128]{1,0:T(8,128)(2,1)S(1)} collective-permute-done((bf16[912,128]{1,0:T(8,128)(2,1)}, bf16[912,128]{1,0:T(8,128)(2,1)S(1)}, u32[]{:S(2)}, u32[]{:S(2)}) %collective-permute-start.4) | collective-permute-done | bytes 233504 | tf_op jit(solution)/shard_map/ppermute | solution.py:559
  25.3 0.0 copy-done.4
  25.3 0.0 copy-done.8
  25.3 0.0 copy-start.5
  25.3 4.8 %leaf.1.part_ref = f32[768,128]{1,0:T(8,128)S(1)} custom-call(s32[96,128]{1,0:T(8,128)S(1)} %copy-done.8, bf16[912,128]{1,0:T(8,128)(2,1)S(1)} %copy-done.4, bf16[912,128]{1,0:T(8,128)(2,1)S(1)} %collective-permute-done.ev_ref, bf16[912,128]{1,0:T(8,128)(2,1)S(1)} %collective-permute-done.4.od_ref, bf16[64,6144]{1,0:T(8,128)(2,1)S(1)} %get-tuple-element.20.wl_ref), custom_call_target="tpu_custom_call" | custom-call | flops 5000000000 | bytes 1048576 | tf_op jit(solution)/shard_map/leaf/pallas_call | solution.py:513
  30.1 0.0 copy-done.5
  30.1 0.0 copy-start.1
  30.1 0.6 %near_tables.1 = (bf16[145,32,128]{2,1,0:T(8,128)(2,1)S(1)}, bf16[49,64,16]{2,1,0:T(8,128)(2,1)S(1)}) custom-call(bf16[912,128]{1,0:T(8,128)(2,1)S(1)} %copy-done.4, bf16[912,128]{1,0:T(8,128)(2,1)S(1)} %collective-permute-done.ev_ref, bf16[912,128]{1,0:T(8,128)(2,1)S(1)} %collective-permute-done.4.od_ref, f32[48,192]{1,0:T(8,128)S(1)} %copy-done.5), custom_call_target="tpu_custom_call" | custom-call | flops 1000000000 | bytes 1048576 | tf_op jit(solution)/shard_map/near_tables/pallas_call | solution.py:479
  30.7 0.0 collective-permute-done.1.after_ref.x3_ref
  30.7 0.1 copy-done.1
  30.8 1.9 %collective-permute-start.2 = (bf16[192,128]{1,0:T(8,128)(2,1)S(1)}, bf16[192,128]{1,0:T(8,128)(2,1)S(1)}, u32[]{:S(2)}, u32[]{:S(2)}) collective-permute-start(bf16[192,128]{1,0:T(8,128)(2,1)S(1)} %pad_maximum_fusion), channel_id=1, source_target_pairs={{0,4},{4,0},{8,12},{12,8},{16,20},{20,16},{24,28},{28,24},{32,36},... | collective-permute-start | bytes 147464 | tf_op jit(solution)/shard_map/ppermute | solution.py:566
  32.7 6.3 %collective-permute-start.3 = (bf16[192,128]{1,0:T(8,128)(2,1)S(1)}, bf16[192,128]{1,0:T(8,128)(2,1)S(1)}, u32[]{:S(2)}, u32[]{:S(2)}) collective-permute-start(bf16[192,128]{1,0:T(8,128)(2,1)S(1)} %pad_maximum_fusion), channel_id=1, source_target_pairs={{4,8},{8,4},{12,16},{16,12},{20,24},{24,20},{28,32},{32,28},{36,40... | collective-permute-start | bytes 147464 | tf_op jit(solution)/shard_map/ppermute | solution.py:567
  39.0 0.0 copy-start.6
  39.0 0.0 copy-start.7
  39.0 7.2 %near.1.near_ref = f32[416,128]{1,0:T(8,128)S(1)} custom-call(s32[96,128]{1,0:T(8,128)S(1)} %copy-done.8, bf16[145,32,128]{2,1,0:T(8,128)(2,1)S(1)} %get-tuple-element.21.tab, bf16[49,64,16]{2,1,0:T(8,128)(2,1)S(1)} %get-tuple-element.22.at, bf16[96,128]{1,0:T(8,128)(2,1)S(1)} %collective-permute-done.1.after_ref.x3_ref), custom_call_target="tpu_custom_call" | custom-call | flops 7000000000 | bytes 1048576 | tf_op jit(solution)/shard_map/near/pallas_call | solution.py:492
  46.2 0.0 collective-permute-done.2.be_ref
  46.2 0.0 collective-permute-done.3.bo_ref
  46.2 0.0 copy-done.6
  46.2 0.0 copy-done.7
  46.3 2.9 %field.1 = f32[48,1024]{1,0:T(8,128)} custom-call(s32[96,128]{1,0:T(8,128)S(1)} %copy-done.8, bf16[48,128]{1,0:T(8,128)(2,1)S(1)} %copy-done.1, bf16[912,128]{1,0:T(8,128)(2,1)S(1)} %collective-permute-done.ev_ref, bf16[96,128]{1,0:T(8,128)(2,1)S(1)} %collective-permute-done.1.after_ref.x3_ref, bf16[192,128]{1,0:T(8,128)(2,1)S(1)} %collective-permute-done.2.be_ref, ...), custom_call_target="tpu_custom_call" | custom-call | flops 3000000000 | bytes 1048576 | tf_op jit(solution)/shard_map/field/pallas_call | solution.py:530
  (3 shorter events, 0.0 us)
Async XLA Ops:
  0.0 21.4 %copy-start.2 = (bf16[96,4096]{1,0:T(8,128)(2,1)S(1)}, bf16[96,4096]{1,0:T(8,128)(2,1)}, u32[]{:S(2)}) copy-start(bf16[96,4096]{1,0:T(8,128)(2,1)} %leaf_ref.1) | copy-start | bytes 2359300
  0.0 21.4 %copy-start.3 = (bf16[64,4096]{1,0:T(8,128)(2,1)S(1)}, bf16[64,4096]{1,0:T(8,128)(2,1)}, u32[]{:S(2)}) copy-start(bf16[64,4096]{1,0:T(8,128)(2,1)} %upper_ref.1) | copy-start | bytes 1572868
  5.7 17.0 %collective-permute-start = (bf16[912,128]{1,0:T(8,128)(2,1)}, bf16[912,128]{1,0:T(8,128)(2,1)S(1)}, u32[]{:S(2)}, u32[]{:S(2)}) collective-permute-start(bf16[912,128]{1,0:T(8,128)(2,1)} %get-tuple-element.16.su_ref.own_ref), channel_id=1, source_target_pairs={{0,1},{1,0},{2,3},{3,2},{4,5},{5,4},{6,7},{7,6},{8,9},{9,8},{10,11... | collective-permute-start | bytes 700424 | tf_op jit(solution)/shard_map/ppermute | solution.py:558
  9.1 16.2 %collective-permute-start.4 = (bf16[912,128]{1,0:T(8,128)(2,1)}, bf16[912,128]{1,0:T(8,128)(2,1)S(1)}, u32[]{:S(2)}, u32[]{:S(2)}) collective-permute-start(bf16[912,128]{1,0:T(8,128)(2,1)} %get-tuple-element.16.su_ref.own_ref), channel_id=1, source_target_pairs={{1,2},{2,1},{3,4},{4,3},{5,6},{6,5},{7,8},{8,7},{9,10},{10,9},{11,... | collective-permute-start | bytes 700424 | tf_op jit(solution)/shard_map/ppermute | solution.py:559
  21.4 0.7 %copy-start = (bf16[48,128]{1,0:T(8,128)(2,1)S(1)}, bf16[48,128]{1,0:T(8,128)(2,1)}, u32[]{:S(2)}) copy-start(bf16[48,128]{1,0:T(8,128)(2,1)} %get-tuple-element.15.after_ref.up_ref) | copy-start | bytes 36868
  22.1 3.2 %copy-start.4 = (bf16[912,128]{1,0:T(8,128)(2,1)S(1)}, bf16[912,128]{1,0:T(8,128)(2,1)}, u32[]{:S(2)}) copy-start(bf16[912,128]{1,0:T(8,128)(2,1)} %get-tuple-element.16.su_ref.own_ref) | copy-start | bytes 700420
  22.1 3.2 %copy-start.8 = (s32[96,128]{1,0:T(8,128)S(1)}, s32[96,128]{1,0:T(8,128)}, u32[]{:S(2)}) copy-start(s32[96,128]{1,0:T(8,128)} %get-tuple-element.14.int_ref) | copy-start | bytes 147460
  22.7 8.0 %collective-permute-start.1 = (bf16[96,128]{1,0:T(8,128)(2,1)S(1)}, bf16[96,128]{1,0:T(8,128)(2,1)S(1)}, u32[]{:S(2)}, u32[]{:S(2)}) collective-permute-start(bf16[96,128]{1,0:T(8,128)(2,1)S(1)} %pad_maximum_fusion.1), channel_id=1, source_target_pairs={{0,3},{1,2},{2,1},{3,0},{4,7},{5,6},{6,5},{7,4},{8,11},{9,10},{10,... | collective-permute-start | bytes 73736 | tf_op jit(solution)/shard_map/ppermute | solution.py:562
  25.3 4.8 %copy-start.5 = (f32[48,192]{1,0:T(8,128)S(1)}, f32[48,192]{1,0:T(8,128)}, u32[]{:S(2)}) copy-start(f32[48,192]{1,0:T(8,128)} %x_ref.1) | copy-start | bytes 110596
  30.1 0.7 %copy-start.1 = (bf16[48,128]{1,0:T(8,128)(2,1)S(1)}, bf16[48,128]{1,0:T(8,128)(2,1)}, u32[]{:S(2)}) copy-start(bf16[48,128]{1,0:T(8,128)(2,1)} %get-tuple-element.15.after_ref.up_ref) | copy-start | bytes 36868
  30.8 15.4 %collective-permute-start.2 = (bf16[192,128]{1,0:T(8,128)(2,1)S(1)}, bf16[192,128]{1,0:T(8,128)(2,1)S(1)}, u32[]{:S(2)}, u32[]{:S(2)}) collective-permute-start(bf16[192,128]{1,0:T(8,128)(2,1)S(1)} %pad_maximum_fusion), channel_id=1, source_target_pairs={{0,4},{4,0},{8,12},{12,8},{16,20},{20,16},{24,28},{28,24},{32,36},... | collective-permute-start | bytes 147464 | tf_op jit(solution)/shard_map/ppermute | solution.py:566
  32.7 13.5 %collective-permute-start.3 = (bf16[192,128]{1,0:T(8,128)(2,1)S(1)}, bf16[192,128]{1,0:T(8,128)(2,1)S(1)}, u32[]{:S(2)}, u32[]{:S(2)}) collective-permute-start(bf16[192,128]{1,0:T(8,128)(2,1)S(1)} %pad_maximum_fusion), channel_id=1, source_target_pairs={{4,8},{8,4},{12,16},{16,12},{20,24},{24,20},{28,32},{32,28},{36,40... | collective-permute-start | bytes 147464 | tf_op jit(solution)/shard_map/ppermute | solution.py:567
  39.0 7.2 %copy-start.6 = (bf16[1536,128]{1,0:T(8,128)(2,1)S(1)}, bf16[1536,128]{1,0:T(8,128)(2,1)}, u32[]{:S(2)}) copy-start(bf16[1536,128]{1,0:T(8,128)(2,1)} %get-tuple-element.18.xv_ref) | copy-start | bytes 1179652
  39.0 7.2 %copy-start.7 = (bf16[1536,128]{1,0:T(8,128)(2,1)S(1)}, bf16[1536,128]{1,0:T(8,128)(2,1)}, u32[]{:S(2)}) copy-start(bf16[1536,128]{1,0:T(8,128)(2,1)} %get-tuple-element.19.xe_ref) | copy-start | bytes 1179652

commit v6 on v5

--- a/solution.py
+++ b/solution.py
@@ -235,7 +235,7 @@
         dst_ref[base + 2 * u + 1, :16] = wide[u * 16 : u * 16 + 16, 128:]
 
 
-STEP = 12
+STEP = 16
 
 
 def leaf_sides(own_ref, ev_ref, od_ref):
@@ -557,9 +557,9 @@
     )
     ev = lax.ppermute(su, "sub", [(i, i ^ 1) for i in range(subs)])
     od = lax.ppermute(su, flat, [(i, ((i + 1) ^ 1) - 1) for i in range(1, chain - 1)])
-    wl, wu = run_tables(leaf_table, upper_table, up)
     pair = jnp.concatenate([up, ev[UP_ROW:]], axis=0)
     x3 = lax.ppermute(pair, "sub", [(i, i ^ 3) for i in range(subs)])
+    wl, wu = run_tables(leaf_table, upper_table, pair)
     tab, at = run_near_tables(su, ev, od, coords)
     part = run_leaf(ints, su, ev, od, wl)
     branch = jnp.concatenate([pair, x3], axis=0)

time: 49.3 us -> 50.4 us (1.022)
  the two profiles are of different devices: /device:TPU:24 before, /device:TPU:16 now
where the time goes in v6:
time: 50.4 us; the launch traced here: 49.4 us
  starting transfers between devices  27.1 us (54%)
  Pallas kernels  20.8 us (41%)
  other arithmetic  0.72 us (1%)
  waiting for transfers between devices  0.55 us (1%)
    ppermute x1, starting transfers between devices, local(): lax.ppermute(su, flat, [(i, (i + 1 ^ 1) - 1) for i in range(1, chain - 1)])  12 us
    ppermute x1, starting transfers between devices, local(): lax.ppermute(branch, 'box', [(i, (i + 1 ^ 1) - 1) for i in range(1, boxes...  7.76 us
    pallas_call x1, Pallas kernels, run_near(): pl.pallas_call(near_kernel, out_shape=shape(8 * VP, 128, dtype=F32), in_s...  6.31 us
    pallas_call x1, Pallas kernels, run_prepare(): pl.pallas_call(prepare_kernel, out_shape=tuple((jax.ShapeDtypeStruct(d, t...  5.66 us
    pallas_call x1, Pallas kernels, run_leaf(): pl.pallas_call(leaf_kernel, out_shape=shape(BOXES * 16, 128, dtype=F32),...  4.77 us
    ppermute x1, starting transfers between devices, local(): ev = lax.ppermute(su, 'sub', [(i, i ^ 1) for i in range(subs)])  3.4 us
    pallas_call x1, Pallas kernels, run_field(): pl.pallas_call(field_kernel, out_shape=shape(BOXES, 1024, dtype=F32), in_...  2.87 us
    ppermute x1, starting transfers between devices, local(): x3 = lax.ppermute(pair, 'sub', [(i, i ^ 3) for i in range(subs)])  2.04 us
  transfers between devices with their start and end apart: 5, of which 1 were waited for; matrix products, arithmetic and copies ran while one was open for 1% of the time, Pallas kernels for 25%

profile of v6, /device:TPU:16, one launch (start us, length us, event | category | flops | bytes accessed | tf_op | source)
XLA Modules:
  0.0 49.4 jit_solution(11495628203592754716)
XLA Ops:
  0.0 0.0 copy-start.1
  0.0 0.0 copy-start.2
  0.0 5.7 %prepare.1 = (s32[96,128]{1,0:T(8,128)}, bf16[1536,128]{1,0:T(8,128)(2,1)}, bf16[912,128]{1,0:T(8,128)(2,1)}, bf16[48,128]{1,0:T(8,128)(2,1)}, bf16[1536,128]{1,0:T(8,128)(2,1)}) custom-call(bf16[48,1024]{1,0:T(8,128)(2,1)} %refs_0_.1, f32[48,192]{1,0:T(8,128)} %x_ref.1, s32[27,48]{1,0:T(8,128)} %bitcast.2, s32[1,48]{1,0:T(1,128)} %bitcast.3, ...), custom_call_target="tpu_custom_call" | custom-call | flops 5000000000 | bytes 1048576 | tf_op jit(solution)/shard_map/prepare/pallas_call | solution.py:440
  5.7 3.4 %collective-permute-start = (bf16[912,128]{1,0:T(8,128)(2,1)}, bf16[912,128]{1,0:T(8,128)(2,1)S(1)}, u32[]{:S(2)}, u32[]{:S(2)}) collective-permute-start(bf16[912,128]{1,0:T(8,128)(2,1)} %get-tuple-element.16.su_ref.own_ref), channel_id=1, source_target_pairs={{0,1},{1,0},{2,3},{3,2},{4,5},{5,4},{6,7},{7,6},{8,9},{9,8},{10,11... | collective-permute-start | bytes 700424 | tf_op jit(solution)/shard_map/ppermute | solution.py:558
  9.1 12.0 %collective-permute-start.4 = (bf16[912,128]{1,0:T(8,128)(2,1)}, bf16[912,128]{1,0:T(8,128)(2,1)S(1)}, u32[]{:S(2)}, u32[]{:S(2)}) collective-permute-start(bf16[912,128]{1,0:T(8,128)(2,1)} %get-tuple-element.16.su_ref.own_ref), channel_id=1, source_target_pairs={{1,2},{2,1},{3,4},{4,3},{5,6},{6,5},{7,8},{8,7},{9,10},{10,9},{11,... | collective-permute-start | bytes 700424 | tf_op jit(solution)/shard_map/ppermute | solution.py:559
  21.1 0.0 collective-permute-done.ev_ref
  21.1 0.7 %pad_maximum_fusion.1.after_ref = bf16[96,128]{1,0:T(8,128)(2,1)S(1)} fusion(bf16[48,128]{1,0:T(8,128)(2,1)S(1)} %slice.4, bf16[48,128]{1,0:T(8,128)(2,1)} %get-tuple-element.15.up_ref), kind=kLoop, calls=%fused_computation.1 | loop fusion | flops 49152 | bytes 49152 | tf_op jit(solution)/shard_map/concatenate | solution.py:560
  21.8 0.0 copy-start.3
  21.8 0.0 copy-start.7
  21.8 2.0 %collective-permute-start.1 = (bf16[96,128]{1,0:T(8,128)(2,1)S(1)}, bf16[96,128]{1,0:T(8,128)(2,1)S(1)}, u32[]{:S(2)}, u32[]{:S(2)}) collective-permute-start(bf16[96,128]{1,0:T(8,128)(2,1)S(1)} %pad_maximum_fusion.1.after_ref), channel_id=1, source_target_pairs={{0,3},{1,2},{2,1},{3,0},{4,7},{5,6},{6,5},{7,4},{8,11},{9,10},{10,... | collective-permute-start | bytes 73736 | tf_op jit(solution)/shard_map/ppermute | solution.py:561
  23.9 0.0 copy-done.1
  23.9 0.0 copy-done.2
  23.9 0.6 %tables.1 = (bf16[64,6144]{1,0:T(8,128)(2,1)S(1)}, bf16[64,4096]{1,0:T(8,128)(2,1)S(1)}) custom-call(bf16[96,4096]{1,0:T(8,128)(2,1)S(1)} %copy-done.1, bf16[64,4096]{1,0:T(8,128)(2,1)S(1)} %copy-done.2, bf16[96,128]{1,0:T(8,128)(2,1)S(1)} %pad_maximum_fusion.1.after_ref), custom_call_target="tpu_custom_call" | custom-call | flops 1000000000 | bytes 1048576 | tf_op jit(solution)/shard_map/tables/pallas_call | solution.py:463
  24.5 0.5 %collective-permute-done.4.od_ref = bf16[912,128]{1,0:T(8,128)(2,1)S(1)} collective-permute-done((bf16[912,128]{1,0:T(8,128)(2,1)}, bf16[912,128]{1,0:T(8,128)(2,1)S(1)}, u32[]{:S(2)}, u32[]{:S(2)}) %collective-permute-start.4) | collective-permute-done | bytes 233504 | tf_op jit(solution)/shard_map/ppermute | solution.py:559
  25.0 0.0 copy-done.3
  25.0 0.0 copy-done.7
  25.0 0.0 copy-start.4
  25.0 4.8 %leaf.1.part_ref = f32[768,128]{1,0:T(8,128)S(1)} custom-call(s32[96,128]{1,0:T(8,128)S(1)} %copy-done.7, bf16[912,128]{1,0:T(8,128)(2,1)S(1)} %copy-done.3, bf16[912,128]{1,0:T(8,128)(2,1)S(1)} %collective-permute-done.ev_ref, bf16[912,128]{1,0:T(8,128)(2,1)S(1)} %collective-permute-done.4.od_ref, bf16[64,6144]{1,0:T(8,128)(2,1)S(1)} %get-tuple-element.20.wl_ref), custom_call_target="tpu_custom_call" | custom-call | flops 5000000000 | bytes 1048576 | tf_op jit(solution)/shard_map/leaf/pallas_call | solution.py:513
  29.8 0.0 copy-done.4
  29.8 0.0 copy-start
  29.8 0.6 %near_tables.1 = (bf16[145,32,128]{2,1,0:T(8,128)(2,1)S(1)}, bf16[49,64,16]{2,1,0:T(8,128)(2,1)S(1)}) custom-call(bf16[912,128]{1,0:T(8,128)(2,1)S(1)} %copy-done.3, bf16[912,128]{1,0:T(8,128)(2,1)S(1)} %collective-permute-done.ev_ref, bf16[912,128]{1,0:T(8,128)(2,1)S(1)} %collective-permute-done.4.od_ref, f32[48,192]{1,0:T(8,128)S(1)} %copy-done.4), custom_call_target="tpu_custom_call" | custom-call | flops 1000000000 | bytes 1048576 | tf_op jit(solution)/shard_map/near_tables/pallas_call | solution.py:479
  30.4 0.0 collective-permute-done.1.after_ref.x3_ref
  30.5 0.1 copy-done
  30.5 1.9 %collective-permute-start.2 = (bf16[192,128]{1,0:T(8,128)(2,1)S(1)}, bf16[192,128]{1,0:T(8,128)(2,1)S(1)}, u32[]{:S(2)}, u32[]{:S(2)}) collective-permute-start(bf16[192,128]{1,0:T(8,128)(2,1)S(1)} %pad_maximum_fusion), channel_id=1, source_target_pairs={{0,4},{4,0},{8,12},{12,8},{16,20},{20,16},{24,28},{28,24},{32,36},... | collective-permute-start | bytes 147464 | tf_op jit(solution)/shard_map/ppermute | solution.py:566
  32.4 7.8 %collective-permute-start.3 = (bf16[192,128]{1,0:T(8,128)(2,1)S(1)}, bf16[192,128]{1,0:T(8,128)(2,1)S(1)}, u32[]{:S(2)}, u32[]{:S(2)}) collective-permute-start(bf16[192,128]{1,0:T(8,128)(2,1)S(1)} %pad_maximum_fusion), channel_id=1, source_target_pairs={{4,8},{8,4},{12,16},{16,12},{20,24},{24,20},{28,32},{32,28},{36,40... | collective-permute-start | bytes 147464 | tf_op jit(solution)/shard_map/ppermute | solution.py:567
  40.2 0.0 copy-start.5
  40.2 0.0 copy-start.6
  40.2 6.3 %near.1.near_ref = f32[416,128]{1,0:T(8,128)S(1)} custom-call(s32[96,128]{1,0:T(8,128)S(1)} %copy-done.7, bf16[145,32,128]{2,1,0:T(8,128)(2,1)S(1)} %get-tuple-element.21.tab, bf16[49,64,16]{2,1,0:T(8,128)(2,1)S(1)} %get-tuple-element.22.at, bf16[96,128]{1,0:T(8,128)(2,1)S(1)} %collective-permute-done.1.after_ref.x3_ref), custom_call_target="tpu_custom_call" | custom-call | flops 7000000000 | bytes 1048576 | tf_op jit(solution)/shard_map/near/pallas_call | solution.py:492
  46.5 0.0 collective-permute-done.2.be_ref
  46.5 0.0 collective-permute-done.3.bo_ref
  46.6 0.0 copy-done.5
  46.6 0.0 copy-done.6
  46.6 2.9 %field.1 = f32[48,1024]{1,0:T(8,128)} custom-call(s32[96,128]{1,0:T(8,128)S(1)} %copy-done.7, bf16[48,128]{1,0:T(8,128)(2,1)S(1)} %copy-done, bf16[912,128]{1,0:T(8,128)(2,1)S(1)} %collective-permute-done.ev_ref, bf16[96,128]{1,0:T(8,128)(2,1)S(1)} %collective-permute-done.1.after_ref.x3_ref, bf16[192,128]{1,0:T(8,128)(2,1)S(1)} %collective-permute-done.2.be_ref, ...), custom_call_target="tpu_custom_call" | custom-call | flops 3000000000 | bytes 1048576 | tf_op jit(solution)/shard_map/field/pallas_call | solution.py:530
  (2 shorter events, 0.0 us)
Async XLA Ops:
  0.0 23.9 %copy-start.1 = (bf16[96,4096]{1,0:T(8,128)(2,1)S(1)}, bf16[96,4096]{1,0:T(8,128)(2,1)}, u32[]{:S(2)}) copy-start(bf16[96,4096]{1,0:T(8,128)(2,1)} %leaf_ref.1) | copy-start | bytes 2359300
  0.0 23.9 %copy-start.2 = (bf16[64,4096]{1,0:T(8,128)(2,1)S(1)}, bf16[64,4096]{1,0:T(8,128)(2,1)}, u32[]{:S(2)}) copy-start(bf16[64,4096]{1,0:T(8,128)(2,1)} %upper_ref.1) | copy-start | bytes 1572868
  5.7 15.4 %collective-permute-start = (bf16[912,128]{1,0:T(8,128)(2,1)}, bf16[912,128]{1,0:T(8,128)(2,1)S(1)}, u32[]{:S(2)}, u32[]{:S(2)}) collective-permute-start(bf16[912,128]{1,0:T(8,128)(2,1)} %get-tuple-element.16.su_ref.own_ref), channel_id=1, source_target_pairs={{0,1},{1,0},{2,3},{3,2},{4,5},{5,4},{6,7},{7,6},{8,9},{9,8},{10,11... | collective-permute-start | bytes 700424 | tf_op jit(solution)/shard_map/ppermute | solution.py:558
  9.1 15.9 %collective-permute-start.4 = (bf16[912,128]{1,0:T(8,128)(2,1)}, bf16[912,128]{1,0:T(8,128)(2,1)S(1)}, u32[]{:S(2)}, u32[]{:S(2)}) collective-permute-start(bf16[912,128]{1,0:T(8,128)(2,1)} %get-tuple-element.16.su_ref.own_ref), channel_id=1, source_target_pairs={{1,2},{2,1},{3,4},{4,3},{5,6},{6,5},{7,8},{8,7},{9,10},{10,9},{11,... | collective-permute-start | bytes 700424 | tf_op jit(solution)/shard_map/ppermute | solution.py:559
  21.8 3.2 %copy-start.3 = (bf16[912,128]{1,0:T(8,128)(2,1)S(1)}, bf16[912,128]{1,0:T(8,128)(2,1)}, u32[]{:S(2)}) copy-start(bf16[912,128]{1,0:T(8,128)(2,1)} %get-tuple-element.16.su_ref.own_ref) | copy-start | bytes 700420
  21.8 3.2 %copy-start.7 = (s32[96,128]{1,0:T(8,128)S(1)}, s32[96,128]{1,0:T(8,128)}, u32[]{:S(2)}) copy-start(s32[96,128]{1,0:T(8,128)} %get-tuple-element.14.int_ref) | copy-start | bytes 147460
  21.8 8.6 %collective-permute-start.1 = (bf16[96,128]{1,0:T(8,128)(2,1)S(1)}, bf16[96,128]{1,0:T(8,128)(2,1)S(1)}, u32[]{:S(2)}, u32[]{:S(2)}) collective-permute-start(bf16[96,128]{1,0:T(8,128)(2,1)S(1)} %pad_maximum_fusion.1.after_ref), channel_id=1, source_target_pairs={{0,3},{1,2},{2,1},{3,0},{4,7},{5,6},{6,5},{7,4},{8,11},{9,10},{10,... | collective-permute-start | bytes 73736 | tf_op jit(solution)/shard_map/ppermute | solution.py:561
  25.0 4.8 %copy-start.4 = (f32[48,192]{1,0:T(8,128)S(1)}, f32[48,192]{1,0:T(8,128)}, u32[]{:S(2)}) copy-start(f32[48,192]{1,0:T(8,128)} %x_ref.1) | copy-start | bytes 110596
  29.8 0.7 %copy-start = (bf16[48,128]{1,0:T(8,128)(2,1)S(1)}, bf16[48,128]{1,0:T(8,128)(2,1)}, u32[]{:S(2)}) copy-start(bf16[48,128]{1,0:T(8,128)(2,1)} %get-tuple-element.15.up_ref) | copy-start | bytes 36868
  30.5 16.0 %collective-permute-start.2 = (bf16[192,128]{1,0:T(8,128)(2,1)S(1)}, bf16[192,128]{1,0:T(8,128)(2,1)S(1)}, u32[]{:S(2)}, u32[]{:S(2)}) collective-permute-start(bf16[192,128]{1,0:T(8,128)(2,1)S(1)} %pad_maximum_fusion), channel_id=1, source_target_pairs={{0,4},{4,0},{8,12},{12,8},{16,20},{20,16},{24,28},{28,24},{32,36},... | collective-permute-start | bytes 147464 | tf_op jit(solution)/shard_map/ppermute | solution.py:566
  32.4 14.1 %collective-permute-start.3 = (bf16[192,128]{1,0:T(8,128)(2,1)S(1)}, bf16[192,128]{1,0:T(8,128)(2,1)S(1)}, u32[]{:S(2)}, u32[]{:S(2)}) collective-permute-start(bf16[192,128]{1,0:T(8,128)(2,1)S(1)} %pad_maximum_fusion), channel_id=1, source_target_pairs={{4,8},{8,4},{12,16},{16,12},{20,24},{24,20},{28,32},{32,28},{36,40... | collective-permute-start | bytes 147464 | tf_op jit(solution)/shard_map/ppermute | solution.py:567
  40.2 6.4 %copy-start.5 = (bf16[1536,128]{1,0:T(8,128)(2,1)S(1)}, bf16[1536,128]{1,0:T(8,128)(2,1)}, u32[]{:S(2)}) copy-start(bf16[1536,128]{1,0:T(8,128)(2,1)} %get-tuple-element.18.xv_ref) | copy-start | bytes 1179652
  40.2 6.4 %copy-start.6 = (bf16[1536,128]{1,0:T(8,128)(2,1)S(1)}, bf16[1536,128]{1,0:T(8,128)(2,1)}, u32[]{:S(2)}) copy-start(bf16[1536,128]{1,0:T(8,128)(2,1)} %get-tuple-element.19.xe_ref) | copy-start | bytes 1179652
